TPU v7x, 32 devices: a whole 2x2x4 slice. The times are simulated.
32 devices in a mesh: row: 8 (over z, y), col: 4 (over x, core).
Axes of the slice: x: 2, y: 2, z: 4, core: 2. Of those that a mesh axis runs over, the one named last changes fastest.
Arguments:
- velocity: float32 [3, 128, 256, 1024], P(None, 'col', 'row'), may hold values from -6 to 6
- derivative_x: float32 [1024, 1024], replicated, may hold values from -4 to 4, as said below
- derivative_y: float32 [256, 256], replicated, may hold values from -4 to 4, as said below
- derivative_z: float32 [128, 128], replicated, may hold values from -4 to 4, as said below
- smoothing_x: float32 [1024, 1024], replicated, may hold values from -2 to 2, as said below
- smoothing_y: float32 [256, 256], replicated, may hold values from -2 to 2, as said below
- smoothing_z: float32 [128, 128], replicated, may hold values from -2 to 2, as said below
Outputs:
- filtered_velocity: float32 [3, 128, 256, 1024], P(None, 'col', 'row')
Inputs may be any that keep to these rules, and one draw needn't show every extreme that they name: derivative_x is diag(m) times the inverse of the periodic tridiagonal matrix with 1 on the diagonal and 9/20 beside it, times the periodic stencil 63/80 (f[i+1] - f[i-1]) + 9/100 (f[i+2] - f[i-2]) - 7/1200 (f[i+3] - f[i-3]); m holds one positive metric factor per grid line. `derivative_y`: as derivative_x, for the y lines. smoothing_x is the inverse of the periodic tridiagonal matrix with 1 on the diagonal and a[i] beside it in row i, times the periodic filter stencil of row i, whose weights are: at offset 0, 11/16 plus 5/8 times a[i]; at offsets -1 and 1 each, 15/64 plus 17/32 times a[i]; at offsets -2 and 2 each, -3/32 plus 3/16 times a[i]; at offsets -3 and 3 each, 1/64 minus 1/32 times a[i]; each a[i] lies in 0.44 to 0.499. `derivative_z`: as derivative_x, for the z lines. `smoothing_y`: as smoothing_x, for the y lines. `smoothing_z`: as smoothing_x, for the z lines.
All inputs are finite; a program needn't handle non-finite values.
Results may differ from a plain program's by a relative error of at most 0.000082.
Values sent between devices are 32-bit elements; how exact they have to be, the bound alone decides.
No kernel may reach another device: no remote copies, remote signals or barrier semaphores. Data moves between devices by JAX's collectives and lax.ppermute only.
A program may use at most 192 MiB of HBM per device.

v0:
```python
import jax
import jax.numpy as jnp
from jax import lax
from jax.sharding import PartitionSpec as P


def along_last(matrix, volume):
    return lax.dot_general(
        volume, matrix, (((3,), (1,)), ((), ())), precision=lax.Precision.HIGHEST
    )


def along_lines(matrix, volume):
    return jnp.dot(matrix, volume, precision=lax.Precision.HIGHEST)


def times_component(volume, component, outer_count):
    line_count = volume.shape[0]
    grouped = volume.reshape(line_count, outer_count, 3, -1)
    return (grouped * grouped[:, :, component : component + 1]).reshape(line_count, -1)


def swap_lines(volume, groups, inner_count, narrow):
    line_count = volume.shape[0]
    local_lines = line_count // groups
    grouped = volume.reshape(groups, local_lines, 3, inner_count, narrow)
    grouped = jnp.transpose(grouped, (3, 0, 2, 1, 4))
    return grouped.reshape(inner_count, groups, 3 * local_lines * narrow)


def pair_to_y(leading, second, num_row, rows_y, narrow):
    sent = (
        lax.all_to_all(
            swap_lines(leading, num_row, rows_y, narrow),
            "row",
            split_axis=1,
            concat_axis=0,
            tiled=True,
        ),
        lax.all_to_all(
            swap_lines(second, num_row, rows_y, narrow),
            "row",
            split_axis=1,
            concat_axis=0,
            tiled=True,
        ),
    )
    total_y = rows_y * num_row
    return (sent[0].reshape(total_y, -1), sent[1].reshape(total_y, -1))


def single_to_z(volume, num_row, rows_z, narrow):
    sent = lax.all_to_all(
        swap_lines(volume, num_row, rows_z, narrow), "row", split_axis=1, concat_axis=0, tiled=True
    )
    return sent.reshape(rows_z * num_row, -1)


def finish_x(matrix, volume, slab_z, rows_y):
    result = lax.dot_general(
        volume, matrix, (((0,), (1,)), ((), ())), precision=lax.Precision.HIGHEST
    )
    return result.reshape(3, slab_z, rows_y, matrix.shape[0])


def on_device(
    velocity, derivative_x, derivative_y, derivative_z, smoothing_x, smoothing_y, smoothing_z
):
    num_row = lax.axis_size("row")
    num_col = lax.axis_size("col")
    count_c, slab_z, rows_y, width_x = velocity.shape
    total_z = slab_z * num_col
    rows_z = total_z // num_row
    narrow = width_x // num_col
    tendency = -along_last(derivative_x, velocity * velocity[0:1])

    def to_z_lines(volume):
        grouped = volume.reshape(count_c, slab_z, rows_y, num_col, narrow)
        return jnp.transpose(grouped, (1, 3, 0, 2, 4)).reshape(slab_z, num_col, -1)

    flow_z, tend_z = (
        lax.all_to_all(to_z_lines(velocity), "col", split_axis=1, concat_axis=0, tiled=True),
        lax.all_to_all(to_z_lines(tendency), "col", split_axis=1, concat_axis=0, tiled=True),
    )
    flow_z = flow_z.reshape(total_z, -1)
    tend_z = tend_z.reshape(total_z, -1)
    tend_z = tend_z - along_lines(derivative_z, times_component(flow_z, 2, 1))
    flow_y, tend_y = pair_to_y(flow_z, tend_z, num_row, rows_y, narrow)
    tend_y = tend_y - along_lines(derivative_y, times_component(flow_y, 1, 1))
    advanced = flow_y + 0.1 * tend_y
    smooth = along_lines(smoothing_y, advanced)
    smooth = single_to_z(smooth, num_row, rows_z, narrow)
    smooth = along_lines(smoothing_z, smooth)
    grouped = smooth.reshape(num_col, slab_z, count_c, rows_y, narrow)
    grouped = jnp.transpose(grouped, (4, 0, 2, 1, 3)).reshape(narrow, num_col, -1)
    smooth = lax.all_to_all(grouped, "col", split_axis=1, concat_axis=0, tiled=True)
    smooth = smooth.reshape(width_x, -1)
    return finish_x(smoothing_x, smooth, slab_z, rows_y)


def solution(mesh):
    in_specs = (P(None, "col", "row", None), P(), P(), P(), P(), P(), P())
    out_specs = P(None, "col", "row", None)
    return jax.shard_map(
        on_device, mesh=mesh, in_specs=in_specs, out_specs=out_specs, check_vma=False
    )
```

profile of v0, /device:TPU:4, one launch (start us, length us, event | category | flops | bytes accessed | tf_op | source)
XLA Modules:
  0.0 1713.6 jit_solution(5563885262509766136)
XLA Ops:
  0.0 15.5 reshape.74
  48.0 45.8 %fusion.8 = f32[3,32,32,1024]{3,2,1,0:T(8,128)} fusion(f32[3,32,32,1024]{3,2,1,0:T(8,128)} %param.7, f32[32,32,1024]{2,1,0:T(8,128)S(1)} %slice_bitcast_fusion, f32[1024,1024]{1,0:T(8,128)} %param.8), kind=kOutput, calls=%fused_computation.15 | convolution fusion | flops 38660997120 | bytes 33554432 | tf_op jit(solution)/shard_map/dot_general | solution.py:8
  93.7 15.8 reshape.78
  133.1 50.5 %all-to-all-done = f32[32,4,24576]{2,0,1:T(8,128)} async-done(((f32[32,4,24576]{2,0,1:T(8,128)}), f32[32,4,24576]{2,0,1:T(8,128)}, u32[]{:S(2)}, u32[]{:S(2)}) %all-to-all-start) | async-done | bytes 12582944 | tf_op jit(solution)/shard_map/all_to_all | solution.py:82
  189.9 18.7 %reshape_reshape.13 = f32[128,1,3,8192]{3,2,0,1:T(4,128)} reshape(f32[4,32,1,24576]{3,1,0,2:T(8,128)} %bitcast.2) | data formatting | bytes 25165824 | tf_op jit(solution)/shard_map/reshape;reshape | solution.py:19
  235.0 12.7 copy.74
  247.7 80.3 %all-to-all-done.2 = f32[32,4,24576]{2,0,1:T(8,128)} async-done(((f32[32,4,24576]{2,0,1:T(8,128)}), f32[32,4,24576]{2,0,1:T(8,128)}, u32[]{:S(2)}, u32[]{:S(2)}) %all-to-all-start.2) | async-done | bytes 12582944 | tf_op jit(solution)/shard_map/all_to_all | solution.py:83
  352.4 23.1 %fusion = f32[128,24576]{0,1:T(8,128)} fusion(f32[128,24576]{0,1:T(8,128)S(1)} %copy-done.1, f32[128,24576]{1,0:T(8,128)S(1)} %bitcast_multiply_fusion, f32[128,128]{1,0:T(8,128)S(1)} %copy-done.3), kind=kOutput, calls=%fused_computation.2 | convolution fusion | flops 4834983936 | bytes 37814272 | tf_op jit(solution)/shard_map/dot_general | solution.py:14
  375.5 12.8 copy.76
  388.3 13.3 copy.101
  401.6 16.3 copy.94
  417.9 13.9 reshape.93
  438.5 13.3 copy.100
  451.8 16.2 copy.92
  468.0 14.0 reshape.92
  482.0 228.8 %all-to-all-done.3 = f32[32,8,12288]{2,0,1:T(8,128)} async-done(((f32[32,8,12288]{2,0,1:T(8,128)}), f32[32,8,12288]{2,0,1:T(8,128)}, u32[]{:S(2)}, u32[]{:S(2)}) %all-to-all-start.3) | async-done | bytes 12582944 | tf_op jit(solution)/shard_map/all_to_all | solution.py:40
  716.6 12.6 copy.81
  729.2 258.9 %all-to-all-done.1 = f32[32,8,12288]{2,0,1:T(8,128)} async-done(((f32[32,8,12288]{2,0,1:T(8,128)}), f32[32,8,12288]{2,0,1:T(8,128)}, u32[]{:S(2)}, u32[]{:S(2)}) %all-to-all-start.1) | async-done | bytes 12582944 | tf_op jit(solution)/shard_map/all_to_all | solution.py:33
  1000.6 18.2 %reshape_reshape.14 = f32[256,1,3,4096]{3,2,0,1:T(4,128)} reshape(f32[8,32,1,12288]{3,1,0,2:T(8,128)} %bitcast.5) | data formatting | bytes 25165824 | tf_op jit(solution)/shard_map/reshape;reshape | solution.py:19
  1045.8 12.6 copy.80
  1058.5 28.8 %fusion.3 = f32[256,12288]{0,1:T(8,128)} fusion(f32[256,12288]{0,1:T(8,128)} %copy.82, f32[256,12288]{0,1:T(8,128)} %copy.81, f32[256,256]{1,0:T(8,128)S(1)} %copy-done, f32[256,12288]{1,0:T(8,128)} %bitcast.6, f32[256,12288]{1,0:T(8,128)} %copy.80), kind=kOutput, calls=%fused_computation.7 | convolution fusion | flops 9676259328 | bytes 63176704 | tf_op jit(solution)/shard_map/dot_general | solution.py:14
  1087.3 14.8 convolution_bitcast_fusion.2
  1102.0 13.0 copy.83
  1115.0 14.3 copy.102
  1129.3 16.6 copy.96
  1157.9 277.0 %all_to_all.90 = f32[16,8,24576]{2,0,1:T(8,128)S(1)} all-to-all(f32[16,8,24576]{2,0,1:T(8,128)} %reshape.94), channel_id=1, replica_groups=mesh['row'=8,'col'=4] {'row'}, dimensions={1} | all-to-all | bytes 25165824 | tf_op jit(solution)/shard_map/all_to_all | solution.py:53
  1434.9 22.5 %convolution_bitcast_fusion = f32[128,24576]{0,1:T(8,128)} fusion(f32[128,24576]{1,0:T(8,128)S(1)} %bitcast.135, f32[128,128]{1,0:T(8,128)S(1)} %copy-done.4), kind=kOutput, calls=%fused_computation | convolution fusion | flops 4831838208 | bytes 25231360 | tf_op jit(solution)/shard_map/dot_general | solution.py:14
  1457.4 12.7 copy.86
  1470.1 13.3 copy.103
  1495.2 147.6 %all_to_all.91 = f32[256,4,3072]{0,2,1:T(8,128)} all-to-all(f32[256,4,3072]{0,2,1:T(8,128)} %bitcast.147), channel_id=1, replica_groups=mesh['row'=8,'col'=4] {'col'}, dimensions={1} | all-to-all | bytes 25165824 | tf_op jit(solution)/shard_map/all_to_all | solution.py:96
  1642.8 12.6 copy.88
  1667.9 45.4 %fusion.11 = f32[3,32,32,1024]{3,2,1,0:T(8,128)} fusion(f32[3,32,32,1024]{3,2,1,0:T(8,128)} %bitcast.152, f32[1024,1024]{1,0:T(8,128)} %param.11), kind=kOutput, calls=%fused_computation.16 | convolution fusion | flops 38654705664 | bytes 29360128 | tf_op jit(solution)/shard_map/dot_general | solution.py:60
  (31 shorter events, 201.6 us)
Async XLA Ops:
  0.0 1058.5 %copy-start = (f32[256,256]{1,0:T(8,128)S(1)}, f32[256,256]{1,0:T(8,128)}, u32[]{:S(2)}) copy-start(f32[256,256]{1,0:T(8,128)} %param.9) | copy-start | bytes 786436
  39.0 144.6 %all-to-all-start = ((f32[32,4,24576]{2,0,1:T(8,128)}), f32[32,4,24576]{2,0,1:T(8,128)}, u32[]{:S(2)}, u32[]{:S(2)}) async-start(f32[32,4,24576]{2,0,1:T(8,128)} %reshape.75), calls=%async_computation | async-start | bytes 25165824 | tf_op jit(solution)/shard_map/all_to_all | solution.py:82
  183.6 144.4 %all-to-all-start.2 = ((f32[32,4,24576]{2,0,1:T(8,128)}), f32[32,4,24576]{2,0,1:T(8,128)}, u32[]{:S(2)}, u32[]{:S(2)}) async-start(f32[32,4,24576]{2,0,1:T(8,128)} %reshape.79), calls=%async_computation.2 | async-start | bytes 25165824 | tf_op jit(solution)/shard_map/all_to_all | solution.py:83
  340.6 11.8 copy-start.1
  340.6 11.8 copy-start.3
  431.7 279.0 %all-to-all-start.3 = ((f32[32,8,12288]{2,0,1:T(8,128)}), f32[32,8,12288]{2,0,1:T(8,128)}, u32[]{:S(2)}, u32[]{:S(2)}) async-start(f32[32,8,12288]{2,0,1:T(8,128)} %reshape.93), calls=%async_computation.3 | async-start | bytes 25165824 | tf_op jit(solution)/shard_map/all_to_all | solution.py:40
  710.8 277.2 %all-to-all-start.1 = ((f32[32,8,12288]{2,0,1:T(8,128)}), f32[32,8,12288]{2,0,1:T(8,128)}, u32[]{:S(2)}, u32[]{:S(2)}) async-start(f32[32,8,12288]{2,0,1:T(8,128)} %reshape.92), calls=%async_computation.1 | async-start | bytes 25165824 | tf_op jit(solution)/shard_map/all_to_all | solution.py:33
  1058.5 28.8 %copy-start.2 = (f32[256,256]{1,0:T(8,128)S(1)}, f32[256,256]{1,0:T(8,128)}, u32[]{:S(2)}) copy-start(f32[256,256]{1,0:T(8,128)} %param.12) | copy-start | bytes 786436
  1157.9 277.0 %copy-start.4 = (f32[128,128]{1,0:T(8,128)S(1)}, f32[128,128]{1,0:T(8,128)}, u32[]{:S(2)}) copy-start(f32[128,128]{1,0:T(8,128)} %param.13) | copy-start | bytes 196612
where the time goes:
time: 1720 us; the launch traced here: 1710 us
  waiting for transfers between devices  618 us (36%)
  local copies, waits for them, and re-layouts  455 us (26%)
  blocking collectives  425 us (25%)
  matrix products  180 us (10%)
  starting transfers between devices  25.4 us (1%)
    all_to_all x1, blocking collectives, single_to_z(): lax.all_to_all(swap_lines(volume, num_row, rows_z, narrow), 'row', split_...  277 us
    all_to_all x1, waiting for transfers between devices, pair_to_y(): lax.all_to_all(swap_lines(leading, num_row, rows_y, narrow), 'row', split...  259 us
    all_to_all x1, waiting for transfers between devices, pair_to_y(): lax.all_to_all(swap_lines(second, num_row, rows_y, narrow), 'row', split_...  229 us
    all_to_all x1, blocking collectives, on_device(): lax.all_to_all(grouped, 'col', split_axis=1, concat_axis=0, tiled=True)  148 us
    dot_general x4, matrix products, along_lines(): return jnp.dot(matrix, volume, precision=lax.Precision.HIGHEST)  89.2 us
    reshape x6, local copies, waits for them, and re-layouts, swap_lines(): return grouped.reshape(inner_count, groups, 3 * local_lines * narrow)  88.9 us
    all_to_all x1, waiting for transfers between devices, on_device(): lax.all_to_all(to_z_lines(tendency), 'col', split_axis=1, concat_axis=0,...  80.3 us
    mul x6, local copies, waits for them, and re-layouts, times_component(): grouped * grouped[:, :, component:component + 1]  60.6 us
  transfers between devices with their start and end apart: 4, of which 4 were waited for; matrix products, arithmetic and copies ran while one was open for 12% of the time, Pallas kernels for 0%

commit v1 on v0

v1 whole, which is shorter than its diff:
```python
import functools

import jax
import jax.numpy as jnp
import numpy as np
from jax import lax
from jax.experimental import pallas as pl
from jax.experimental.pallas import tpu as pltpu
from jax.sharding import PartitionSpec as P

STEP = 0.1
PADE = 9.0 / 20.0
PADE_STENCIL = (63.0 / 80.0, 9.0 / 100.0, -7.0 / 1200.0)
SPAN = 128
LANES = 256
DEPTH = 256
ROWS = 128
TILE = 256
MIB = 1024 * 1024


def numpy_lanes(blocks):
    index = np.arange(SPAN)[None, :]

    def flip(value, level):
        return value[:, index[0] ^ (1 << level)]

    def pick(level, own_right, own_left):
        return np.where((index >> level) & 1 == 1, own_right, own_left)

    return flip, pick


def kernel_lanes(blocks):
    index = lax.broadcasted_iota(jnp.int32, (1, SPAN), 1)

    def pick(level, own_right, own_left):
        return jnp.where((index >> level) & 1 == 1, own_right, own_left)

    def flip(value, level):
        step = 1 << level
        return pick(level, pltpu.roll(value, step, 1), pltpu.roll(value, SPAN - step, 1))

    return flip, pick


def chain_tables(flip, pick, alpha, beta, gamma, delta, blocks):
    levels = blocks.bit_length() - 1
    zero = alpha * 0.0
    unit = zero + 1.0
    width = 2 * levels

    def combine(terms):
        terms = list(terms)
        return [sum(c * v[j] for c, v in terms) for j in range(width)]

    def spot(at):
        return [unit if j == at else zero for j in range(width)]

    def choose(level, own_right, own_left):
        return [pick(level, r, l) for r, l in zip(own_right, own_left)]

    coefs = [alpha, beta, gamma, delta]
    h_own, k_own = [zero] * width, [zero] * width
    merges, saved = [], []
    for level in range(levels):
        sibling = [flip(value, level) for value in coefs]
        h_sib, k_sib = spot(2 * level), spot(2 * level + 1)
        saved.append((coefs, sibling, h_own, k_own, h_sib, k_sib))
        if level == levels - 1:
            break
        a1, b1, g1, d1 = choose(level, sibling, coefs)
        a2, b2, g2, d2 = choose(level, coefs, sibling)
        scale = 1.0 / (1.0 - d1 * a2)
        h_h2, h_k1 = b1 * scale, b1 * scale * a2
        k_k1, k_h2 = g2 * scale, g2 * scale * d1
        own_left = [unit, h_k1, h_h2, zero, zero, k_k1, k_h2, unit]
        own_right = [h_h2, zero, unit, h_k1, k_h2, unit, zero, k_k1]
        merge = choose(level, own_right, own_left)
        merges.append(merge)
        planes = (h_own, k_own, h_sib, k_sib)
        h_own, k_own = combine(zip(merge[:4], planes)), combine(zip(merge[4:], planes))
        coefs = [a1 + b1 * scale * a2 * g1, b1 * scale * b2, g2 * scale * g1, d2 + g2 * scale * d1 * b2]
    (ao, bo, go, do), (ab, bb, gb, db), h_o, k_o, h_b, k_b = saved[-1]
    m00 = 1.0 - (gb * go + db * ao)
    m01 = -(gb * do + db * bo)
    m10 = -(ab * go + bb * ao)
    m11 = 1.0 - (ab * do + bb * bo)
    inverse = 1.0 / (m00 * m11 - m01 * m10)
    right0 = combine([(unit, k_b), (gb, k_o), (db, h_o)])
    right1 = combine([(unit, h_b), (ab, k_o), (bb, h_o)])
    g_in = combine([(inverse * m11, right0), (-inverse * m01, right1)])
    h_in = combine([(inverse * m00, right1), (-inverse * m10, right0)])
    for level in range(levels - 2, -1, -1):
        (ao, bo, go, do), (ab, bb, gb, db), h_o, k_o, h_b, k_b = saved[level]
        left = 1.0 / (1.0 - do * ab)
        right = 1.0 / (1.0 - db * ao)
        h_left = combine([(left, h_b), (left * ab, k_o), (left * ab * go, g_in), (left * bb, h_in)])
        g_right = combine([(right, k_b), (right * gb, g_in), (right * db, h_o), (right * db * bo, h_in)])
        h_in, g_in = choose(level, h_in, h_left), choose(level, g_right, g_in)
    if blocks == 4:
        merge = [flip(value, 1) for value in merges[0]]

        def raw(end):
            over = [end[2] * merge[j] + end[3] * merge[4 + j] for j in range(4)]
            return end[:2] + over[2:] + over[:2]

        return raw(g_in) + raw(h_in)
    return sum(merges, []) + g_in + h_in


def table_counts(blocks):
    levels = blocks.bit_length() - 1
    return (0, 6) if blocks == 4 else (8 * (levels - 1), 2 * levels)


def end_rows(a_past, stencil_past, sign):
    a1, a2, a3 = a_past
    (p1, p2, p3), (_, q2, q3), (_, _, s3) = stencil_past
    zero = p1 * 0.0
    r1 = [sign * p1, sign * p2, sign * p3]
    r2 = [sign * q2, sign * q3, zero]
    w2 = [sign * s3 / a3, zero, zero]
    w1 = [(x - y) / a2 for x, y in zip(r2, w2)]
    w0 = [(x - y) / a1 - z for x, y, z in zip(r1, w1, w2)]
    return w0, w1, w2


def functionals(xp, index, a, a_left, a_right, stencils, symmetric, first_row, last_row):
    n = a.shape[0]
    low = 1.0 if symmetric else -1.0
    past = lambda rows: tuple(stencils(r)[1:] for r in rows)
    right = end_rows(a_right, past(a_right), low)
    left = end_rows(a_left, past(a_left), 1.0)
    at = lambda i, value: xp.where(index == i, value, 0.0)
    centre, *bands = stencils(a)

    def end(row):
        total = centre * row
        for k, band in enumerate(bands, 1):
            part = band * row
            edge = xp.zeros_like(part[:k])
            total = total + xp.concatenate([edge, part[:-k]], axis=0)
            total = total + low * xp.concatenate([part[k:], edge], axis=0)
        for i in range(3):
            moved = row[n - 1 : n] * (right[0][i] + a[n - 1 : n] * right[1][i]) + row[n - 2 : n - 1] * a[n - 2 : n - 1] * right[0][i]
            total = total - at(n - 1 - i, moved)
            moved = row[0:1] * (left[0][i] + a[0:1] * left[1][i]) + row[1:2] * a[1:2] * left[0][i]
            total = total - at(i, moved)
        return total

    tail = lambda w: sum(at(n - 1 - i, c) for i, c in enumerate(w))
    head = lambda w: sum(at(i, c) for i, c in enumerate(w))
    return [tail(right[1]), tail(right[2]), head(left[1]), head(left[2]), end(first_row), end(last_row)]


def pade_line(count, blocks):
    n = count // blocks
    full = np.eye(count) + PADE * (np.eye(count, k=1) + np.eye(count, k=-1))
    full[0, -1] = full[-1, 0] = PADE
    band = np.zeros((count, count))
    for k, c in enumerate(PADE_STENCIL, 1):
        band += c * (np.roll(np.eye(count), k, axis=1) - np.roll(np.eye(count), -k, axis=1))
    beside = np.linalg.solve(full, band)[0, 1]
    inside = np.linalg.inv(np.eye(n) + PADE * (np.eye(n, k=1) + np.eye(n, k=-1)))
    stencils = lambda a: [a * 0.0] + [a * 0.0 + c for c in PADE_STENCIL]
    side = [np.full((1, 1), PADE)] * 3
    index = np.arange(n)[:, None]
    taps = functionals(
        np, index, np.full((n, 1), PADE), side, side, stencils, False, inside[0][:, None], inside[-1][:, None]
    )
    spread = np.stack([-PADE * inside[:, 0], -PADE * inside[:, -1]], axis=1)
    every = lambda value: np.full((1, SPAN), value)
    flip, pick = numpy_lanes(blocks)
    table = chain_tables(
        flip, pick, every(spread[0, 0]), every(spread[0, 1]), every(spread[-1, 0]), every(spread[-1, 1]), blocks
    )
    return beside, np.concatenate(taps, axis=1), spread, np.concatenate(table, axis=0)


def exact_dot(x, y):
    return jnp.dot(x, y, precision=lax.Precision.HIGHEST, preferred_element_type=jnp.float32)


def iota(shape, axis):
    return lax.broadcasted_iota(jnp.int32, shape, axis)


def place_of(lane, n, group, inner):
    return (lane // group, lane % group) if inner else (lane % n, lane // n)


def block_rows(matrix_ref, block, n):
    return matrix_ref[pl.ds(pl.multiple_of(block * n, 8), n), :]


def store_stack(out_ref, rows, taps, block, n, group, inner):
    wide = n * group
    count = rows.shape[1]
    place, line = place_of(iota((1, wide), 1), n, group, inner)
    tiled = exact_dot(rows, (iota((count, wide), 0) == block * n + place).astype(jnp.float32))
    if inner:
        whole = jnp.broadcast_to(tiled[:, None, :], (n, group, wide)).reshape(wide, wide)
    else:
        whole = jnp.concatenate([tiled] * group, axis=0)
    _, row_line = place_of(iota((wide, 1), 0), n, group, inner)
    whole = jnp.where(row_line == line, whole, 0.0)
    mask = iota((group, wide), 0) == line
    both = jnp.concatenate([whole] + [jnp.where(mask, tap, 0.0) for tap in taps], axis=0)
    high = both.astype(jnp.bfloat16)
    half = both.shape[0]
    out_ref[:half] = high
    out_ref[half:] = (both - high.astype(jnp.float32)).astype(jnp.bfloat16)


def ordered(odd, taps):
    r1, r2, l1, l2, h, k = taps
    pick = lambda x, y: jnp.where(odd, x, y)
    return [pick(l1, r1), pick(l2, r2), h, k, pick(r1, l1), pick(r2, l2)]


def store_table(out_ref, odd, spread, factor):
    _, n, lanes = out_ref.shape
    row = iota((n, lanes), 0)
    side = odd.astype(jnp.int32)
    for j in range(2):
        out_ref[j] = jnp.broadcast_to(spread[j] * factor, (n, lanes))
        for k, first in enumerate((side, 1 - side)):
            spot = row == first * j + (1 - first) * (n - 1 - j)
            out_ref[2 + 2 * k + j] = jnp.where(spot, factor, 0.0)


def store_chain(out_ref, rows, block):
    own = jnp.sum(jnp.where(iota(rows.shape, 1) == block, rows, 0.0), axis=1, keepdims=True)
    out_ref[...] = jnp.broadcast_to(own, out_ref.shape)


def derivative_kernel(lines, pos_ref, *refs):
    refs = list(refs)
    take = lambda k: [refs.pop(0) for _ in range(k)]
    matrices, tap_refs, spreads, chain_refs = (take(len(lines)) for _ in range(4))
    stacks, tables, chains = (take(len(lines)) for _ in range(3))
    for axis, (n, group, inner, beside) in enumerate(lines):
        block = pos_ref[axis]
        odd = block % 2 == 1
        rows = block_rows(matrices[axis], block, n)
        count = rows.shape[1]
        next_one = iota((n, count), 1) == (block * n + iota((n, count), 0) + 1) % count
        metric = jnp.sum(jnp.where(next_one, rows, 0.0), axis=1, keepdims=True) * (1.0 / beside)
        taps = [tap_refs[axis][j : j + 1, :] for j in range(6)]
        store_stack(stacks[axis], -STEP * rows, ordered(odd, taps), block, n, group, inner)
        spread = [spreads[axis][:, j : j + 1] for j in range(2)]
        store_table(tables[axis], odd, spread, -STEP * metric)
        store_chain(chains[axis], chain_refs[axis][...], block)


def filter_stencils(a):
    return [
        11.0 / 16.0 + 5.0 / 8.0 * a,
        15.0 / 64.0 + 17.0 / 32.0 * a,
        -3.0 / 32.0 + 3.0 / 16.0 * a,
        1.0 / 64.0 - 1.0 / 32.0 * a,
    ]


def block_ends(a, out_ref):
    n = a.shape[0]
    a = [a[i : i + 1, :] for i in range(n)]
    down, up = [jnp.ones_like(a[0])], [jnp.ones_like(a[0])]
    for i in range(1, n):
        down.append(1.0 / (1.0 - a[i] * a[i - 1] * down[i - 1]))
        j = n - 1 - i
        up.insert(0, 1.0 / (1.0 - a[j] * a[j + 1] * up[0]))
    column = row = up[0]
    out_ref[0, 0:1, :] = column
    out_ref[2, 0:1, :] = row
    for i in range(1, n):
        column = -a[i] * up[i] * column
        row = -a[i - 1] * up[i] * row
        out_ref[0, i : i + 1, :] = column
        out_ref[2, i : i + 1, :] = row
    column = row = down[-1]
    out_ref[1, n - 1 : n, :] = column
    out_ref[3, n - 1 : n, :] = row
    for i in range(n - 2, -1, -1):
        column = -a[i] * down[i] * column
        row = -a[i + 1] * down[i] * row
        out_ref[1, i : i + 1, :] = column
        out_ref[3, i : i + 1, :] = row


def smoothing_kernel(lines, pos_ref, *refs):
    refs = list(refs)
    take = lambda k: [refs.pop(0) for _ in range(k)]
    matrices = take(len(lines))
    stacks, tables, chains = take(len(lines)), take(len(lines)), take(len(lines))
    scratch = take(len(lines))
    for axis, (n, group, inner, blocks) in enumerate(lines):
        block = pos_ref[axis]
        odd = block % 2 == 1
        matrix = matrices[axis][...]
        count = matrix.shape[0]
        row, lane = iota((count, count), 0), iota((count, count), 1)
        middle = jnp.sum(jnp.where(row == lane, matrix, 0.0), axis=0, keepdims=True)
        near = (row == (lane + 1) % count) | (lane == (row + 1) % count)
        beside = jnp.sum(jnp.where(near, matrix, 0.0), axis=0, keepdims=True)
        along = (11.0 / 16.0 - middle) / (beside - 5.0 / 8.0)
        sorted_out = jnp.where(iota((n, count), 1) % n == iota((n, count), 0), along, 0.0)
        a = exact_dot(sorted_out, (iota((count, SPAN), 0) // n == iota((count, SPAN), 1)).astype(jnp.float32))
        ends_ref = scratch[axis]
        block_ends(a, ends_ref)
        column0, column1, row0, row1 = (ends_ref[j] for j in range(4))
        first, last = a[0:1], a[n - 1 : n]
        spread = [-first * column0, -last * column1]
        flip, pick = kernel_lanes(blocks)
        chain = chain_tables(
            flip, pick, spread[0][0:1], spread[1][0:1], spread[0][n - 1 : n], spread[1][n - 1 : n], blocks
        )
        store_chain(chains[axis], jnp.concatenate(chain, axis=0), block)
        index = iota((1, SPAN), 1)
        after = lambda v: jnp.where(index == blocks - 1, pltpu.roll(v, blocks - 1, 1), pltpu.roll(v, SPAN - 1, 1))
        before = lambda v: jnp.where(index == 0, pltpu.roll(v, SPAN - blocks + 1, 1), pltpu.roll(v, 1, 1))
        a_right = [after(a[i : i + 1]) for i in range(3)]
        a_left = [before(a[n - 1 - i : n - i]) for i in range(3)]
        used = index < blocks
        a_right = [jnp.where(used, v, 0.44) for v in a_right]
        a_left = [jnp.where(used, v, 0.44) for v in a_left]
        taps = functionals(jnp, iota((n, SPAN), 0), a, a_left, a_right, filter_stencils, True, row0, row1)
        own = lambda v: jnp.sum(jnp.where(iota((n, SPAN), 1) == block, v, 0.0), axis=1, keepdims=True)
        wide = n * group
        place, _ = place_of(iota((1, wide), 1), n, group, inner)
        at_place = iota((n, wide), 0) == place
        tap_rows = [jnp.sum(jnp.where(at_place, own(t), 0.0), axis=0, keepdims=True) for t in taps]
        rows = block_rows(matrices[axis], block, n)
        store_stack(stacks[axis], rows, ordered(odd, tap_rows), block, n, group, inner)
        store_table(tables[axis], odd, [own(s) for s in spread], jnp.ones((n, 1), jnp.float32))


def stack_shape(n, group):
    return jax.ShapeDtypeStruct((2 * group * (n + 6), group * n), jnp.bfloat16)


def derivative_call(pos, matrices, lines):
    ready = [pade_line(m.shape[0], blocks) for m, (_, _, _, blocks) in zip(matrices, lines)]
    expanded = []
    for (n, group, inner, _), (_, taps, _, _) in zip(lines, ready):
        place, _ = place_of(np.arange(n * group), n, group, inner)
        expanded.append(jnp.asarray(taps[place].T.astype(np.float32)))
    spreads = [jnp.asarray(spread.astype(np.float32)) for _, _, spread, _ in ready]
    chains = [jnp.asarray(table.astype(np.float32)) for _, _, _, table in ready]
    setup = [(n, group, inner, beside) for (n, group, inner, _), (beside, _, _, _) in zip(lines, ready)]
    out = pl.pallas_call(
        functools.partial(derivative_kernel, setup),
        in_specs=[SMEM] + [VMEM] * (4 * len(lines)),
        out_shape=[stack_shape(n, group) for n, group, _, _ in lines]
        + [shape_of(6, n, SPAN) for n, _, _, _ in lines]
        + [shape_of(*chain.shape) for chain in chains],
        compiler_params=params(32),
        name="derivative_lines",
    )(pos, *matrices, *expanded, *spreads, *chains)
    k = len(lines)
    return out[:k], out[k : 2 * k], out[2 * k :]


def smoothing_call(pos, matrices, lines):
    rows = [merged + 2 * planes for merged, planes in (table_counts(blocks) for _, _, _, blocks in lines)]
    out = pl.pallas_call(
        functools.partial(smoothing_kernel, lines),
        in_specs=[SMEM] + [VMEM] * len(lines),
        out_shape=[stack_shape(n, group) for n, group, _, _ in lines]
        + [shape_of(6, n, SPAN) for n, _, _, _ in lines]
        + [shape_of(r, SPAN) for r in rows],
        scratch_shapes=[pltpu.VMEM((4, n, SPAN), jnp.float32) for n, _, _, _ in lines],
        compiler_params=params(32),
        name="smoothing_lines",
    )(pos, *matrices)
    k = len(lines)
    return out[:k], out[k : 2 * k], out[2 * k :]


def split(values):
    high = values.astype(jnp.bfloat16)
    return high, (values - high.astype(jnp.float32)).astype(jnp.bfloat16)


def times(stack, values):
    half = stack.shape[0] // 2
    high, low = split(values)
    dot = functools.partial(jnp.dot, preferred_element_type=jnp.float32)
    first = dot(stack, high)
    return first[:half] + first[half:] + dot(stack[:half], low)


def put_taps(taps, group, at, writers):
    for j, targets in enumerate(writers):
        for ref, plane in targets:
            ref[plane, at : at + group, :] = taps[j * group : (j + 1) * group]


def writers_of(outs, blocks):
    if blocks == 4:
        near, away, ends = outs
        return [
            [(near, 0)],
            [(near, 1)],
            [(near, 2), (away, 2), (ends, 0)],
            [(near, 3), (away, 3), (ends, 1)],
            [(away, 0)],
            [(away, 1)],
        ]
    near, away = outs
    return [[(near, j)] for j in range(4)] + [[(away, j)] for j in range(2)]


def out_planes(blocks):
    return [4, 4, 2] if blocks == 4 else [4, 2]


def along_y(stack, read, count_z, count_y, write, writers):
    group = min(count_z, DEPTH // count_y)
    for at in range(0, count_z, group):
        values = read(slice(at, at + group), slice(0, count_y))
        result = times(stack, values.reshape(group * count_y, -1))
        write(slice(at, at + group), slice(0, count_y), result[: group * count_y].reshape(values.shape))
        put_taps(result[group * count_y :], group, at, writers)


def along_z(stack, read, count_z, count_y, write, writers):
    group = min(count_y, DEPTH // count_z)
    for at in range(0, count_y, group):
        values = read(slice(0, count_z), slice(at, at + group))
        result = times(stack, values.reshape(count_z * group, -1))
        write(slice(0, count_z), slice(at, at + group), result[: count_z * group].reshape(values.shape))
        put_taps(result[count_z * group :], group, at, writers)


def flux_kernel(blocks_y, blocks_z, v_ref, ly_ref, lz_ref, t_ref, *outs):
    count_c, count_z, count_y, _ = v_ref.shape
    outs = list(outs)
    for c in range(count_c):
        outs_y = [outs.pop(0) for _ in out_planes(blocks_y)]
        outs_z = [outs.pop(0) for _ in out_planes(blocks_z)]

        def write_y(zs, ys, value, c=c):
            t_ref[c, zs, ys] = v_ref[c, zs, ys] + value

        def write_z(zs, ys, value, c=c):
            t_ref[c, zs, ys] += value

        flux = lambda k: lambda zs, ys: v_ref[c, zs, ys] * v_ref[k, zs, ys]
        along_y(ly_ref[...], flux(1), count_z, count_y, write_y, writers_of(outs_y, blocks_y))
        along_z(lz_ref[...], flux(2), count_z, count_y, write_z, writers_of(outs_z, blocks_z))


def ends_of(chain_ref, blocks, planes):
    merged, count = table_counts(blocks)
    weight = lambda i, j: chain_ref[merged + i * count + j : merged + i * count + j + 1, :]
    return [sum(weight(i, j) * plane for j, plane in enumerate(planes)) for i in range(2)]


def spans(width):
    return [slice(x, x + SPAN) for x in range(0, width, SPAN)]


def far_planes(parts, blocks, xs):
    if blocks == 4:
        near, away, opposite = parts
        return [near[2, :, xs], near[3, :, xs], away[2, :, xs], away[3, :, xs], opposite[0, :, xs], opposite[1, :, xs]]
    near, _, *rest = parts
    return [near[2, :, xs], near[3, :, xs]] + [ref[j, :, xs] for ref in rest for j in range(2)]


def mend_y(read, write, chain_ref, table_ref, parts, blocks, ends_ref, dims):
    count_z, count_y, width = dims
    near, away = parts[:2]
    for xs in spans(width):
        ends_ref[0], ends_ref[1] = ends_of(chain_ref, blocks, far_planes(parts, blocks, xs))
        for y in range(0, count_y, 8):
            ys = slice(y, y + 8)
            column = [table_ref[j, ys, :] for j in range(6)]
            for z in range(count_z):
                at = slice(z, z + 1)
                value = read(z, ys, xs) + column[0] * ends_ref[0, at, :] + column[1] * ends_ref[1, at, :]
                if y == 0 or y == count_y - 8:
                    value = value + column[2] * near[0, at, xs] + column[3] * near[1, at, xs]
                    value = value + column[4] * away[0, at, xs] + column[5] * away[1, at, xs]
                write(z, ys, xs, value)


def mend_z(read, write, chain_ref, table_ref, parts, blocks, count_z, width):
    near, away = parts[:2]
    for xs in spans(width):
        g, h = ends_of(chain_ref, blocks, far_planes(parts, blocks, xs))
        for z in range(count_z):
            factor = [table_ref[j, z : z + 1, :] for j in range(6)]
            value = read(z, xs) + factor[0] * g + factor[1] * h
            if z in (0, count_z - 1):
                value = value + factor[2] * near[0, :, xs] + factor[4] * away[0, :, xs]
            if z in (1, count_z - 2):
                value = value + factor[3] * near[1, :, xs] + factor[5] * away[1, :, xs]
            write(z, xs, value)


def advance_kernel(blocks_y, blocks_z, *refs):
    refs = list(refs)
    take = lambda n: [refs.pop(0) for _ in range(n)]
    t_ref, lz_ref, cy_ref, cz_ref, sy_ref, sz_ref = take(6)
    y_parts, z_parts = take(part_count(blocks_y)), take(part_count(blocks_z))
    (out_ref,) = take(1)
    outs = take(len(out_planes(blocks_z)))
    whole, ends = take(2)
    _, count_z, count_y, width = t_ref.shape

    def store_y(z, ys, xs, value):
        whole[z, ys, xs] = value

    def store_z(z, xs, value):
        whole[z, :, xs] = value

    def write(zs, ys, value):
        out_ref[zs, ys] = value

    dims = (count_z, count_y, width)
    mend_y(lambda z, ys, xs: t_ref[0, z, ys, xs], store_y, cy_ref, sy_ref, y_parts, blocks_y, ends, dims)
    mend_z(lambda z, xs: whole[z, :, xs], store_z, cz_ref, sz_ref, z_parts, blocks_z, count_z, width)
    along_z(lz_ref[...], lambda zs, ys: whole[zs, ys], count_z, count_y, write, writers_of(outs, blocks_z))


def filter_kernel(blocks_y, blocks_z, *refs):
    refs = list(refs)
    take = lambda n: [refs.pop(0) for _ in range(n)]
    t_ref, ly_ref, cz_ref, sz_ref = take(4)
    z_parts = take(part_count(blocks_z))
    (out_ref,) = take(1)
    outs = take(len(out_planes(blocks_y)))
    (whole,) = take(1)
    count_z, count_y, width = t_ref.shape

    def store_z(z, xs, value):
        whole[z, :, xs] = value

    def write(zs, ys, value):
        out_ref[zs, ys] = value

    mend_z(lambda z, xs: t_ref[z, :, xs], store_z, cz_ref, sz_ref, z_parts, blocks_z, count_z, width)
    along_y(ly_ref[...], lambda zs, ys: whole[zs, ys], count_z, count_y, write, writers_of(outs, blocks_y))


def split_once(matrix_ref, high_ref, low_ref, factor):
    @pl.when(pl.program_id(0) == 0)
    def _():
        count = matrix_ref.shape[0]
        step = min(count, 128)
        for at in range(0, count, step):
            high_ref[at : at + step], low_ref[at : at + step] = split(matrix_ref[at : at + step] * factor)


def cut(array, start, count):
    whole = array.shape[1]
    start = start % whole
    if start + count <= whole:
        return array[:, start : start + count]
    return jnp.concatenate([array[:, start:], array[:, : start + count - whole]], axis=1)


def rows_times(values, high_ref, low_ref, write):
    high, low = split(values)
    dot = lambda x, w: lax.dot_general(x, w, (((1,), (1,)), ((), ())), preferred_element_type=jnp.float32)
    width = values.shape[1]
    for at in range(0, width, TILE):
        near = min(width, 2 * TILE)
        start = at - TILE // 2
        w_high, w_low = high_ref[at : at + TILE, :], low_ref[at : at + TILE, :]
        x_near, w_near = cut(high, start, near), cut(w_high, start, near)
        total = dot(x_near, w_near) + (dot(cut(low, start, near), w_near) + dot(x_near, cut(w_low, start, near)))
        if near < width:
            total = total + dot(cut(high, start + near, width - near), cut(w_high, start + near, width - near))
        write(slice(at, at + TILE), total)


def flux_x_kernel(v_ref, t_ref, matrix_ref, out_ref, high_ref, low_ref):
    split_once(matrix_ref, high_ref, low_ref, -STEP)
    values = v_ref[...] * v_ref[0:1]

    def write(xs, value):
        out_ref[:, :, :, xs] = t_ref[:, :, :, xs] + value.reshape(values.shape[:3] + (-1,))

    rows_times(values.reshape(-1, values.shape[-1]), high_ref, low_ref, write)


def last_kernel(blocks_y, aliased, *refs):
    refs = list(refs)
    take = lambda n: [refs.pop(0) for _ in range(n)]
    t_ref, matrix_ref, cy_ref, sy_ref = take(4)
    y_parts = take(part_count(blocks_y))
    take(aliased)
    (out_ref,) = take(1)
    whole, ends, high_ref, low_ref = take(4)
    count_z, count_y, width = t_ref.shape
    split_once(matrix_ref, high_ref, low_ref, 1.0)

    def store_y(z, ys, xs, value):
        whole[z, ys, xs] = value

    dims = (count_z, count_y, width)
    mend_y(lambda z, ys, xs: t_ref[z, ys, xs], store_y, cy_ref, sy_ref, y_parts, blocks_y, ends, dims)

    def write(xs, value):
        out_ref[0, :, :, xs] = value.reshape((count_z, count_y, -1))

    rows_times(whole[...].reshape(-1, width), high_ref, low_ref, write)


def merge_kernel(first_row, offset, chain_ref, own_ref, other_ref, out_ref):
    for xs in spans(out_ref.shape[2]):
        planes = [ref[offset + j, :, xs] for ref in (own_ref, other_ref) for j in range(2)]
        for i in range(2):
            row = first_row + 4 * i
            out_ref[i, :, xs] = sum(chain_ref[row + j : row + j + 1, :] * plane for j, plane in enumerate(planes))


def params(mib):
    return pltpu.CompilerParams(vmem_limit_bytes=mib * MIB)


def shape_of(*dims):
    return jax.ShapeDtypeStruct(dims, jnp.float32)


SMEM = pl.BlockSpec(memory_space=pltpu.SMEM)
VMEM = pl.BlockSpec(memory_space=pltpu.VMEM)


def part_count(blocks):
    return 3 if blocks == 4 else blocks.bit_length()


def whole_spec(array):
    return pl.BlockSpec(array.shape, lambda *_: (0,) * array.ndim)


def lane_spec(dims):
    return pl.BlockSpec(tuple(dims) + (LANES,), lambda i: (0,) * len(dims) + (i,))


def cost(flops, size):
    return pl.CostEstimate(flops=int(flops), bytes_accessed=int(size), transcendentals=0)


def flux_call(velocity, ly, lz, blocks_y, blocks_z):
    nc, nz, ny, width = velocity.shape
    size = nc * nz * ny * width
    planes = [(k, nz) for k in out_planes(blocks_y)] + [(k, ny) for k in out_planes(blocks_z)]
    planes = planes * nc
    out = pl.pallas_call(
        functools.partial(flux_kernel, blocks_y, blocks_z),
        grid=(width // LANES,),
        in_specs=[lane_spec((nc, nz, ny)), whole_spec(ly), whole_spec(lz)],
        out_specs=[lane_spec((nc, nz, ny))] + [lane_spec(dims) for dims in planes],
        out_shape=[shape_of(nc, nz, ny, width)] + [shape_of(*dims, width) for dims in planes],
        compiler_params=params(60),
        cost_estimate=cost(size * 2 * 256 * 8, size * 9),
        name="flux_yz",
    )(velocity, ly, lz)
    each = len(planes) // nc
    first = len(out_planes(blocks_y))
    parts = [out[1 + c * each : 1 + (c + 1) * each] for c in range(nc)]
    return out[0], [(p[:first], p[first:]) for p in parts]


def flux_x_call(velocity, t, matrix, part, parts):
    nc, nz, ny, width = velocity.shape
    group = max(1, min(nz // parts, ROWS // ny))
    steps = nz // parts // group
    block = pl.BlockSpec((nc, group, ny, width), lambda i: (0, part * steps + i, 0, 0))
    size = nc * nz * ny * width // parts
    return pl.pallas_call(
        flux_x_kernel,
        grid=(steps,),
        in_specs=[block, block, whole_spec(matrix)],
        out_specs=block,
        out_shape=shape_of(nc, nz, ny, width),
        scratch_shapes=[pltpu.VMEM(matrix.shape, jnp.bfloat16)] * 2,
        input_output_aliases={1: 0},
        compiler_params=params(60),
        cost_estimate=cost(size * 4 * width, size * 13),
        name="flux_x",
    )(velocity, t, matrix)


def advance_call(t, c, lz, cy, cz, sy, sz, y_parts, z_parts, blocks_y, blocks_z):
    _, nz, ny, width = t.shape
    size = nz * ny * width
    planes = list(y_parts) + list(z_parts)
    outs = [(k, ny) for k in out_planes(blocks_z)]
    component = pl.BlockSpec((1, nz, ny, LANES), lambda i: (c, 0, 0, i))
    return pl.pallas_call(
        functools.partial(advance_kernel, blocks_y, blocks_z),
        grid=(width // LANES,),
        in_specs=[component] + [whole_spec(a) for a in (lz, cy, cz, sy, sz)]
        + [lane_spec(p.shape[:2]) for p in planes],
        out_specs=[lane_spec((nz, ny))] + [lane_spec(dims) for dims in outs],
        out_shape=[shape_of(nz, ny, width)] + [shape_of(*dims, width) for dims in outs],
        scratch_shapes=[pltpu.VMEM((nz, ny, LANES), jnp.float32), pltpu.VMEM((2, nz, SPAN), jnp.float32)],
        compiler_params=params(60),
        cost_estimate=cost(size * 2 * 256 * 4, size * 9),
        name="advance_z",
    )(t, lz, cy, cz, sy, sz, *planes)


def filter_call(t, ly, cz, sz, z_parts, blocks_y, blocks_z):
    nz, ny, width = t.shape
    size = nz * ny * width
    outs = [(k, nz) for k in out_planes(blocks_y)]
    return pl.pallas_call(
        functools.partial(filter_kernel, blocks_y, blocks_z),
        grid=(width // LANES,),
        in_specs=[lane_spec((nz, ny))] + [whole_spec(a) for a in (ly, cz, sz)] + [lane_spec(p.shape[:2]) for p in z_parts],
        out_specs=[lane_spec((nz, ny))] + [lane_spec(dims) for dims in outs],
        out_shape=[shape_of(nz, ny, width)] + [shape_of(*dims, width) for dims in outs],
        scratch_shapes=[pltpu.VMEM((nz, ny, LANES), jnp.float32)],
        compiler_params=params(60),
        cost_estimate=cost(size * 2 * 256 * 4, size * 9),
        name="filter_y",
    )(t, ly, cz, sz, *z_parts)


def last_call(whole, t, c, count_c, matrix, cy, sy, y_parts, blocks_y):
    nz, ny, width = t.shape
    group = max(8, min(nz, DEPTH // ny))
    block = pl.BlockSpec((group, ny, width), lambda i: (i, 0, 0))
    plane = lambda k: pl.BlockSpec((k, group, width), lambda i: (0, i, 0))
    size = nz * ny * width
    aliased = [] if whole is None else [whole]
    operands = [t, matrix, cy, sy, *y_parts, *aliased]
    return pl.pallas_call(
        functools.partial(last_kernel, blocks_y, len(aliased)),
        grid=(nz // group,),
        in_specs=[block] + [whole_spec(a) for a in (matrix, cy, sy)]
        + [plane(p.shape[0]) for p in y_parts]
        + [pl.BlockSpec(memory_space=pl.ANY)] * len(aliased),
        out_specs=pl.BlockSpec((1, group, ny, width), lambda i: (c, i, 0, 0)),
        out_shape=shape_of(count_c, nz, ny, width),
        scratch_shapes=[pltpu.VMEM((group, ny, width), jnp.float32), pltpu.VMEM((2, group, SPAN), jnp.float32)]
        + [pltpu.VMEM(matrix.shape, jnp.bfloat16)] * 2,
        input_output_aliases={len(operands) - 1: 0} if aliased else {},
        compiler_params=params(60),
        cost_estimate=cost(size * 6 * width, size * 13),
        name="filter_x",
    )(*operands)


def merge_call(chain, first_row, own, other):
    offset = own.shape[0] - 2
    dims = own.shape[1:]
    size = 2 * dims[0] * dims[1]
    return pl.pallas_call(
        functools.partial(merge_kernel, first_row, offset),
        in_specs=[VMEM] * 3,
        out_shape=shape_of(2, *dims),
        cost_estimate=cost(size * 8, size * 12),
        name="merge",
    )(chain, own, other)


def exchange(axis, outs, chain):
    blocks = lax.axis_size(axis)
    near_pairs = [(i, i ^ 1) for i in range(blocks)]
    away_pairs = [(i, (i - 1 if i % 2 == 0 else i + 1) % blocks) for i in range(blocks)]
    near = lax.ppermute(outs[0], axis, near_pairs)
    parts = [near, lax.ppermute(outs[1], axis, away_pairs)]
    if blocks == 4:
        return parts + [lax.ppermute(outs[2], axis, [(i, i ^ 2) for i in range(blocks)])]
    own, other = outs[0], near
    for level in range(1, blocks.bit_length() - 1):
        own = merge_call(chain, 8 * (level - 1), own, other)
        other = lax.ppermute(own, axis, [(i, i ^ (1 << level)) for i in range(blocks)])
        parts.append(other)
    return parts


def on_device(velocity, derivative_x, derivative_y, derivative_z, smoothing_x, smoothing_y, smoothing_z):
    num_row, num_col = lax.axis_size("row"), lax.axis_size("col")
    pos = jnp.stack([lax.axis_index("row"), lax.axis_index("col")]).astype(jnp.int32)
    count_c, nz, ny, _ = velocity.shape
    lines = ((ny, min(nz, DEPTH // ny), False, num_row), (nz, min(ny, DEPTH // nz), True, num_col))

    (ly, lz), (dy, dz), (cy, cz) = derivative_call(pos, (derivative_y, derivative_z), lines)
    flux, parts = flux_call(velocity, ly, lz, num_row, num_col)
    flux_parts = [
        (exchange("row", y_outs, cy), exchange("col", z_outs, cz)) for y_outs, z_outs in parts
    ]
    (my, mz), (sy, sz), (fy, fz) = smoothing_call(pos, (smoothing_y, smoothing_z), lines)
    for part in range(2):
        flux = flux_x_call(velocity, flux, derivative_x, part, 2)
    out = None
    for c, (y_parts, z_parts) in enumerate(flux_parts):
        t, *z_outs = advance_call(flux, c, mz, cy, cz, dy, dz, y_parts, z_parts, num_row, num_col)
        z_parts = exchange("col", z_outs, fz)
        t, *y_outs = filter_call(t, my, fz, sz, z_parts, num_row, num_col)
        y_parts = exchange("row", y_outs, fy)
        out = last_call(out, t, c, count_c, smoothing_x, fy, sy, y_parts, num_row)
    return out


def solution(mesh):
    in_specs = (P(None, "col", "row", None), P(), P(), P(), P(), P(), P())
    out_specs = P(None, "col", "row", None)
    return jax.shard_map(
        on_device, mesh=mesh, in_specs=in_specs, out_specs=out_specs, check_vma=False
    )
```

time: 1720 us -> 298 us (0.17)
  waiting for transfers between devices: 618 us -> 84.2 us
  local copies, waits for them, and re-layouts: 455 us -> 23.2 us
  blocking collectives: 425 us -> 0 us
  matrix products: 180 us -> 0 us
  Pallas kernels: 0 us -> 146 us
  starting transfers between devices: 25.4 us -> 43.2 us
    all_to_all x4 -> x0, waiting for transfers between devices: 618 us -> none  [the longest x1 259 us: pair_to_y(): lax.all_to_all(swap_lines(leading, num_row, rows_y, narrow), 'row', split...]
    all_to_all x2 -> x0, blocking collectives: 425 us -> none  [the longest x1 277 us: single_to_z(): lax.all_to_all(swap_lines(volume, num_row, rows_z, narrow), 'row', split_...]
    reshape x15 -> x0, local copies, waits for them, and re-layouts: 205 us -> none  [the longest x6 88.9 us: swap_lines(): return grouped.reshape(inner_count, groups, 3 * local_lines * narrow)]
    dot_general x6 -> x0, matrix products: 180 us -> none  [the longest x4 89.2 us: along_lines(): return jnp.dot(matrix, volume, precision=lax.Precision.HIGHEST)]
    pallas_call x0 -> x26, Pallas kernels: none -> 146 us  [the longest x3 31.3 us: last_call(): pl.pallas_call(functools.partial(last_kernel, blocks_y, len(aliased)), gr...]
    ppermute x0 -> x42, waiting for transfers between devices: none -> 84.2 us  [the longest x12 34.8 us: exchange(): near = lax.ppermute(outs[0], axis, near_pairs)]
    mul x7 -> x0, local copies, waits for them, and re-layouts: 63.1 us -> none  [the longest x6 60.6 us: times_component(): grouped * grouped[:, :, component:component + 1]]
    ppermute x0 -> x42, starting transfers between devices: none -> 43.2 us  [the longest x12 13.4 us: exchange(): lax.ppermute(own, axis, [(i, i ^ 1 << level) for i in range(blocks)])]
  transfers between devices with their start and end apart: 4 -> 42, of which waited for: 4 -> 11; matrix products, arithmetic and copies ran while one was open for 12% -> 0% of each run, Pallas kernels for 0% -> 40%
where the time goes in v1:
time: 298 us; the launch traced here: 297 us
  Pallas kernels  146 us (49%)
  waiting for transfers between devices  84.2 us (28%)
  starting transfers between devices  43.2 us (14%)
  local copies, waits for them, and re-layouts  23.2 us (8%)
    ppermute x12, waiting for transfers between devices, exchange(): near = lax.ppermute(outs[0], axis, near_pairs)  34.8 us
    pallas_call x3, Pallas kernels, last_call(): pl.pallas_call(functools.partial(last_kernel, blocks_y, len(aliased)), gr...  31.3 us
    ppermute x12, waiting for transfers between devices, exchange(): lax.ppermute(own, axis, [(i, i ^ 1 << level) for i in range(blocks)])  30 us
    pallas_call x2, Pallas kernels, flux_x_call(): pl.pallas_call(flux_x_kernel, grid=(steps,), in_specs=[block, block, whol...  26.6 us
    pallas_call x3, Pallas kernels, advance_call(): pl.pallas_call(functools.partial(advance_kernel, blocks_y, blocks_z), gri...  24.6 us
    unnamed x128, local copies, waits for them, and re-layouts  23.2 us
    pallas_call x12, Pallas kernels, merge_call(): pl.pallas_call(functools.partial(merge_kernel, first_row, offset), in_spe...  22.8 us
    pallas_call x3, Pallas kernels, filter_call(): pl.pallas_call(functools.partial(filter_kernel, blocks_y, blocks_z), grid...  20.6 us
  transfers between devices with their start and end apart: 42, of which 11 were waited for; matrix products, arithmetic and copies ran while one was open for 0% of the time, Pallas kernels for 40%

profile of v1, /device:TPU:4, one launch (start us, length us, event | category | flops | bytes accessed | tf_op | source)
XLA Modules:
  0.0 296.6 jit_solution(11692509239367320138)
XLA Ops:
  10.3 16.8 %flux_yz.1 = (f32[3,32,32,1024]{3,2,1,0:T(8,128)}, f32[4,32,1024]{2,1,0:T(8,128)}, f32[2,32,1024]{2,1,0:T(8,128)}, f32[4,32,1024]{2,1,0:T(8,128)}, f32[4,32,1024...) custom-call(f32[3,32,32,1024]{3,2,1,0:T(8,128)} %v_ref.5, ...), custom_call_target="tpu_custom_call" | custom-call | flops 12884901888 | bytes 28311552 | tf_op jit(solution)/shard_map/flux_yz/pallas_call | solution.py:655
  27.2 2.0 collective-permute-start.14
  32.2 3.5 %collective-permute-start = (f32[4,32,1024]{2,1,0:T(8,128)}, f32[4,32,1024]{2,1,0:T(8,128)S(1)}, u32[]{:S(2)}, u32[]{:S(2)}) collective-permute-start(f32[4,32,1024]{2,1,0:T(8,128)} %get-tuple-element.62.own_ref), channel_id=1, source_target_pairs={{0,4},{4,0},{8,12},{12,8},{16,20},{20,16},{24,28},{28,24},{1,5},{5... | collective-permute-start | bytes 1572872 | tf_op jit(solution)/shard_map/ppermute | solution.py:770
  35.8 2.2 collective-permute-done.1.refs_7_
  40.9 12.5 %collective-permute-done.28.other_ref.refs_6_ = f32[4,32,1024]{2,1,0:T(8,128)S(1)} collective-permute-done((f32[4,32,1024]{2,1,0:T(8,128)}, f32[4,32,1024]{2,1,0:T(8,128)S(1)}, u32[]{:S(2)}, u32[]{:S(2)}) %collective-permute-start.28) | collective-permute-done | bytes 524320 | tf_op jit(solution)/shard_map/ppermute | solution.py:770
  55.0 2.0 merge.20.own_ref
  57.0 13.3 %collective-permute-done.14.other_ref.refs_6_ = f32[4,32,1024]{2,1,0:T(8,128)S(1)} collective-permute-done((f32[4,32,1024]{2,1,0:T(8,128)}, f32[4,32,1024]{2,1,0:T(8,128)S(1)}, u32[]{:S(2)}, u32[]{:S(2)}) %collective-permute-start.14) | collective-permute-done | bytes 524320 | tf_op jit(solution)/shard_map/ppermute | solution.py:770
  71.9 2.0 merge.16.own_ref
  76.0 4.4 %collective-permute-done.other_ref.refs_6_ = f32[4,32,1024]{2,1,0:T(8,128)S(1)} collective-permute-done((f32[4,32,1024]{2,1,0:T(8,128)}, f32[4,32,1024]{2,1,0:T(8,128)S(1)}, u32[]{:S(2)}, u32[]{:S(2)}) %collective-permute-start) | collective-permute-done | bytes 524320 | tf_op jit(solution)/shard_map/ppermute | solution.py:770
  82.1 13.3 %flux_x.2.t_ref = f32[3,32,32,1024]{3,2,1,0:T(8,128)} custom-call(f32[3,32,32,1024]{3,2,1,0:T(8,128)} %v_ref.5, f32[3,32,32,1024]{3,2,1,0:T(8,128)} %get-tuple-element.56.t_ref, f32[1024,1024]{1,0:T(8,128)} %matrix_ref.3), custom_call_target="tpu_custom_call", output_to_operand_aliasing={{}: (1, {})} | custom-call | flops 6442450944 | bytes 20447232 | tf_op jit(solution)/shard_map/flux_x/pallas_call | solution.py:677
  103.6 2.6 collective-permute-start.31
  106.2 13.3 %flux_x.3.refs_0_ = f32[3,32,32,1024]{3,2,1,0:T(8,128)} custom-call(f32[3,32,32,1024]{3,2,1,0:T(8,128)} %v_ref.5, f32[3,32,32,1024]{3,2,1,0:T(8,128)} %flux_x.2.t_ref, f32[1024,1024]{1,0:T(8,128)} %matrix_ref.3), custom_call_target="tpu_custom_call", output_to_operand_aliasing={{}: (1, {})} | custom-call | flops 6442450944 | bytes 20447232 | tf_op jit(solution)/shard_map/flux_x/pallas_call | solution.py:677
  127.4 8.3 %advance_z.5 = (f32[32,32,1024]{2,1,0:T(8,128)}, f32[4,32,1024]{2,1,0:T(8,128)}, f32[4,32,1024]{2,1,0:T(8,128)}, f32[2,32,1024]{2,1,0:T(8,128)}) custom-call(f32[3,32,32,1024]{3,2,1,0:T(8,128)} %flux_x.3.refs_0_, bf16[608,256]{1,0:T(8,128)(2,1)} %copy-done, f32[28,128]{1,0:T(8,128)} %copy-done.1, f32[12,128]{1,0:T(8,128)} %copy-done.8, ...), custom_call_target="tpu_custom_call" | custom-call | flops 2147483648 | bytes 9437184 | tf_op jit(solution)/shard_map/advance_z/pallas_call | solution.py:697
  138.3 2.6 collective-permute-start.3
  142.1 8.1 %advance_z.4 = (f32[32,32,1024]{2,1,0:T(8,128)}, f32[4,32,1024]{2,1,0:T(8,128)}, f32[4,32,1024]{2,1,0:T(8,128)}, f32[2,32,1024]{2,1,0:T(8,128)}) custom-call(f32[3,32,32,1024]{3,2,1,0:T(8,128)} %flux_x.3.refs_0_, bf16[608,256]{1,0:T(8,128)(2,1)} %copy-done, f32[28,128]{1,0:T(8,128)} %copy-done.1, f32[12,128]{1,0:T(8,128)} %copy-done.8, ...), custom_call_target="tpu_custom_call" | custom-call | flops 2147483648 | bytes 9437184 | tf_op jit(solution)/shard_map/advance_z/pallas_call | solution.py:697
  153.8 8.2 %advance_z.3 = (f32[32,32,1024]{2,1,0:T(8,128)}, f32[4,32,1024]{2,1,0:T(8,128)}, f32[4,32,1024]{2,1,0:T(8,128)}, f32[2,32,1024]{2,1,0:T(8,128)}) custom-call(f32[3,32,32,1024]{3,2,1,0:T(8,128)} %flux_x.3.refs_0_, bf16[608,256]{1,0:T(8,128)(2,1)} %copy-done, f32[28,128]{1,0:T(8,128)} %copy-done.1, f32[12,128]{1,0:T(8,128)} %copy-done.8, ...), custom_call_target="tpu_custom_call" | custom-call | flops 2147483648 | bytes 9437184 | tf_op jit(solution)/shard_map/advance_z/pallas_call | solution.py:697
  162.0 5.2 %collective-permute-done.23.refs_6_ = f32[2,32,1024]{2,1,0:T(8,128)S(1)} collective-permute-done((f32[2,32,1024]{2,1,0:T(8,128)}, f32[2,32,1024]{2,1,0:T(8,128)S(1)}, u32[]{:S(2)}, u32[]{:S(2)}) %collective-permute-start.23) | collective-permute-done | bytes 262176 | tf_op jit(solution)/shard_map/ppermute | solution.py:773
  169.3 6.9 %filter_y.5 = (f32[32,32,1024]{2,1,0:T(8,128)}, f32[4,32,1024]{2,1,0:T(8,128)}, f32[2,32,1024]{2,1,0:T(8,128)}) custom-call(f32[32,32,1024]{2,1,0:T(8,128)} %get-tuple-element.96.refs_0_, bf16[608,256]{1,0:T(8,128)(2,1)} %copy-done.16, f32[12,128]{1,0:T(8,128)} %copy-done.20, f32[6,32,128]{2,1,0:T(8,128)} %copy-done.19, ...), custom_call_target="tpu_custom_call" | custom-call | flops 2147483648 | bytes 9437184 | tf_op jit(solution)/shard_map/filter_y/pallas_call | solution.py:715
  177.6 6.9 %filter_y.4 = (f32[32,32,1024]{2,1,0:T(8,128)}, f32[4,32,1024]{2,1,0:T(8,128)}, f32[2,32,1024]{2,1,0:T(8,128)}) custom-call(f32[32,32,1024]{2,1,0:T(8,128)} %get-tuple-element.84.refs_0_, bf16[608,256]{1,0:T(8,128)(2,1)} %copy-done.16, f32[12,128]{1,0:T(8,128)} %copy-done.20, f32[6,32,128]{2,1,0:T(8,128)} %copy-done.19, f32[4,32,1024]{2,1,0:T(8,128)} %copy-done.52, ...), custom_call_target="tpu_custom_call" | custom-call | flops 2147483648 | bytes 9437184 | tf_op jit(solution)/shard_map/filter_y/pallas_call | solution.py:715
  186.0 7.9 %collective-permute-done.9.refs_6_ = f32[2,32,1024]{2,1,0:T(8,128)S(1)} collective-permute-done((f32[2,32,1024]{2,1,0:T(8,128)}, f32[2,32,1024]{2,1,0:T(8,128)S(1)}, u32[]{:S(2)}, u32[]{:S(2)}) %collective-permute-start.9) | collective-permute-done | bytes 262176 | tf_op jit(solution)/shard_map/ppermute | solution.py:773
  194.9 6.9 %filter_y.3 = (f32[32,32,1024]{2,1,0:T(8,128)}, f32[4,32,1024]{2,1,0:T(8,128)}, f32[2,32,1024]{2,1,0:T(8,128)}) custom-call(f32[32,32,1024]{2,1,0:T(8,128)} %get-tuple-element.67.refs_0_, bf16[608,256]{1,0:T(8,128)(2,1)} %copy-done.16, f32[12,128]{1,0:T(8,128)} %copy-done.20, f32[6,32,128]{2,1,0:T(8,128)} %copy-done.19, f32[4,32,1024]{2,1,0:T(8,128)} %copy-done.54, ...), custom_call_target="tpu_custom_call" | custom-call | flops 2147483648 | bytes 9437184 | tf_op jit(solution)/shard_map/filter_y/pallas_call | solution.py:715
  203.2 2.0 merge.22.own_ref
  207.5 2.0 merge.18.own_ref
  210.0 4.6 %collective-permute-done.10.other_ref.refs_4_ = f32[4,32,1024]{2,1,0:T(8,128)S(1)} collective-permute-done((f32[4,32,1024]{2,1,0:T(8,128)}, f32[4,32,1024]{2,1,0:T(8,128)S(1)}, u32[]{:S(2)}, u32[]{:S(2)}) %collective-permute-start.10) | collective-permute-done | bytes 524320 | tf_op jit(solution)/shard_map/ppermute | solution.py:770
  215.4 2.0 merge.14.own_ref
  222.3 2.5 collective-permute-start.25
  227.4 2.7 collective-permute-done.12.other_ref.refs_6_
  232.6 4.1 %collective-permute-done.39.refs_5_ = f32[2,32,1024]{2,1,0:T(8,128)S(1)} collective-permute-done((f32[2,32,1024]{2,1,0:T(8,128)S(1)}, f32[2,32,1024]{2,1,0:T(8,128)S(1)}, u32[]{:S(2)}, u32[]{:S(2)}) %collective-permute-start.39) | collective-permute-done | bytes 262176 | tf_op jit(solution)/shard_map/ppermute | solution.py:771
  237.0 26.0 %collective-permute-done.41.refs_7_ = f32[2,32,1024]{2,1,0:T(8,128)S(1)} collective-permute-done((f32[2,32,1024]{2,1,0:T(8,128)}, f32[2,32,1024]{2,1,0:T(8,128)S(1)}, u32[]{:S(2)}, u32[]{:S(2)}) %collective-permute-start.41) | collective-permute-done | bytes 262176 | tf_op jit(solution)/shard_map/ppermute | solution.py:777
  263.7 10.4 %filter_x.3.refs_8_ = f32[3,32,32,1024]{3,2,1,0:T(8,128)} custom-call(f32[32,32,1024]{2,1,0:T(8,128)} %get-tuple-element.100.refs_0_, f32[1024,1024]{1,0:T(8,128)} %refs_1_.9, f32[28,128]{1,0:T(8,128)} %copy-done.2, f32[6,32,128]{2,1,0:T(8,128)} %copy-done.5, f32[4,32,1024]{2,1,0:T(8,128)} %copy-done.36, f32[2,32,1024]{2,1,0:T(8,128)} %copy-done.62, ...), custom_call_target="tpu_custom_call" | custom-call | flops 6442450944 | bytes 13631488 | tf_op jit(solution)/shard_map/filter_x/pallas_call | solution.py:736
  274.9 10.4 %filter_x.4.refs_8_ = f32[3,32,32,1024]{3,2,1,0:T(8,128)} custom-call(f32[32,32,1024]{2,1,0:T(8,128)} %get-tuple-element.88.refs_0_, f32[1024,1024]{1,0:T(8,128)} %refs_1_.9, f32[28,128]{1,0:T(8,128)} %copy-done.2, f32[6,32,128]{2,1,0:T(8,128)} %copy-done.5, f32[4,32,1024]{2,1,0:T(8,128)} %copy-done.21, ...), custom_call_target="tpu_custom_call", output_to_operand_aliasing={{}: (8, {})} | custom-call | flops 6442450944 | bytes 13631488 | tf_op jit(solution)/shard_map/filter_x/pallas_call | solution.py:736
  286.2 10.4 %filter_x.5 = f32[3,32,32,1024]{3,2,1,0:T(8,128)} custom-call(f32[32,32,1024]{2,1,0:T(8,128)} %get-tuple-element.74.refs_0_, f32[1024,1024]{1,0:T(8,128)} %refs_1_.9, f32[28,128]{1,0:T(8,128)} %copy-done.2, f32[6,32,128]{2,1,0:T(8,128)} %copy-done.5, f32[4,32,1024]{2,1,0:T(8,128)} %copy-done.22, ...), custom_call_target="tpu_custom_call", output_to_operand_aliasing={{}: (8, {})} | custom-call | flops 6442450944 | bytes 13631488 | tf_op jit(solution)/shard_map/filter_x/pallas_call | solution.py:736
  (207 shorter events, 70.3 us)
Async XLA Ops:
  27.1 26.3 %collective-permute-start.28 = (f32[4,32,1024]{2,1,0:T(8,128)}, f32[4,32,1024]{2,1,0:T(8,128)S(1)}, u32[]{:S(2)}, u32[]{:S(2)}) collective-permute-start(f32[4,32,1024]{2,1,0:T(8,128)} %get-tuple-element.91.own_ref), channel_id=1, source_target_pairs={{0,4},{4,0},{8,12},{12,8},{16,20},{20,16},{24,28},{28,24},{1,5},{5... | collective-permute-start | bytes 1572872 | tf_op jit(solution)/shard_map/ppermute | solution.py:770
  27.2 43.1 %collective-permute-start.14 = (f32[4,32,1024]{2,1,0:T(8,128)}, f32[4,32,1024]{2,1,0:T(8,128)S(1)}, u32[]{:S(2)}, u32[]{:S(2)}) collective-permute-start(f32[4,32,1024]{2,1,0:T(8,128)} %get-tuple-element.79.own_ref), channel_id=1, source_target_pairs={{0,4},{4,0},{8,12},{12,8},{16,20},{20,16},{24,28},{28,24},{1,5},{5... | collective-permute-start | bytes 1572872 | tf_op jit(solution)/shard_map/ppermute | solution.py:770
  32.2 48.2 %collective-permute-start = (f32[4,32,1024]{2,1,0:T(8,128)}, f32[4,32,1024]{2,1,0:T(8,128)S(1)}, u32[]{:S(2)}, u32[]{:S(2)}) collective-permute-start(f32[4,32,1024]{2,1,0:T(8,128)} %get-tuple-element.62.own_ref), channel_id=1, source_target_pairs={{0,4},{4,0},{8,12},{12,8},{16,20},{20,16},{24,28},{28,24},{1,5},{5... | collective-permute-start | bytes 1572872 | tf_op jit(solution)/shard_map/ppermute | solution.py:770
  37.9 36.0 %collective-permute-start.15 = (f32[2,32,1024]{2,1,0:T(8,128)}, f32[2,32,1024]{2,1,0:T(8,128)S(1)}, u32[]{:S(2)}, u32[]{:S(2)}) collective-permute-start(f32[2,32,1024]{2,1,0:T(8,128)} %get-tuple-element.80), channel_id=1, source_target_pairs={{0,28},{4,8},{8,4},{12,16},{16,12},{20,24},{24,20},{28,0},{1,29},{... | collective-permute-start | bytes 786440 | tf_op jit(solution)/shard_map/ppermute | solution.py:771
  39.5 35.9 %collective-permute-start.20 = (f32[2,32,1024]{2,1,0:T(8,128)}, f32[2,32,1024]{2,1,0:T(8,128)S(1)}, u32[]{:S(2)}, u32[]{:S(2)}) collective-permute-start(f32[2,32,1024]{2,1,0:T(8,128)} %get-tuple-element.83), channel_id=1, source_target_pairs={{0,2},{1,3},{2,0},{3,1},{4,6},{5,7},{6,4},{7,5},{8,10},{9,11},{10,... | collective-permute-start | bytes 786440 | tf_op jit(solution)/shard_map/ppermute | solution.py:773
  53.5 22.0 %collective-permute-start.29 = (f32[2,32,1024]{2,1,0:T(8,128)}, f32[2,32,1024]{2,1,0:T(8,128)S(1)}, u32[]{:S(2)}, u32[]{:S(2)}) collective-permute-start(f32[2,32,1024]{2,1,0:T(8,128)} %get-tuple-element.92), channel_id=1, source_target_pairs={{0,28},{4,8},{8,4},{12,16},{16,12},{20,24},{24,20},{28,0},{1,29},{... | collective-permute-start | bytes 786440 | tf_op jit(solution)/shard_map/ppermute | solution.py:771
  73.9 25.3 %collective-permute-start.34 = (f32[2,32,1024]{2,1,0:T(8,128)}, f32[2,32,1024]{2,1,0:T(8,128)S(1)}, u32[]{:S(2)}, u32[]{:S(2)}) collective-permute-start(f32[2,32,1024]{2,1,0:T(8,128)} %get-tuple-element.95), channel_id=1, source_target_pairs={{0,2},{1,3},{2,0},{3,1},{4,6},{5,7},{6,4},{7,5},{8,10},{9,11},{10,... | collective-permute-start | bytes 786440 | tf_op jit(solution)/shard_map/ppermute | solution.py:773
  75.4 25.3 %collective-permute-start.4 = (f32[4,32,1024]{2,1,0:T(8,128)}, f32[4,32,1024]{2,1,0:T(8,128)S(1)}, u32[]{:S(2)}, u32[]{:S(2)}) collective-permute-start(f32[4,32,1024]{2,1,0:T(8,128)} %get-tuple-element.64), channel_id=1, source_target_pairs={{0,1},{1,0},{2,3},{3,2},{4,5},{5,4},{6,7},{7,6},{8,9},{9,8},{10,11... | collective-permute-start | bytes 1572872 | tf_op jit(solution)/shard_map/ppermute | solution.py:770
  75.5 25.4 %collective-permute-start.32 = (f32[4,32,1024]{2,1,0:T(8,128)}, f32[4,32,1024]{2,1,0:T(8,128)S(1)}, u32[]{:S(2)}, u32[]{:S(2)}) collective-permute-start(f32[4,32,1024]{2,1,0:T(8,128)} %get-tuple-element.93), channel_id=1, source_target_pairs={{0,1},{1,0},{2,3},{3,2},{4,5},{5,4},{6,7},{7,6},{8,9},{9,8},{10,11... | collective-permute-start | bytes 1572872 | tf_op jit(solution)/shard_map/ppermute | solution.py:770
  80.4 22.7 %collective-permute-start.33 = (f32[4,32,1024]{2,1,0:T(8,128)}, f32[4,32,1024]{2,1,0:T(8,128)}, u32[]{:S(2)}, u32[]{:S(2)}) collective-permute-start(f32[4,32,1024]{2,1,0:T(8,128)} %get-tuple-element.94), channel_id=1, source_target_pairs={{0,3},{1,2},{2,1},{3,0},{4,7},{5,6},{6,5},{7,4},{8,11},{9,10},{10,... | collective-permute-start | bytes 1572872 | tf_op jit(solution)/shard_map/ppermute | solution.py:771
  80.5 23.1 %collective-permute-start.16 = (f32[2,32,1024]{2,1,0:T(8,128)}, f32[2,32,1024]{2,1,0:T(8,128)S(1)}, u32[]{:S(2)}, u32[]{:S(2)}) collective-permute-start(f32[2,32,1024]{2,1,0:T(8,128)} %merge.16.own_ref), channel_id=1, source_target_pairs={{0,8},{4,12},{8,0},{12,4},{16,24},{20,28},{24,16},{28,20},{1,9},{5... | collective-permute-start | bytes 786440 | tf_op jit(solution)/shard_map/ppermute | solution.py:777
  99.2 51.0 %collective-permute-start.5 = (f32[4,32,1024]{2,1,0:T(8,128)S(1)}, f32[4,32,1024]{2,1,0:T(8,128)S(1)}, u32[]{:S(2)}, u32[]{:S(2)}) collective-permute-start(f32[4,32,1024]{2,1,0:T(8,128)S(1)} %copy-done.50), channel_id=1, source_target_pairs={{0,3},{1,2},{2,1},{3,0},{4,7},{5,6},{6,5},{7,4},{8,11},{9,10},{10,... | collective-permute-start | bytes 1572872 | tf_op jit(solution)/shard_map/ppermute | solution.py:771
  100.7 37.6 %collective-permute-start.18 = (f32[4,32,1024]{2,1,0:T(8,128)}, f32[4,32,1024]{2,1,0:T(8,128)S(1)}, u32[]{:S(2)}, u32[]{:S(2)}) collective-permute-start(f32[4,32,1024]{2,1,0:T(8,128)} %get-tuple-element.81), channel_id=1, source_target_pairs={{0,1},{1,0},{2,3},{3,2},{4,5},{5,4},{6,7},{7,6},{8,9},{9,8},{10,11... | collective-permute-start | bytes 1572872 | tf_op jit(solution)/shard_map/ppermute | solution.py:770
  101.7 39.1 %collective-permute-start.19 = (f32[4,32,1024]{2,1,0:T(8,128)}, f32[4,32,1024]{2,1,0:T(8,128)S(1)}, u32[]{:S(2)}, u32[]{:S(2)}) collective-permute-start(f32[4,32,1024]{2,1,0:T(8,128)} %get-tuple-element.82), channel_id=1, source_target_pairs={{0,3},{1,2},{2,1},{3,0},{4,7},{5,6},{6,5},{7,4},{8,11},{9,10},{10,... | collective-permute-start | bytes 1572872 | tf_op jit(solution)/shard_map/ppermute | solution.py:771
  103.1 32.6 %collective-permute-start.2 = (f32[2,32,1024]{2,1,0:T(8,128)}, f32[2,32,1024]{2,1,0:T(8,128)S(1)}, u32[]{:S(2)}, u32[]{:S(2)}) collective-permute-start(f32[2,32,1024]{2,1,0:T(8,128)} %merge.12.own_ref), channel_id=1, source_target_pairs={{0,8},{4,12},{8,0},{12,4},{16,24},{20,28},{24,16},{28,20},{1,9},{5... | collective-permute-start | bytes 786440 | tf_op jit(solution)/shard_map/ppermute | solution.py:777
  103.6 17.7 %collective-permute-start.31 = (f32[2,32,1024]{2,1,0:T(8,128)}, f32[2,32,1024]{2,1,0:T(8,128)}, u32[]{:S(2)}, u32[]{:S(2)}) collective-permute-start(f32[2,32,1024]{2,1,0:T(8,128)} %merge.21), channel_id=1, source_target_pairs={{0,16},{4,20},{8,24},{12,28},{16,0},{20,4},{24,8},{28,12},{1,17},{... | collective-permute-start | bytes 786440 | tf_op jit(solution)/shard_map/ppermute | solution.py:777
  121.3 20.1 %collective-permute-start.17 = (f32[2,32,1024]{2,1,0:T(8,128)}, f32[2,32,1024]{2,1,0:T(8,128)S(1)}, u32[]{:S(2)}, u32[]{:S(2)}) collective-permute-start(f32[2,32,1024]{2,1,0:T(8,128)} %merge.17), channel_id=1, source_target_pairs={{0,16},{4,20},{8,24},{12,28},{16,0},{20,4},{24,8},{28,12},{1,17},{... | collective-permute-start | bytes 786440 | tf_op jit(solution)/shard_map/ppermute | solution.py:777
  135.8 31.4 %collective-permute-start.35 = (f32[4,32,1024]{2,1,0:T(8,128)}, f32[4,32,1024]{2,1,0:T(8,128)}, u32[]{:S(2)}, u32[]{:S(2)}) collective-permute-start(f32[4,32,1024]{2,1,0:T(8,128)} %get-tuple-element.97), channel_id=1, source_target_pairs={{0,1},{1,0},{2,3},{3,2},{4,5},{5,4},{6,7},{7,6},{8,9},{9,8},{10,11... | collective-permute-start | bytes 1572872 | tf_op jit(solution)/shard_map/ppermute | solution.py:770
  141.4 26.4 %collective-permute-start.36 = (f32[4,32,1024]{2,1,0:T(8,128)}, f32[4,32,1024]{2,1,0:T(8,128)S(1)}, u32[]{:S(2)}, u32[]{:S(2)}) collective-permute-start(f32[4,32,1024]{2,1,0:T(8,128)} %get-tuple-element.98), channel_id=1, source_target_pairs={{0,3},{1,2},{2,1},{3,0},{4,7},{5,6},{6,5},{7,4},{8,11},{9,10},{10,... | collective-permute-start | bytes 1572872 | tf_op jit(solution)/shard_map/ppermute | solution.py:771
  153.1 23.1 %collective-permute-start.21 = (f32[4,32,1024]{2,1,0:T(8,128)}, f32[4,32,1024]{2,1,0:T(8,128)S(1)}, u32[]{:S(2)}, u32[]{:S(2)}) collective-permute-start(f32[4,32,1024]{2,1,0:T(8,128)} %get-tuple-element.85), channel_id=1, source_target_pairs={{0,1},{1,0},{2,3},{3,2},{4,5},{5,4},{6,7},{7,6},{8,9},{9,8},{10,11... | collective-permute-start | bytes 1572872 | tf_op jit(solution)/shard_map/ppermute | solution.py:770
  153.1 23.6 %collective-permute-start.22 = (f32[4,32,1024]{2,1,0:T(8,128)}, f32[4,32,1024]{2,1,0:T(8,128)S(1)}, u32[]{:S(2)}, u32[]{:S(2)}) collective-permute-start(f32[4,32,1024]{2,1,0:T(8,128)} %get-tuple-element.86), channel_id=1, source_target_pairs={{0,3},{1,2},{2,1},{3,0},{4,7},{5,6},{6,5},{7,4},{8,11},{9,10},{10,... | collective-permute-start | bytes 1572872 | tf_op jit(solution)/shard_map/ppermute | solution.py:771
  167.1 26.7 %collective-permute-start.7 = (f32[4,32,1024]{2,1,0:T(8,128)}, f32[4,32,1024]{2,1,0:T(8,128)S(1)}, u32[]{:S(2)}, u32[]{:S(2)}) collective-permute-start(f32[4,32,1024]{2,1,0:T(8,128)} %get-tuple-element.71), channel_id=1, source_target_pairs={{0,1},{1,0},{2,3},{3,2},{4,5},{5,4},{6,7},{7,6},{8,9},{9,8},{10,11... | collective-permute-start | bytes 1572872 | tf_op jit(solution)/shard_map/ppermute | solution.py:770
  167.1 26.7 %collective-permute-start.8 = (f32[4,32,1024]{2,1,0:T(8,128)}, f32[4,32,1024]{2,1,0:T(8,128)S(1)}, u32[]{:S(2)}, u32[]{:S(2)}) collective-permute-start(f32[4,32,1024]{2,1,0:T(8,128)} %get-tuple-element.72), channel_id=1, source_target_pairs={{0,3},{1,2},{2,1},{3,0},{4,7},{5,6},{6,5},{7,4},{8,11},{9,10},{10,... | collective-permute-start | bytes 1572872 | tf_op jit(solution)/shard_map/ppermute | solution.py:771
  167.8 26.0 %collective-permute-start.9 = (f32[2,32,1024]{2,1,0:T(8,128)}, f32[2,32,1024]{2,1,0:T(8,128)S(1)}, u32[]{:S(2)}, u32[]{:S(2)}) collective-permute-start(f32[2,32,1024]{2,1,0:T(8,128)} %get-tuple-element.73), channel_id=1, source_target_pairs={{0,2},{1,3},{2,0},{3,1},{4,6},{5,7},{6,4},{7,5},{8,10},{9,11},{10,... | collective-permute-start | bytes 786440 | tf_op jit(solution)/shard_map/ppermute | solution.py:773
  176.2 26.2 %collective-permute-start.38 = (f32[4,32,1024]{2,1,0:T(8,128)}, f32[4,32,1024]{2,1,0:T(8,128)S(1)}, u32[]{:S(2)}, u32[]{:S(2)}) collective-permute-start(f32[4,32,1024]{2,1,0:T(8,128)} %get-tuple-element.101.own_ref), channel_id=1, source_target_pairs={{0,4},{4,0},{8,12},{12,8},{16,20},{20,16},{24,28},{28,24},{1,5},{5... | collective-permute-start | bytes 1572872 | tf_op jit(solution)/shard_map/ppermute | solution.py:770
  184.4 22.3 %collective-permute-start.24 = (f32[4,32,1024]{2,1,0:T(8,128)}, f32[4,32,1024]{2,1,0:T(8,128)S(1)}, u32[]{:S(2)}, u32[]{:S(2)}) collective-permute-start(f32[4,32,1024]{2,1,0:T(8,128)} %get-tuple-element.89.own_ref), channel_id=1, source_target_pairs={{0,4},{4,0},{8,12},{12,8},{16,20},{20,16},{24,28},{28,24},{1,5},{5... | collective-permute-start | bytes 1572872 | tf_op jit(solution)/shard_map/ppermute | solution.py:770
  219.0 17.8 %collective-permute-start.39 = (f32[2,32,1024]{2,1,0:T(8,128)S(1)}, f32[2,32,1024]{2,1,0:T(8,128)S(1)}, u32[]{:S(2)}, u32[]{:S(2)}) collective-permute-start(f32[2,32,1024]{2,1,0:T(8,128)S(1)} %copy-done.56), channel_id=1, source_target_pairs={{0,28},{4,8},{8,4},{12,16},{16,12},{20,24},{24,20},{28,0},{1,29},{... | collective-permute-start | bytes 786440 | tf_op jit(solution)/shard_map/ppermute | solution.py:771
  221.9 41.1 %collective-permute-start.41 = (f32[2,32,1024]{2,1,0:T(8,128)}, f32[2,32,1024]{2,1,0:T(8,128)S(1)}, u32[]{:S(2)}, u32[]{:S(2)}) collective-permute-start(f32[2,32,1024]{2,1,0:T(8,128)} %merge.23), channel_id=1, source_target_pairs={{0,16},{4,20},{8,24},{12,28},{16,0},{20,4},{24,8},{28,12},{1,17},{... | collective-permute-start | bytes 786440 | tf_op jit(solution)/shard_map/ppermute | solution.py:777
  222.3 51.8 %collective-permute-start.25 = (f32[2,32,1024]{2,1,0:T(8,128)S(1)}, f32[2,32,1024]{2,1,0:T(8,128)S(1)}, u32[]{:S(2)}, u32[]{:S(2)}) collective-permute-start(f32[2,32,1024]{2,1,0:T(8,128)S(1)} %copy-done.57), channel_id=1, source_target_pairs={{0,28},{4,8},{8,4},{12,16},{16,12},{20,24},{24,20},{28,0},{1,29},{... | collective-permute-start | bytes 786440 | tf_op jit(solution)/shard_map/ppermute | solution.py:771
  224.8 60.5 %collective-permute-start.11 = (f32[2,32,1024]{2,1,0:T(8,128)S(1)}, f32[2,32,1024]{2,1,0:T(8,128)S(1)}, u32[]{:S(2)}, u32[]{:S(2)}) collective-permute-start(f32[2,32,1024]{2,1,0:T(8,128)S(1)} %copy-done.58), channel_id=1, source_target_pairs={{0,28},{4,8},{8,4},{12,16},{16,12},{20,24},{24,20},{28,0},{1,29},{... | collective-permute-start | bytes 786440 | tf_op jit(solution)/shard_map/ppermute | solution.py:771
  230.1 44.0 %collective-permute-start.27 = (f32[2,32,1024]{2,1,0:T(8,128)}, f32[2,32,1024]{2,1,0:T(8,128)S(1)}, u32[]{:S(2)}, u32[]{:S(2)}) collective-permute-start(f32[2,32,1024]{2,1,0:T(8,128)} %merge.19), channel_id=1, source_target_pairs={{0,16},{4,20},{8,24},{12,28},{16,0},{20,4},{24,8},{28,12},{1,17},{... | collective-permute-start | bytes 786440 | tf_op jit(solution)/shard_map/ppermute | solution.py:777
  236.7 48.6 %collective-permute-start.13 = (f32[2,32,1024]{2,1,0:T(8,128)}, f32[2,32,1024]{2,1,0:T(8,128)S(1)}, u32[]{:S(2)}, u32[]{:S(2)}) collective-permute-start(f32[2,32,1024]{2,1,0:T(8,128)} %merge.15), channel_id=1, source_target_pairs={{0,16},{4,20},{8,24},{12,28},{16,0},{20,4},{24,8},{28,12},{1,17},{... | collective-permute-start | bytes 786440 | tf_op jit(solution)/shard_map/ppermute | solution.py:777
  (74 other events, 474.5 us)

commit v2 on v1

--- a/solution.py
+++ b/solution.py
@@ -17,6 +17,9 @@
 ROWS = 128
 TILE = 256
 MIB = 1024 * 1024
+SMALL_MIB = 24
+ADVANCE_MIB = 50
+WEIGHT = 1000
 
 
 def numpy_lanes(blocks):
@@ -98,20 +101,12 @@
         h_left = combine([(left, h_b), (left * ab, k_o), (left * ab * go, g_in), (left * bb, h_in)])
         g_right = combine([(right, k_b), (right * gb, g_in), (right * db, h_o), (right * db * bo, h_in)])
         h_in, g_in = choose(level, h_in, h_left), choose(level, g_right, g_in)
-    if blocks == 4:
-        merge = [flip(value, 1) for value in merges[0]]
-
-        def raw(end):
-            over = [end[2] * merge[j] + end[3] * merge[4 + j] for j in range(4)]
-            return end[:2] + over[2:] + over[:2]
-
-        return raw(g_in) + raw(h_in)
     return sum(merges, []) + g_in + h_in
 
 
 def table_counts(blocks):
     levels = blocks.bit_length() - 1
-    return (0, 6) if blocks == 4 else (8 * (levels - 1), 2 * levels)
+    return 8 * (levels - 1), 2 * levels
 
 
 def end_rows(a_past, stencil_past, sign):
@@ -235,23 +230,19 @@
     out_ref[...] = jnp.broadcast_to(own, out_ref.shape)
 
 
-def derivative_kernel(lines, pos_ref, *refs):
-    refs = list(refs)
-    take = lambda k: [refs.pop(0) for _ in range(k)]
-    matrices, tap_refs, spreads, chain_refs = (take(len(lines)) for _ in range(4))
-    stacks, tables, chains = (take(len(lines)) for _ in range(3))
-    for axis, (n, group, inner, beside) in enumerate(lines):
+def prepare_derivatives(lines, pos_ref, matrices, constants_ref, stacks, tables, chains):
+    for axis, (n, group, inner, beside, (tap_at, spread_at, chain_at, chain_rows)) in enumerate(lines):
         block = pos_ref[axis]
         odd = block % 2 == 1
         rows = block_rows(matrices[axis], block, n)
         count = rows.shape[1]
         next_one = iota((n, count), 1) == (block * n + iota((n, count), 0) + 1) % count
         metric = jnp.sum(jnp.where(next_one, rows, 0.0), axis=1, keepdims=True) * (1.0 / beside)
-        taps = [tap_refs[axis][j : j + 1, :] for j in range(6)]
+        taps = [constants_ref[tap_at + j : tap_at + j + 1, : n * group] for j in range(6)]
         store_stack(stacks[axis], -STEP * rows, ordered(odd, taps), block, n, group, inner)
-        spread = [spreads[axis][:, j : j + 1] for j in range(2)]
+        spread = [constants_ref[spread_at : spread_at + n, j : j + 1] for j in range(2)]
         store_table(tables[axis], odd, spread, -STEP * metric)
-        store_chain(chains[axis], chain_refs[axis][...], block)
+        store_chain(chains[axis], constants_ref[chain_at : chain_at + chain_rows, :SPAN], block)
 
 
 def filter_stencils(a):
@@ -340,40 +331,40 @@
     return jax.ShapeDtypeStruct((2 * group * (n + 6), group * n), jnp.bfloat16)
 
 
-def derivative_call(pos, matrices, lines):
-    ready = [pade_line(m.shape[0], blocks) for m, (_, _, _, blocks) in zip(matrices, lines)]
-    expanded = []
-    for (n, group, inner, _), (_, taps, _, _) in zip(lines, ready):
+def derivative_constants(matrices, lines):
+    rows, setup, at = [], [], 0
+
+    def add(value):
+        nonlocal at
+        start = at
+        high = -(-value.shape[0] // 8) * 8
+        rows.append(np.pad(value, ((0, high - value.shape[0]), (0, DEPTH - value.shape[1]))))
+        at += high
+        return start
+
+    for matrix, (n, group, inner, blocks) in zip(matrices, lines):
+        beside, taps, spread, table = pade_line(matrix.shape[0], blocks)
         place, _ = place_of(np.arange(n * group), n, group, inner)
-        expanded.append(jnp.asarray(taps[place].T.astype(np.float32)))
-    spreads = [jnp.asarray(spread.astype(np.float32)) for _, _, spread, _ in ready]
-    chains = [jnp.asarray(table.astype(np.float32)) for _, _, _, table in ready]
-    setup = [(n, group, inner, beside) for (n, group, inner, _), (beside, _, _, _) in zip(lines, ready)]
-    out = pl.pallas_call(
-        functools.partial(derivative_kernel, setup),
-        in_specs=[SMEM] + [VMEM] * (4 * len(lines)),
-        out_shape=[stack_shape(n, group) for n, group, _, _ in lines]
-        + [shape_of(6, n, SPAN) for n, _, _, _ in lines]
-        + [shape_of(*chain.shape) for chain in chains],
-        compiler_params=params(32),
-        name="derivative_lines",
-    )(pos, *matrices, *expanded, *spreads, *chains)
-    k = len(lines)
-    return out[:k], out[k : 2 * k], out[2 * k :]
-
-
-def smoothing_call(pos, matrices, lines):
+        where = (add(taps[place].T), add(spread), add(table), table.shape[0])
+        setup.append((n, group, inner, beside, where))
+    return jnp.asarray(np.concatenate(rows, axis=0).astype(np.float32)), setup
+
+
+def smoothing_call(order, pos, matrices, lines):
     rows = [merged + 2 * planes for merged, planes in (table_counts(blocks) for _, _, _, blocks in lines)]
-    out = pl.pallas_call(
+    out, _ = order.call(
         functools.partial(smoothing_kernel, lines),
-        in_specs=[SMEM] + [VMEM] * len(lines),
-        out_shape=[stack_shape(n, group) for n, group, _, _ in lines]
+        [pos, *matrices],
+        [SMEM] + [VMEM] * len(lines),
+        [VMEM] * (3 * len(lines)),
+        [stack_shape(n, group) for n, group, _, _ in lines]
         + [shape_of(6, n, SPAN) for n, _, _, _ in lines]
         + [shape_of(r, SPAN) for r in rows],
         scratch_shapes=[pltpu.VMEM((4, n, SPAN), jnp.float32) for n, _, _, _ in lines],
-        compiler_params=params(32),
+        compiler_params=params(SMALL_MIB),
+        cost_estimate=cost(10**7, 10**7),
         name="smoothing_lines",
-    )(pos, *matrices)
+    )
     k = len(lines)
     return out[:k], out[k : 2 * k], out[2 * k :]
 
@@ -397,23 +388,12 @@
             ref[plane, at : at + group, :] = taps[j * group : (j + 1) * group]
 
 
-def writers_of(outs, blocks):
-    if blocks == 4:
-        near, away, ends = outs
-        return [
-            [(near, 0)],
-            [(near, 1)],
-            [(near, 2), (away, 2), (ends, 0)],
-            [(near, 3), (away, 3), (ends, 1)],
-            [(away, 0)],
-            [(away, 1)],
-        ]
+def writers_of(outs, near_at=0, away_at=0):
     near, away = outs
-    return [[(near, j)] for j in range(4)] + [[(away, j)] for j in range(2)]
-
-
-def out_planes(blocks):
-    return [4, 4, 2] if blocks == 4 else [4, 2]
+    return [[(near, 4 * near_at + j)] for j in range(4)] + [[(away, 2 * away_at + j)] for j in range(2)]
+
+
+OUT_PLANES = (4, 2)
 
 
 def along_y(stack, read, count_z, count_y, write, writers):
@@ -434,12 +414,18 @@
         put_taps(result[count_z * group :], group, at, writers)
 
 
-def flux_kernel(blocks_y, blocks_z, v_ref, ly_ref, lz_ref, t_ref, *outs):
+def flux_kernel(lines, blocks_y, blocks_z, pos_ref, v_ref, dy_ref, dz_ref, constants_ref, t_ref, *refs):
     count_c, count_z, count_y, _ = v_ref.shape
-    outs = list(outs)
+    *tables, ly_ref, lz_ref = refs[-6:]
+    outs = list(refs[:-6])
+
+    @pl.when(pl.program_id(0) == 0)
+    def _():
+        prepare_derivatives(
+            lines, pos_ref, (dy_ref, dz_ref), constants_ref, (ly_ref, lz_ref), tables[:2], tables[2:]
+        )
+
     for c in range(count_c):
-        outs_y = [outs.pop(0) for _ in out_planes(blocks_y)]
-        outs_z = [outs.pop(0) for _ in out_planes(blocks_z)]
 
         def write_y(zs, ys, value, c=c):
             t_ref[c, zs, ys] = v_ref[c, zs, ys] + value
@@ -448,8 +434,10 @@
             t_ref[c, zs, ys] += value
 
         flux = lambda k: lambda zs, ys: v_ref[c, zs, ys] * v_ref[k, zs, ys]
-        along_y(ly_ref[...], flux(1), count_z, count_y, write_y, writers_of(outs_y, blocks_y))
-        along_z(lz_ref[...], flux(2), count_z, count_y, write_z, writers_of(outs_z, blocks_z))
+        y_writers = writers_of((outs[c], outs[count_c]), 0, c)
+        z_writers = writers_of(outs[count_c + 1 :], c, c)
+        along_y(ly_ref[...], flux(1), count_z, count_y, write_y, y_writers)
+        along_z(lz_ref[...], flux(2), count_z, count_y, write_z, z_writers)
 
 
 def ends_of(chain_ref, blocks, planes):
@@ -463,11 +451,10 @@
 
 
 def far_planes(parts, blocks, xs):
-    if blocks == 4:
-        near, away, opposite = parts
-        return [near[2, :, xs], near[3, :, xs], away[2, :, xs], away[3, :, xs], opposite[0, :, xs], opposite[1, :, xs]]
-    near, _, *rest = parts
-    return [near[2, :, xs], near[3, :, xs]] + [ref[j, :, xs] for ref in rest for j in range(2)]
+    near, away, *rest = parts
+    far = [(near, 2), (near, 3)] + ([(away, 2), (away, 3)] if blocks == 4 else [])
+    far += [(ref, j) for ref in rest for j in range(2)]
+    return [ref[j, :, xs] for ref, j in far]
 
 
 def mend_y(read, write, chain_ref, table_ref, parts, blocks, ends_ref, dims):
@@ -507,7 +494,7 @@
     t_ref, lz_ref, cy_ref, cz_ref, sy_ref, sz_ref = take(6)
     y_parts, z_parts = take(part_count(blocks_y)), take(part_count(blocks_z))
     (out_ref,) = take(1)
-    outs = take(len(out_planes(blocks_z)))
+    outs = take(len(OUT_PLANES))
     whole, ends = take(2)
     _, count_z, count_y, width = t_ref.shape
 
@@ -523,16 +510,17 @@
     dims = (count_z, count_y, width)
     mend_y(lambda z, ys, xs: t_ref[0, z, ys, xs], store_y, cy_ref, sy_ref, y_parts, blocks_y, ends, dims)
     mend_z(lambda z, xs: whole[z, :, xs], store_z, cz_ref, sz_ref, z_parts, blocks_z, count_z, width)
-    along_z(lz_ref[...], lambda zs, ys: whole[zs, ys], count_z, count_y, write, writers_of(outs, blocks_z))
-
-
-def filter_kernel(blocks_y, blocks_z, *refs):
+    along_z(lz_ref[...], lambda zs, ys: whole[zs, ys], count_z, count_y, write, writers_of(outs))
+
+
+def filter_kernel(blocks_y, blocks_z, aliased, *refs):
     refs = list(refs)
     take = lambda n: [refs.pop(0) for _ in range(n)]
     t_ref, ly_ref, cz_ref, sz_ref = take(4)
     z_parts = take(part_count(blocks_z))
+    take(aliased)
     (out_ref,) = take(1)
-    outs = take(len(out_planes(blocks_y)))
+    outs = take(len(OUT_PLANES))
     (whole,) = take(1)
     count_z, count_y, width = t_ref.shape
 
@@ -543,7 +531,7 @@
         out_ref[zs, ys] = value
 
     mend_z(lambda z, xs: t_ref[z, :, xs], store_z, cz_ref, sz_ref, z_parts, blocks_z, count_z, width)
-    along_y(ly_ref[...], lambda zs, ys: whole[zs, ys], count_z, count_y, write, writers_of(outs, blocks_y))
+    along_y(ly_ref[...], lambda zs, ys: whole[zs, ys], count_z, count_y, write, writers_of(outs))
 
 
 def split_once(matrix_ref, high_ref, low_ref, factor):
@@ -611,12 +599,21 @@
     rows_times(whole[...].reshape(-1, width), high_ref, low_ref, write)
 
 
-def merge_kernel(first_row, offset, chain_ref, own_ref, other_ref, out_ref):
-    for xs in spans(out_ref.shape[2]):
-        planes = [ref[offset + j, :, xs] for ref in (own_ref, other_ref) for j in range(2)]
-        for i in range(2):
-            row = first_row + 4 * i
-            out_ref[i, :, xs] = sum(chain_ref[row + j : row + j + 1, :] * plane for j, plane in enumerate(planes))
+def merge_kernel(first_row, chain_ref, own_ref, other_ref, *refs):
+    *extra, out_ref = refs
+    high = own_ref.shape[0] // max(1, out_ref.shape[0] // 4)
+    skip = 2 if extra else 0
+    for c in range(out_ref.shape[0] // (2 + skip)):
+        for ref in extra:
+            out_ref[4 * c : 4 * c + 2] = ref[2 * c : 2 * c + 2]
+        start = c * high + high - 2
+        for xs in spans(out_ref.shape[2]):
+            planes = [ref[start + j, :, xs] for ref in (own_ref, other_ref) for j in range(2)]
+            for i in range(2):
+                row = first_row + 4 * i
+                out_ref[(2 + skip) * c + skip + i, :, xs] = sum(
+                    chain_ref[row + j : row + j + 1, :] * plane for j, plane in enumerate(planes)
+                )
 
 
 def params(mib):
@@ -632,7 +629,41 @@
 
 
 def part_count(blocks):
-    return 3 if blocks == 4 else blocks.bit_length()
+    return 2 if blocks == 4 else blocks.bit_length()
+
+
+def hbm_of(*dims):
+    return pltpu.HBM(dims, jnp.float32)
+
+
+def vmem_of(*dims):
+    return pltpu.VMEM(dims, jnp.float32)
+
+
+class Order:
+    def __init__(self):
+        self.token = jnp.zeros((8, SPAN), jnp.float32)
+
+    def call(self, kernel, operands, in_specs, out_specs, out_shape, carry=(), aliases=None, **kwargs):
+        carry = [self.token, *carry]
+        n_in, n_out, k = len(operands), len(out_shape), len(carry)
+        aliases = dict(aliases or {})
+        aliases.update({n_in + i: n_out + i for i in range(k)})
+
+        def body(*refs):
+            kernel(*refs[:n_in], *refs[n_in + k : n_in + k + n_out], *refs[n_in + 2 * k + n_out :])
+
+        untouched = [pl.BlockSpec(memory_space=pl.ANY)] * k
+        out = pl.pallas_call(
+            body,
+            in_specs=list(in_specs) + untouched,
+            out_specs=list(out_specs) + untouched,
+            out_shape=list(out_shape) + [hbm_of(*a.shape) for a in carry],
+            input_output_aliases=aliases,
+            **kwargs,
+        )(*operands, *carry)
+        self.token = out[n_out]
+        return list(out[:n_out]), list(out[n_out + 1 :])
 
 
 def whole_spec(array):
@@ -644,139 +675,211 @@
 
 
 def cost(flops, size):
-    return pl.CostEstimate(flops=int(flops), bytes_accessed=int(size), transcendentals=0)
-
-
-def flux_call(velocity, ly, lz, blocks_y, blocks_z):
+    return pl.CostEstimate(flops=WEIGHT * int(flops), bytes_accessed=WEIGHT * int(size), transcendentals=0)
+
+
+def flux_call(order, pos, velocity, matrices, lines, blocks_y, blocks_z):
     nc, nz, ny, width = velocity.shape
     size = nc * nz * ny * width
-    planes = [(k, nz) for k in out_planes(blocks_y)] + [(k, ny) for k in out_planes(blocks_z)]
-    planes = planes * nc
-    out = pl.pallas_call(
-        functools.partial(flux_kernel, blocks_y, blocks_z),
+    constants, setup = derivative_constants(matrices, lines)
+    planes = [(4, nz)] * nc + [(2 * nc, nz), (4 * nc, ny), (2 * nc, ny)]
+    tables = [(6, n, SPAN) for n, _, _, _ in lines]
+    tables += [(merged + 2 * count, SPAN) for merged, count in map(table_counts, (blocks_y, blocks_z))]
+    constant = lambda dims: pl.BlockSpec(dims, lambda i: (0,) * len(dims))
+    out, _ = order.call(
+        functools.partial(flux_kernel, setup, blocks_y, blocks_z),
+        [pos, velocity, *matrices, constants],
+        [SMEM, lane_spec((nc, nz, ny))] + [whole_spec(a) for a in (*matrices, constants)],
+        [lane_spec((nc, nz, ny))] + [lane_spec(dims) for dims in planes] + [constant(dims) for dims in tables],
+        [hbm_of(nc, nz, ny, width)]
+        + [hbm_of(*dims, width) for dims in planes]
+        + [hbm_of(*dims) for dims in tables],
         grid=(width // LANES,),
-        in_specs=[lane_spec((nc, nz, ny)), whole_spec(ly), whole_spec(lz)],
-        out_specs=[lane_spec((nc, nz, ny))] + [lane_spec(dims) for dims in planes],
-        out_shape=[shape_of(nc, nz, ny, width)] + [shape_of(*dims, width) for dims in planes],
-        compiler_params=params(60),
+        scratch_shapes=[pltpu.VMEM(stack_shape(n, group).shape, jnp.bfloat16) for n, group, _, _ in lines],
+        compiler_params=params(64),
         cost_estimate=cost(size * 2 * 256 * 8, size * 9),
         name="flux_yz",
-    )(velocity, ly, lz)
-    each = len(planes) // nc
-    first = len(out_planes(blocks_y))
-    parts = [out[1 + c * each : 1 + (c + 1) * each] for c in range(nc)]
-    return out[0], [(p[:first], p[first:]) for p in parts]
-
-
-def flux_x_call(velocity, t, matrix, part, parts):
+    )
+    count = 1 + len(planes)
+    return out[0], out[1:count], out[count:]
+
+
+def flux_x_call(order, velocity, t, matrix, part, parts, carry):
     nc, nz, ny, width = velocity.shape
     group = max(1, min(nz // parts, ROWS // ny))
     steps = nz // parts // group
     block = pl.BlockSpec((nc, group, ny, width), lambda i: (0, part * steps + i, 0, 0))
     size = nc * nz * ny * width // parts
-    return pl.pallas_call(
+    (out,), carry = order.call(
         flux_x_kernel,
+        [velocity, t, matrix],
+        [block, block, whole_spec(matrix)],
+        [block],
+        [hbm_of(nc, nz, ny, width)],
+        carry,
+        {1: 0},
         grid=(steps,),
-        in_specs=[block, block, whole_spec(matrix)],
-        out_specs=block,
-        out_shape=shape_of(nc, nz, ny, width),
         scratch_shapes=[pltpu.VMEM(matrix.shape, jnp.bfloat16)] * 2,
-        input_output_aliases={1: 0},
-        compiler_params=params(60),
+        compiler_params=params(64),
         cost_estimate=cost(size * 4 * width, size * 13),
         name="flux_x",
-    )(velocity, t, matrix)
-
-
-def advance_call(t, c, lz, cy, cz, sy, sz, y_parts, z_parts, blocks_y, blocks_z):
+    )
+    return out, carry
+
+
+def advance_call(order, t, c, lz, cy, cz, sy, sz, y_parts, z_parts, blocks_y, blocks_z, carry):
     _, nz, ny, width = t.shape
     size = nz * ny * width
     planes = list(y_parts) + list(z_parts)
-    outs = [(k, ny) for k in out_planes(blocks_z)]
+    outs = [(k, ny) for k in OUT_PLANES]
     component = pl.BlockSpec((1, nz, ny, LANES), lambda i: (c, 0, 0, i))
-    return pl.pallas_call(
+    return order.call(
         functools.partial(advance_kernel, blocks_y, blocks_z),
+        [t, lz, cy, cz, sy, sz] + [p.array for p in planes],
+        [component] + [whole_spec(a) for a in (lz, cy, cz, sy, sz)] + [p.lane_spec() for p in planes],
+        [lane_spec((nz, ny))] + [lane_spec(dims) for dims in outs],
+        [vmem_of(nz, ny, width)] + [hbm_of(*dims, width) for dims in outs],
+        carry,
         grid=(width // LANES,),
-        in_specs=[component] + [whole_spec(a) for a in (lz, cy, cz, sy, sz)]
-        + [lane_spec(p.shape[:2]) for p in planes],
-        out_specs=[lane_spec((nz, ny))] + [lane_spec(dims) for dims in outs],
-        out_shape=[shape_of(nz, ny, width)] + [shape_of(*dims, width) for dims in outs],
         scratch_shapes=[pltpu.VMEM((nz, ny, LANES), jnp.float32), pltpu.VMEM((2, nz, SPAN), jnp.float32)],
-        compiler_params=params(60),
+        compiler_params=params(ADVANCE_MIB),
         cost_estimate=cost(size * 2 * 256 * 4, size * 9),
         name="advance_z",
-    )(t, lz, cy, cz, sy, sz, *planes)
-
-
-def filter_call(t, ly, cz, sz, z_parts, blocks_y, blocks_z):
+    )
+
+
+def filter_call(order, t, c, count_c, ly, cz, sz, z_parts, whole, blocks_y, blocks_z):
     nz, ny, width = t.shape
     size = nz * ny * width
-    outs = [(k, nz) for k in out_planes(blocks_y)]
-    return pl.pallas_call(
-        functools.partial(filter_kernel, blocks_y, blocks_z),
+    aliased = [] if whole is None else [whole]
+    operands = [t, ly, cz, sz] + [p.array for p in z_parts] + aliased
+    out, _ = order.call(
+        functools.partial(filter_kernel, blocks_y, blocks_z, len(aliased)),
+        operands,
+        [lane_spec((nz, ny))]
+        + [whole_spec(a) for a in (ly, cz, sz)]
+        + [p.lane_spec() for p in z_parts]
+        + [pl.BlockSpec(memory_space=pl.ANY)] * len(aliased),
+        [lane_spec((nz, ny)), lane_spec((4, nz)), pl.BlockSpec((2, nz, LANES), lambda i: (c, 0, i))],
+        [vmem_of(nz, ny, width), hbm_of(4, nz, width), hbm_of(2 * count_c, nz, width)],
+        (),
+        {len(operands) - 1: 2} if aliased else {},
         grid=(width // LANES,),
-        in_specs=[lane_spec((nz, ny))] + [whole_spec(a) for a in (ly, cz, sz)] + [lane_spec(p.shape[:2]) for p in z_parts],
-        out_specs=[lane_spec((nz, ny))] + [lane_spec(dims) for dims in outs],
-        out_shape=[shape_of(nz, ny, width)] + [shape_of(*dims, width) for dims in outs],
         scratch_shapes=[pltpu.VMEM((nz, ny, LANES), jnp.float32)],
-        compiler_params=params(60),
+        compiler_params=params(SMALL_MIB),
         cost_estimate=cost(size * 2 * 256 * 4, size * 9),
         name="filter_y",
-    )(t, ly, cz, sz, *z_parts)
-
-
-def last_call(whole, t, c, count_c, matrix, cy, sy, y_parts, blocks_y):
+    )
+    return out
+
+
+def last_call(order, whole, t, c, count_c, matrix, cy, sy, y_parts, blocks_y):
     nz, ny, width = t.shape
     group = max(8, min(nz, DEPTH // ny))
     block = pl.BlockSpec((group, ny, width), lambda i: (i, 0, 0))
-    plane = lambda k: pl.BlockSpec((k, group, width), lambda i: (0, i, 0))
     size = nz * ny * width
     aliased = [] if whole is None else [whole]
-    operands = [t, matrix, cy, sy, *y_parts, *aliased]
-    return pl.pallas_call(
+    operands = [t, matrix, cy, sy] + [p.array for p in y_parts] + aliased
+    (out,), _ = order.call(
         functools.partial(last_kernel, blocks_y, len(aliased)),
+        operands,
+        [block]
+        + [whole_spec(a) for a in (matrix, cy, sy)]
+        + [p.row_spec(group) for p in y_parts]
+        + [pl.BlockSpec(memory_space=pl.ANY)] * len(aliased),
+        [pl.BlockSpec((1, group, ny, width), lambda i: (c, i, 0, 0))],
+        [hbm_of(count_c, nz, ny, width)],
+        (),
+        {len(operands) - 1: 0} if aliased else {},
         grid=(nz // group,),
-        in_specs=[block] + [whole_spec(a) for a in (matrix, cy, sy)]
-        + [plane(p.shape[0]) for p in y_parts]
-        + [pl.BlockSpec(memory_space=pl.ANY)] * len(aliased),
-        out_specs=pl.BlockSpec((1, group, ny, width), lambda i: (c, i, 0, 0)),
-        out_shape=shape_of(count_c, nz, ny, width),
         scratch_shapes=[pltpu.VMEM((group, ny, width), jnp.float32), pltpu.VMEM((2, group, SPAN), jnp.float32)]
         + [pltpu.VMEM(matrix.shape, jnp.bfloat16)] * 2,
-        input_output_aliases={len(operands) - 1: 0} if aliased else {},
-        compiler_params=params(60),
+        compiler_params=params(SMALL_MIB),
         cost_estimate=cost(size * 6 * width, size * 13),
         name="filter_x",
-    )(*operands)
-
-
-def merge_call(chain, first_row, own, other):
-    offset = own.shape[0] - 2
-    dims = own.shape[1:]
-    size = 2 * dims[0] * dims[1]
-    return pl.pallas_call(
-        functools.partial(merge_kernel, first_row, offset),
-        in_specs=[VMEM] * 3,
-        out_shape=shape_of(2, *dims),
+    )
+    return out
+
+
+class Planes:
+    def __init__(self, array, count, index=0):
+        self.array, self.count, self.index = array, count, index
+
+    def lane_spec(self):
+        return pl.BlockSpec((self.count, self.array.shape[1], LANES), lambda i: (self.index, 0, i))
+
+    def row_spec(self, group):
+        return pl.BlockSpec((self.count, group, self.array.shape[2]), lambda i: (self.index, i, 0))
+
+
+def merge_call(order, chain, first_row, own, other, extra=(), carry=()):
+    planes, lines, width = own.shape
+    count = planes if extra else 2
+    size = count * lines * width
+    if extra:
+        ends = whole_spec
+    else:
+        ends = lambda a: pl.BlockSpec((2, lines, width), lambda i: (a.shape[0] // 2 - 1, 0, 0))
+    (out,), carry = order.call(
+        functools.partial(merge_kernel, first_row),
+        [chain, own, other, *extra],
+        [whole_spec(chain), ends(own), ends(other)] + [whole_spec(a) for a in extra],
+        [pl.BlockSpec((count, lines, width), lambda i: (0, 0, 0))],
+        [hbm_of(count, lines, width)],
+        carry,
+        grid=(1,),
+        compiler_params=params(SMALL_MIB),
         cost_estimate=cost(size * 8, size * 12),
         name="merge",
-    )(chain, own, other)
-
-
-def exchange(axis, outs, chain):
+    )
+    return out, carry
+
+
+def send(axis, array, target):
     blocks = lax.axis_size(axis)
-    near_pairs = [(i, i ^ 1) for i in range(blocks)]
-    away_pairs = [(i, (i - 1 if i % 2 == 0 else i + 1) % blocks) for i in range(blocks)]
-    near = lax.ppermute(outs[0], axis, near_pairs)
-    parts = [near, lax.ppermute(outs[1], axis, away_pairs)]
-    if blocks == 4:
-        return parts + [lax.ppermute(outs[2], axis, [(i, i ^ 2) for i in range(blocks)])]
-    own, other = outs[0], near
-    for level in range(1, blocks.bit_length() - 1):
-        own = merge_call(chain, 8 * (level - 1), own, other)
-        other = lax.ppermute(own, axis, [(i, i ^ (1 << level)) for i in range(blocks)])
-        parts.append(other)
-    return parts
+    return lax.ppermute(array, axis, [(i, target(i) % blocks) for i in range(blocks)])
+
+
+def partner(i):
+    return i ^ 1
+
+
+def other_neighbour(i):
+    return i - 1 if i % 2 == 0 else i + 1
+
+
+class Exchange:
+    def __init__(self, order, axis, near, chain, away=None):
+        self.order, self.axis, self.own, self.chain, self.away = order, axis, near, chain, away
+        self.blocks = lax.axis_size(axis)
+        self.steps = 1 if self.blocks == 4 else self.blocks.bit_length() - 2
+        self.far = []
+
+    def begin(self):
+        self.near = self.last = send(self.axis, self.own, partner)
+
+    def step(self, carry=()):
+        if len(self.far) == self.steps:
+            return carry
+        if self.blocks == 4:
+            both, carry = merge_call(self.order, self.chain, 0, self.own, self.last, [self.away], carry)
+            self.far = [send(self.axis, both, other_neighbour)]
+            return carry
+        level = len(self.far) + 1
+        self.own, carry = merge_call(self.order, self.chain, 8 * (level - 1), self.own, self.last, (), carry)
+        self.last = send(self.axis, self.own, lambda i: i ^ (1 << level))
+        self.far.append(self.last)
+        return carry
+
+    def finish(self):
+        while len(self.far) < self.steps:
+            self.step()
+
+    def parts(self, away, c, near_at=0):
+        self.finish()
+        if self.blocks == 4:
+            return [Planes(self.near, 4, near_at), Planes(self.far[0], 4, near_at)]
+        return [Planes(self.near, 4, near_at), Planes(away, 2, c)] + [Planes(array, 2) for array in self.far]
 
 
 def on_device(velocity, derivative_x, derivative_y, derivative_z, smoothing_x, smoothing_y, smoothing_z):
@@ -784,22 +887,87 @@
     pos = jnp.stack([lax.axis_index("row"), lax.axis_index("col")]).astype(jnp.int32)
     count_c, nz, ny, _ = velocity.shape
     lines = ((ny, min(nz, DEPTH // ny), False, num_row), (nz, min(ny, DEPTH // nz), True, num_col))
-
-    (ly, lz), (dy, dz), (cy, cz) = derivative_call(pos, (derivative_y, derivative_z), lines)
-    flux, parts = flux_call(velocity, ly, lz, num_row, num_col)
-    flux_parts = [
-        (exchange("row", y_outs, cy), exchange("col", z_outs, cz)) for y_outs, z_outs in parts
-    ]
-    (my, mz), (sy, sz), (fy, fz) = smoothing_call(pos, (smoothing_y, smoothing_z), lines)
-    for part in range(2):
-        flux = flux_x_call(velocity, flux, derivative_x, part, 2)
+    order = Order()
+
+    flux, outs, (dy, dz, cy, cz) = flux_call(
+        order, pos, velocity, (derivative_y, derivative_z), lines, num_row, num_col
+    )
+    *y_near, y_away, z_near, z_away = outs
+    four = num_col == 4
+    if four:
+        z_ex = [Exchange(order, "col", z_near, cz, z_away)]
+        z_ex[0].begin()
+    else:
+        cut_near = lambda c: lax.slice_in_dim(z_near, 4 * c, 4 * c + 4)
+        z_ex = [Exchange(order, "col", cut_near(c), cz) for c in range(count_c)]
+        for ex in z_ex:
+            ex.begin()
+    y_ex = [Exchange(order, "row", near, cy) for near in y_near]
+    y_ex[0].begin()
+    flux, (y_ex[1].own, y_ex[2].own, y_away) = flux_x_call(
+        order, velocity, flux, derivative_x, 0, 2, [y_ex[1].own, y_ex[2].own, y_away]
+    )
+    y_ex[0].step()
+    y_ex[1].begin()
+    for ex in z_ex:
+        (y_away,) = ex.step([y_away])
+        ex.finish()
+    y_came = send("row", y_away, other_neighbour)
+    flux, (y_ex[2].own,) = flux_x_call(order, velocity, flux, derivative_x, 1, 2, [y_ex[2].own])
+    y_ex[0].step()
+    y_ex[1].step()
+    y_ex[2].begin()
+    (my, mz), (sy, sz), (fy, fz) = smoothing_call(order, pos, (smoothing_y, smoothing_z), lines)
+    y_ex[1].step()
+    y_ex[2].step()
+    z_came = None if four else send("col", z_away, other_neighbour)
+
+    t_z, t_y = [None] * count_c, [None] * count_c
+    f_ex = [None] * count_c
+    g_ex = [None] * count_c
+    z_back = [None] * count_c
+
+    def advance(c):
+        y_parts = y_ex[c].parts(y_came, c)
+        z_parts = z_ex[0].parts(None, c, c) if four else z_ex[c].parts(z_came, c)
+        (t_z[c], near, away), _ = advance_call(
+            order, flux, c, mz, cy, cz, dy, dz, y_parts, z_parts, num_row, num_col, []
+        )
+        f_ex[c] = Exchange(order, "col", near, fz, away if four else None)
+        f_ex[c].begin()
+        z_back[c] = None if four else send("col", away, other_neighbour)
+
+    def filter_yz(c, whole):
+        z_parts = f_ex[c].parts(z_back[c], 0)
+        t_y[c], near, whole = filter_call(
+            order, t_z[c], c, count_c, my, fz, sz, z_parts, whole, num_row, num_col
+        )
+        g_ex[c] = Exchange(order, "row", near, fy)
+        g_ex[c].begin()
+        return whole
+
+    advance(0)
+    y_ex[2].step()
+    advance(1)
+    f_ex[0].step()
+    advance(2)
+    f_ex[1].step()
+    whole = filter_yz(0, None)
+    f_ex[2].step()
+    whole = filter_yz(1, whole)
+    g_ex[0].step()
+    whole = filter_yz(2, whole)
+    g_ex[1].step()
+    (whole,) = g_ex[0].step([whole])
+    came = send("row", whole, other_neighbour)
+    g_ex[2].step()
+    g_ex[1].step()
     out = None
-    for c, (y_parts, z_parts) in enumerate(flux_parts):
-        t, *z_outs = advance_call(flux, c, mz, cy, cz, dy, dz, y_parts, z_parts, num_row, num_col)
-        z_parts = exchange("col", z_outs, fz)
-        t, *y_outs = filter_call(t, my, fz, sz, z_parts, num_row, num_col)
-        y_parts = exchange("row", y_outs, fy)
-        out = last_call(out, t, c, count_c, smoothing_x, fy, sy, y_parts, num_row)
+    for c in range(count_c):
+        y_parts = g_ex[c].parts(came, c)
+        out = last_call(order, out, t_y[c], c, count_c, smoothing_x, fy, sy, y_parts, num_row)
+        if c == 0:
+            g_ex[2].step()
     return out
 
 

time: 298 us -> 248 us (0.83)
  waiting for transfers between devices: 84.2 us -> 66.3 us
  starting transfers between devices: 43.2 us -> 26.4 us
  Pallas kernels: 146 us -> 136 us
  local copies, waits for them, and re-layouts: 23.2 us -> 15.6 us
    ppermute x42 -> x28, waiting for transfers between devices: 84.2 us -> 66.3 us  [send(): lax.ppermute(array, axis, [(i, target(i) % blocks) for i in range(blocks)])]
    ppermute x42 -> x28, starting transfers between devices: 43.2 us -> 26.4 us  [send(): lax.ppermute(array, axis, [(i, target(i) % blocks) for i in range(blocks)])]
    pallas_call x26 -> x29, Pallas kernels: 146 us -> 136 us  [call(): pl.pallas_call(body, in_specs=list(in_specs) + untouched, out_specs=list(...]
    unnamed x128 -> x78, local copies, waits for them, and re-layouts: 23.2 us -> 15 us
  transfers between devices with their start and end apart: 42 -> 28, of which waited for: 11 -> 10; matrix products, arithmetic and copies ran while one was open for 0% -> 0% of each run, Pallas kernels for 40% -> 44%
where the time goes in v2:
time: 248 us; the launch traced here: 245 us
  Pallas kernels  136 us (55%)
  waiting for transfers between devices  66.3 us (27%)
  starting transfers between devices  26.4 us (11%)
  local copies, waits for them, and re-layouts  15.6 us (6%)
    pallas_call x29, Pallas kernels, call(): pl.pallas_call(body, in_specs=list(in_specs) + untouched, out_specs=list(...  136 us
    ppermute x28, waiting for transfers between devices, send(): lax.ppermute(array, axis, [(i, target(i) % blocks) for i in range(blocks)])  66.3 us
    ppermute x28, starting transfers between devices, send(): lax.ppermute(array, axis, [(i, target(i) % blocks) for i in range(blocks)])  26.4 us
    unnamed x78, local copies, waits for them, and re-layouts  15 us
  transfers between devices with their start and end apart: 28, of which 10 were waited for; matrix products, arithmetic and copies ran while one was open for 0% of the time, Pallas kernels for 44%

profile of v2, /device:TPU:4, one launch (start us, length us, event | category | flops | bytes accessed | tf_op | source)
XLA Modules:
  0.0 245.0 jit_solution(11909921133403959085)
XLA Ops:
  1.2 17.4 %flux_yz.1 = (f32[3,32,32,1024]{3,2,1,0:T(8,128)}, f32[4,32,1024]{2,1,0:T(8,128)}, f32[4,32,1024]{2,1,0:T(8,128)}, f32[4,32,1024]{2,1,0:T(8,128)}, f32[6,32,1024...) custom-call(s32[2]{0:T(128)} %pad_add_fusion.refs_0_, ...), custom_call_target="tpu_custom_call", output_to_operand_aliasing={{11}: (5, {})} | custom-call | flops 12884901888000 | bytes 28311552000 | tf_op jit(solution)/shard_map/flux_yz/pallas_call | solution.py:657
  18.8 13.3 %flux_x.2 = (f32[3,32,32,1024]{3,2,1,0:T(8,128)}, f32[8,128]{1,0:T(8,128)}, f32[4,32,1024]{2,1,0:T(8,128)}, f32[4,32,1024]{2,1,0:T(8,128)}, f32[6,32,1024]{2,1,0:T(8,128)}) custom-call(f32[3,32,32,1024]{3,2,1,0:T(8,128)} %refs_0_.3, ...), custom_call_target="tpu_custom_call", output_to_operand_aliasing={{0}: (1, {}), {1}: (3, {}), {2}: (4, {}), {3}: (5, {}), {4}... | custom-call | flops 6442450944000 | bytes 20447232000 | tf_op jit(solution)/shard_map/flux_x/pallas_call | solution.py:657
  32.1 2.0 collective-permute-start.2
  35.8 1.7 merge.16
  42.4 2.8 %merge.17 = (f32[12,32,1024]{2,1,0:T(8,128)}, f32[8,128]{1,0:T(8,128)}, f32[6,32,1024]{2,1,0:T(8,128)}) custom-call(f32[16,128]{1,0:T(8,128)S(1)} %copy-done.36, f32[12,32,1024]{2,1,0:T(8,128)S(1)} %copy-done.1, f32[12,32,1024]{2,1,0:T(8,128)} %collective-permute-done.refs_2_.refs_10_, ...), custom_call_target="tpu_custom_call", output_to_operand_aliasing={{1}: (4, {}), {2}: (5, {})} | custom-call | flops 3145728000 | bytes 4718592000 | tf_op jit(solution)/shard_map/merge/pallas_call | solution.py:657
  45.9 13.3 %flux_x.3 = (f32[3,32,32,1024]{3,2,1,0:T(8,128)}, f32[8,128]{1,0:T(8,128)}, f32[4,32,1024]{2,1,0:T(8,128)}) custom-call(f32[3,32,32,1024]{3,2,1,0:T(8,128)} %refs_0_.3, f32[3,32,32,1024]{3,2,1,0:T(8,128)} %get-tuple-element.100.refs_1_, f32[1024,1024]{1,0:T(8,128)} %refs_2_.6, ...), custom_call_target="tpu_custom_call", output_to_operand_aliasing={{0}: (1, {}), {1}: (3, {}), {2}: (4, {})} | custom-call | flops 6442450944000 | bytes 20447232000 | tf_op jit(solution)/shard_map/flux_x/pallas_call | solution.py:657
  68.0 2.7 %collective-permute-start.6 = (f32[2,32,1024]{2,1,0:T(8,128)}, f32[2,32,1024]{2,1,0:T(8,128)S(1)}, u32[]{:S(2)}, u32[]{:S(2)}) collective-permute-start(f32[2,32,1024]{2,1,0:T(8,128)} %get-tuple-element.122.refs_1_), channel_id=1, source_target_pairs={{0,8},{4,12},{8,0},{12,4},{16,24},{20,28},{24,16},{28,20},{1,9},{5... | collective-permute-start | bytes 786440 | tf_op jit(solution)/shard_map/ppermute | solution.py:840
  74.4 1.9 smoothing_lines.1
  76.3 17.7 %collective-permute-done.6.refs_2_.refs_8_ = f32[2,32,1024]{2,1,0:T(8,128)S(1)} collective-permute-done((f32[2,32,1024]{2,1,0:T(8,128)}, f32[2,32,1024]{2,1,0:T(8,128)S(1)}, u32[]{:S(2)}, u32[]{:S(2)}) %collective-permute-start.6) | collective-permute-done | bytes 262176 | tf_op jit(solution)/shard_map/ppermute | solution.py:840
  97.5 7.6 %advance_z.3 = (f32[32,32,1024]{2,1,0:T(8,128)S(1)}, f32[4,32,1024]{2,1,0:T(8,128)}, f32[2,32,1024]{2,1,0:T(8,128)}, f32[8,128]{1,0:T(8,128)}) custom-call(f32[3,32,32,1024]{3,2,1,0:T(8,128)} %get-tuple-element.111.refs_0_, bf16[608,256]{1,0:T(8,128)(2,1)} %copy-done.35, ...), custom_call_target="tpu_custom_call", output_to_operand_aliasing={{3}: (12, {})} | custom-call | flops 2147483648000 | bytes 9437184000 | tf_op jit(solution)/shard_map/advance_z/pallas_call | solution.py:657
  105.1 5.5 %collective-permute-done.7.refs_2_.refs_8_ = f32[2,32,1024]{2,1,0:T(8,128)} collective-permute-done((f32[2,32,1024]{2,1,0:T(8,128)}, f32[2,32,1024]{2,1,0:T(8,128)}, u32[]{:S(2)}, u32[]{:S(2)}) %collective-permute-start.7) | collective-permute-done | bytes 262176 | tf_op jit(solution)/shard_map/ppermute | solution.py:840
  112.4 7.4 %advance_z.4 = (f32[32,32,1024]{2,1,0:T(8,128)S(1)}, f32[4,32,1024]{2,1,0:T(8,128)}, f32[2,32,1024]{2,1,0:T(8,128)}, f32[8,128]{1,0:T(8,128)}) custom-call(f32[3,32,32,1024]{3,2,1,0:T(8,128)} %get-tuple-element.111.refs_0_, bf16[608,256]{1,0:T(8,128)(2,1)} %copy-done.35, ...), custom_call_target="tpu_custom_call", output_to_operand_aliasing={{3}: (12, {})} | custom-call | flops 2147483648000 | bytes 9437184000 | tf_op jit(solution)/shard_map/advance_z/pallas_call | solution.py:657
  120.3 2.0 merge.23
  122.4 3.1 %collective-permute-done.10.refs_9_ = f32[2,32,1024]{2,1,0:T(8,128)} collective-permute-done((f32[2,32,1024]{2,1,0:T(8,128)}, f32[2,32,1024]{2,1,0:T(8,128)}, u32[]{:S(2)}, u32[]{:S(2)}) %collective-permute-start.10) | collective-permute-done | bytes 262176 | tf_op jit(solution)/shard_map/ppermute | solution.py:840
  125.5 7.4 %advance_z.5 = (f32[32,32,1024]{2,1,0:T(8,128)S(1)}, f32[4,32,1024]{2,1,0:T(8,128)}, f32[2,32,1024]{2,1,0:T(8,128)}, f32[8,128]{1,0:T(8,128)}) custom-call(f32[3,32,32,1024]{3,2,1,0:T(8,128)} %get-tuple-element.111.refs_0_, bf16[608,256]{1,0:T(8,128)(2,1)} %copy-done.35, ...), custom_call_target="tpu_custom_call", output_to_operand_aliasing={{3}: (12, {})} | custom-call | flops 2147483648000 | bytes 9437184000 | tf_op jit(solution)/shard_map/advance_z/pallas_call | solution.py:657
  133.0 2.0 merge.24
  136.6 5.5 %filter_y.3 = (f32[32,32,1024]{2,1,0:T(8,128)S(1)}, f32[4,32,1024]{2,1,0:T(8,128)}, f32[6,32,1024]{2,1,0:T(8,128)}, f32[8,128]{1,0:T(8,128)}) custom-call(f32[32,32,1024]{2,1,0:T(8,128)S(1)} %get-tuple-element.143.refs_0_, bf16[608,256]{1,0:T(8,128)(2,1)S(1)} %get-tuple-element.139.refs_1_, ...), custom_call_target="tpu_custom_call", output_to_operand_aliasing={{3}: (6, {})} | custom-call | flops 2147483648000 | bytes 9437184000 | tf_op jit(solution)/shard_map/filter_y/pallas_call | solution.py:657
  142.2 1.9 merge.25
  145.3 3.6 %collective-permute-done.17.refs_5_ = f32[4,32,1024]{2,1,0:T(8,128)} collective-permute-done((f32[4,32,1024]{2,1,0:T(8,128)}, f32[4,32,1024]{2,1,0:T(8,128)}, u32[]{:S(2)}, u32[]{:S(2)}) %collective-permute-start.17) | collective-permute-done | bytes 524320 | tf_op jit(solution)/shard_map/ppermute | solution.py:840
  148.9 5.5 %filter_y.4 = (f32[32,32,1024]{2,1,0:T(8,128)S(1)}, f32[4,32,1024]{2,1,0:T(8,128)}, f32[6,32,1024]{2,1,0:T(8,128)}, f32[8,128]{1,0:T(8,128)}) custom-call(f32[32,32,1024]{2,1,0:T(8,128)S(1)} %get-tuple-element.151.refs_0_, bf16[608,256]{1,0:T(8,128)(2,1)S(1)} %get-tuple-element.139.refs_1_, ...), custom_call_target="tpu_custom_call", output_to_operand_aliasing={{2}: (6, {}), {3}: (7, {})} | custom-call | flops 2147483648000 | bytes 9437184000 | tf_op jit(solution)/shard_map/filter_y/pallas_call | solution.py:657
  155.2 3.8 %collective-permute-done.18.refs_2_.refs_4_ = f32[4,32,1024]{2,1,0:T(8,128)} collective-permute-done((f32[4,32,1024]{2,1,0:T(8,128)}, f32[4,32,1024]{2,1,0:T(8,128)}, u32[]{:S(2)}, u32[]{:S(2)}) %collective-permute-start.18) | collective-permute-done | bytes 524320 | tf_op jit(solution)/shard_map/ppermute | solution.py:840
  159.0 1.7 merge.26
  160.8 2.1 collective-permute-start.20
  162.9 5.5 %filter_y.5 = (f32[32,32,1024]{2,1,0:T(8,128)S(1)}, f32[4,32,1024]{2,1,0:T(8,128)}, f32[6,32,1024]{2,1,0:T(8,128)}, f32[8,128]{1,0:T(8,128)}) custom-call(f32[32,32,1024]{2,1,0:T(8,128)S(1)} %get-tuple-element.138.refs_0_, bf16[608,256]{1,0:T(8,128)(2,1)S(1)} %get-tuple-element.139.refs_1_, ...), custom_call_target="tpu_custom_call", output_to_operand_aliasing={{2}: (6, {}), {3}: (7, {})} | custom-call | flops 2147483648000 | bytes 9437184000 | tf_op jit(solution)/shard_map/filter_y/pallas_call | solution.py:657
  173.5 3.0 %collective-permute-start.22 = (f32[6,32,1024]{2,1,0:T(8,128)}, f32[6,32,1024]{2,1,0:T(8,128)S(1)}, u32[]{:S(2)}, u32[]{:S(2)}) collective-permute-start(f32[6,32,1024]{2,1,0:T(8,128)} %get-tuple-element.168), channel_id=1, source_target_pairs={{0,28},{4,8},{8,4},{12,16},{16,12},{20,24},{24,20},{28,0},{1,29},{... | collective-permute-start | bytes 2359304 | tf_op jit(solution)/shard_map/ppermute | solution.py:840
  177.2 2.7 %collective-permute-start.24 = (f32[2,32,1024]{2,1,0:T(8,128)}, f32[2,32,1024]{2,1,0:T(8,128)S(1)}, u32[]{:S(2)}, u32[]{:S(2)}) collective-permute-start(f32[2,32,1024]{2,1,0:T(8,128)} %get-tuple-element.172), channel_id=1, source_target_pairs={{0,16},{4,20},{8,24},{12,28},{16,0},{20,4},{24,8},{28,12},{1,17},{... | collective-permute-start | bytes 786440 | tf_op jit(solution)/shard_map/ppermute | solution.py:840
  179.9 25.4 %collective-permute-done.19.refs_2_.refs_4_ = f32[4,32,1024]{2,1,0:T(8,128)S(1)} collective-permute-done((f32[4,32,1024]{2,1,0:T(8,128)}, f32[4,32,1024]{2,1,0:T(8,128)S(1)}, u32[]{:S(2)}, u32[]{:S(2)}) %collective-permute-start.19) | collective-permute-done | bytes 524320 | tf_op jit(solution)/shard_map/ppermute | solution.py:840
  210.5 1.9 collective-permute-start.27
  212.5 8.5 %filter_x.3 = (f32[3,32,32,1024]{3,2,1,0:T(8,128)}, f32[8,128]{1,0:T(8,128)}) custom-call(f32[32,32,1024]{2,1,0:T(8,128)S(1)} %get-tuple-element.171.refs_0_, f32[1024,1024]{1,0:T(8,128)S(1)} %copy-done, f32[28,128]{1,0:T(8,128)S(1)} %get-tuple-element.156.refs_0_.refs_2_, ...), custom_call_target="tpu_custom_call", output_to_operand_aliasing={{1}: (8, {})} | custom-call | flops 6442450944000 | bytes 13631488000 | tf_op jit(solution)/shard_map/filter_x/pallas_call | solution.py:657
  225.4 8.5 %filter_x.4 = (f32[3,32,32,1024]{3,2,1,0:T(8,128)}, f32[8,128]{1,0:T(8,128)}) custom-call(f32[32,32,1024]{2,1,0:T(8,128)S(1)} %get-tuple-element.178.refs_0_, f32[1024,1024]{1,0:T(8,128)S(1)} %copy-done, f32[28,128]{1,0:T(8,128)S(1)} %get-tuple-element.156.refs_0_.refs_2_, ...), custom_call_target="tpu_custom_call", output_to_operand_aliasing={{0}: (8, {}), {1}: (9, {})} | custom-call | flops 6442450944000 | bytes 13631488000 | tf_op jit(solution)/shard_map/filter_x/pallas_call | solution.py:657
  233.9 2.7 %collective-permute-done.26.refs_7_ = f32[2,32,1024]{2,1,0:T(8,128)} collective-permute-done((f32[2,32,1024]{2,1,0:T(8,128)}, f32[2,32,1024]{2,1,0:T(8,128)}, u32[]{:S(2)}, u32[]{:S(2)}) %collective-permute-start.26) | collective-permute-done | bytes 262176 | tf_op jit(solution)/shard_map/ppermute | solution.py:840
  236.6 8.4 %filter_x.5 = (f32[3,32,32,1024]{3,2,1,0:T(8,128)}, f32[8,128]{1,0:T(8,128)}) custom-call(f32[32,32,1024]{2,1,0:T(8,128)S(1)} %get-tuple-element.160.refs_0_, f32[1024,1024]{1,0:T(8,128)S(1)} %copy-done, f32[28,128]{1,0:T(8,128)S(1)} %get-tuple-element.156.refs_0_.refs_2_, ...), custom_call_target="tpu_custom_call", output_to_operand_aliasing={{0}: (8, {}), {1}: (9, {})} | custom-call | flops 6442450944000 | bytes 13631488000 | tf_op jit(solution)/shard_map/filter_x/pallas_call | solution.py:657
  (133 shorter events, 46.2 us)
Async XLA Ops:
  18.6 20.5 %collective-permute-start = (f32[12,32,1024]{2,1,0:T(8,128)}, f32[12,32,1024]{2,1,0:T(8,128)}, u32[]{:S(2)}, u32[]{:S(2)}) collective-permute-start(f32[12,32,1024]{2,1,0:T(8,128)} %get-tuple-element.102.refs_1_), channel_id=1, source_target_pairs={{0,1},{1,0},{2,3},{3,2},{4,5},{5,4},{6,7},{7,6},{8,9},{9,8},{10,11... | collective-permute-start | bytes 4718600 | tf_op jit(solution)/shard_map/ppermute | solution.py:840
  18.7 15.4 %collective-permute-start.1 = (f32[4,32,1024]{2,1,0:T(8,128)}, f32[4,32,1024]{2,1,0:T(8,128)}, u32[]{:S(2)}, u32[]{:S(2)}) collective-permute-start(f32[4,32,1024]{2,1,0:T(8,128)} %get-tuple-element.105.refs_1_), channel_id=1, source_target_pairs={{0,4},{4,0},{8,12},{12,8},{16,20},{20,16},{24,28},{28,24},{1,5},{5... | collective-permute-start | bytes 1572872 | tf_op jit(solution)/shard_map/ppermute | solution.py:840
  32.1 32.4 %collective-permute-start.2 = (f32[4,32,1024]{2,1,0:T(8,128)}, f32[4,32,1024]{2,1,0:T(8,128)}, u32[]{:S(2)}, u32[]{:S(2)}) collective-permute-start(f32[4,32,1024]{2,1,0:T(8,128)} %get-tuple-element.112.refs_1_), channel_id=1, source_target_pairs={{0,4},{4,0},{8,12},{12,8},{16,20},{20,16},{24,28},{28,24},{1,5},{5... | collective-permute-start | bytes 1572872 | tf_op jit(solution)/shard_map/ppermute | solution.py:840
  37.6 23.5 %collective-permute-start.3 = (f32[2,32,1024]{2,1,0:T(8,128)}, f32[2,32,1024]{2,1,0:T(8,128)}, u32[]{:S(2)}, u32[]{:S(2)}) collective-permute-start(f32[2,32,1024]{2,1,0:T(8,128)} %get-tuple-element.113.refs_1_), channel_id=1, source_target_pairs={{0,8},{4,12},{8,0},{12,4},{16,24},{20,28},{24,16},{28,20},{1,9},{5... | collective-permute-start | bytes 786440 | tf_op jit(solution)/shard_map/ppermute | solution.py:840
  45.2 51.4 %collective-permute-start.9 = (f32[12,32,1024]{2,1,0:T(8,128)}, f32[12,32,1024]{2,1,0:T(8,128)}, u32[]{:S(2)}, u32[]{:S(2)}) collective-permute-start(f32[12,32,1024]{2,1,0:T(8,128)} %get-tuple-element.127), channel_id=1, source_target_pairs={{0,3},{1,2},{2,1},{3,0},{4,7},{5,6},{6,5},{7,4},{8,11},{9,10},{10,... | collective-permute-start | bytes 4718600 | tf_op jit(solution)/shard_map/ppermute | solution.py:840
  59.2 35.7 %collective-permute-start.4 = (f32[4,32,1024]{2,1,0:T(8,128)}, f32[4,32,1024]{2,1,0:T(8,128)S(1)}, u32[]{:S(2)}, u32[]{:S(2)}) collective-permute-start(f32[4,32,1024]{2,1,0:T(8,128)} %get-tuple-element.120.refs_1_), channel_id=1, source_target_pairs={{0,4},{4,0},{8,12},{12,8},{16,20},{20,16},{24,28},{28,24},{1,5},{5... | collective-permute-start | bytes 1572872 | tf_op jit(solution)/shard_map/ppermute | solution.py:840
  59.7 36.9 %collective-permute-start.5 = (f32[6,32,1024]{2,1,0:T(8,128)}, f32[6,32,1024]{2,1,0:T(8,128)S(1)}, u32[]{:S(2)}, u32[]{:S(2)}) collective-permute-start(f32[6,32,1024]{2,1,0:T(8,128)} %get-tuple-element.121), channel_id=1, source_target_pairs={{0,28},{4,8},{8,4},{12,16},{16,12},{20,24},{24,20},{28,0},{1,29},{... | collective-permute-start | bytes 2359304 | tf_op jit(solution)/shard_map/ppermute | solution.py:840
  66.3 27.8 %copy-start.32 = (f32[28,128]{1,0:T(8,128)S(1)}, f32[28,128]{1,0:T(8,128)}, u32[]{:S(2)}) copy-start(f32[28,128]{1,0:T(8,128)} %get-tuple-element.104.refs_0_.refs_2_) | copy-start | bytes 43012
  68.0 26.9 %copy-start.13 = (f32[4,32,1024]{2,1,0:T(8,128)S(1)}, f32[4,32,1024]{2,1,0:T(8,128)}, u32[]{:S(2)}) copy-start(f32[4,32,1024]{2,1,0:T(8,128)} %get-tuple-element.120.refs_1_) | copy-start | bytes 1572868
  68.0 26.0 %collective-permute-start.6 = (f32[2,32,1024]{2,1,0:T(8,128)}, f32[2,32,1024]{2,1,0:T(8,128)S(1)}, u32[]{:S(2)}, u32[]{:S(2)}) collective-permute-start(f32[2,32,1024]{2,1,0:T(8,128)} %get-tuple-element.122.refs_1_), channel_id=1, source_target_pairs={{0,8},{4,12},{8,0},{12,4},{16,24},{20,28},{24,16},{28,20},{1,9},{5... | collective-permute-start | bytes 786440 | tf_op jit(solution)/shard_map/ppermute | solution.py:840
  70.7 25.8 %collective-permute-start.8 = (f32[2,32,1024]{2,1,0:T(8,128)}, f32[2,32,1024]{2,1,0:T(8,128)S(1)}, u32[]{:S(2)}, u32[]{:S(2)}) collective-permute-start(f32[2,32,1024]{2,1,0:T(8,128)} %get-tuple-element.126), channel_id=1, source_target_pairs={{0,16},{4,20},{8,24},{12,28},{16,0},{20,4},{24,8},{28,12},{1,17},{... | collective-permute-start | bytes 786440 | tf_op jit(solution)/shard_map/ppermute | solution.py:840
  76.3 20.3 %copy-start.35 = (bf16[608,256]{1,0:T(8,128)(2,1)}, bf16[608,256]{1,0:T(8,128)(2,1)S(1)}, u32[]{:S(2)}) copy-start(bf16[608,256]{1,0:T(8,128)(2,1)S(1)} %get-tuple-element.117.refs_1_) | copy-start | bytes 933892
  94.8 17.5 %collective-permute-start.12 = (f32[2,32,1024]{2,1,0:T(8,128)}, f32[2,32,1024]{2,1,0:T(8,128)}, u32[]{:S(2)}, u32[]{:S(2)}) collective-permute-start(f32[2,32,1024]{2,1,0:T(8,128)} %get-tuple-element.134), channel_id=1, source_target_pairs={{0,16},{4,20},{8,24},{12,28},{16,0},{20,4},{24,8},{28,12},{1,17},{... | collective-permute-start | bytes 786440 | tf_op jit(solution)/shard_map/ppermute | solution.py:840
  96.5 14.2 %collective-permute-start.7 = (f32[2,32,1024]{2,1,0:T(8,128)}, f32[2,32,1024]{2,1,0:T(8,128)}, u32[]{:S(2)}, u32[]{:S(2)}) collective-permute-start(f32[2,32,1024]{2,1,0:T(8,128)} %get-tuple-element.125.refs_1_), channel_id=1, source_target_pairs={{0,8},{4,12},{8,0},{12,4},{16,24},{20,28},{24,16},{28,20},{1,9},{5... | collective-permute-start | bytes 786440 | tf_op jit(solution)/shard_map/ppermute | solution.py:840
  112.4 13.2 %collective-permute-start.10 = (f32[2,32,1024]{2,1,0:T(8,128)}, f32[2,32,1024]{2,1,0:T(8,128)}, u32[]{:S(2)}, u32[]{:S(2)}) collective-permute-start(f32[2,32,1024]{2,1,0:T(8,128)} %get-tuple-element.130), channel_id=1, source_target_pairs={{0,16},{4,20},{8,24},{12,28},{16,0},{20,4},{24,8},{28,12},{1,17},{... | collective-permute-start | bytes 786440 | tf_op jit(solution)/shard_map/ppermute | solution.py:840
  112.4 8.0 %collective-permute-start.11 = (f32[4,32,1024]{2,1,0:T(8,128)}, f32[4,32,1024]{2,1,0:T(8,128)}, u32[]{:S(2)}, u32[]{:S(2)}) collective-permute-start(f32[4,32,1024]{2,1,0:T(8,128)} %get-tuple-element.132.refs_1_), channel_id=1, source_target_pairs={{0,1},{1,0},{2,3},{3,2},{4,5},{5,4},{6,7},{7,6},{8,9},{9,8},{10,11... | collective-permute-start | bytes 1572872 | tf_op jit(solution)/shard_map/ppermute | solution.py:840
  119.8 13.2 %collective-permute-start.15 = (f32[4,32,1024]{2,1,0:T(8,128)}, f32[4,32,1024]{2,1,0:T(8,128)}, u32[]{:S(2)}, u32[]{:S(2)}) collective-permute-start(f32[4,32,1024]{2,1,0:T(8,128)} %get-tuple-element.145.refs_1_), channel_id=1, source_target_pairs={{0,1},{1,0},{2,3},{3,2},{4,5},{5,4},{6,7},{7,6},{8,9},{9,8},{10,11... | collective-permute-start | bytes 1572872 | tf_op jit(solution)/shard_map/ppermute | solution.py:840
  122.3 14.3 %collective-permute-start.14 = (f32[4,32,1024]{2,1,0:T(8,128)}, f32[4,32,1024]{2,1,0:T(8,128)}, u32[]{:S(2)}, u32[]{:S(2)}) collective-permute-start(f32[4,32,1024]{2,1,0:T(8,128)} %get-tuple-element.144), channel_id=1, source_target_pairs={{0,3},{1,2},{2,1},{3,0},{4,7},{5,6},{6,5},{7,4},{8,11},{9,10},{10,... | collective-permute-start | bytes 1572872 | tf_op jit(solution)/shard_map/ppermute | solution.py:840
  132.9 9.2 %collective-permute-start.13 = (f32[4,32,1024]{2,1,0:T(8,128)}, f32[4,32,1024]{2,1,0:T(8,128)}, u32[]{:S(2)}, u32[]{:S(2)}) collective-permute-start(f32[4,32,1024]{2,1,0:T(8,128)} %get-tuple-element.141.refs_1_), channel_id=1, source_target_pairs={{0,1},{1,0},{2,3},{3,2},{4,5},{5,4},{6,7},{7,6},{8,9},{9,8},{10,11... | collective-permute-start | bytes 1572872 | tf_op jit(solution)/shard_map/ppermute | solution.py:840
  135.0 13.9 %collective-permute-start.17 = (f32[4,32,1024]{2,1,0:T(8,128)}, f32[4,32,1024]{2,1,0:T(8,128)}, u32[]{:S(2)}, u32[]{:S(2)}) collective-permute-start(f32[4,32,1024]{2,1,0:T(8,128)} %get-tuple-element.152), channel_id=1, source_target_pairs={{0,3},{1,2},{2,1},{3,0},{4,7},{5,6},{6,5},{7,4},{8,11},{9,10},{10,... | collective-permute-start | bytes 1572872 | tf_op jit(solution)/shard_map/ppermute | solution.py:840
  144.1 18.8 %collective-permute-start.16 = (f32[4,32,1024]{2,1,0:T(8,128)}, f32[4,32,1024]{2,1,0:T(8,128)}, u32[]{:S(2)}, u32[]{:S(2)}) collective-permute-start(f32[4,32,1024]{2,1,0:T(8,128)} %get-tuple-element.150), channel_id=1, source_target_pairs={{0,3},{1,2},{2,1},{3,0},{4,7},{5,6},{6,5},{7,4},{8,11},{9,10},{10,... | collective-permute-start | bytes 1572872 | tf_op jit(solution)/shard_map/ppermute | solution.py:840
  144.3 14.7 %collective-permute-start.18 = (f32[4,32,1024]{2,1,0:T(8,128)}, f32[4,32,1024]{2,1,0:T(8,128)}, u32[]{:S(2)}, u32[]{:S(2)}) collective-permute-start(f32[4,32,1024]{2,1,0:T(8,128)} %get-tuple-element.157.refs_1_), channel_id=1, source_target_pairs={{0,4},{4,0},{8,12},{12,8},{16,20},{20,16},{24,28},{28,24},{1,5},{5... | collective-permute-start | bytes 1572872 | tf_op jit(solution)/shard_map/ppermute | solution.py:840
  154.4 15.7 %collective-permute-start.21 = (f32[4,32,1024]{2,1,0:T(8,128)}, f32[4,32,1024]{2,1,0:T(8,128)}, u32[]{:S(2)}, u32[]{:S(2)}) collective-permute-start(f32[4,32,1024]{2,1,0:T(8,128)} %get-tuple-element.164.refs_1_), channel_id=1, source_target_pairs={{0,4},{4,0},{8,12},{12,8},{16,20},{20,16},{24,28},{28,24},{1,5},{5... | collective-permute-start | bytes 1572872 | tf_op jit(solution)/shard_map/ppermute | solution.py:840
  160.8 11.1 %collective-permute-start.20 = (f32[2,32,1024]{2,1,0:T(8,128)}, f32[2,32,1024]{2,1,0:T(8,128)}, u32[]{:S(2)}, u32[]{:S(2)}) collective-permute-start(f32[2,32,1024]{2,1,0:T(8,128)} %get-tuple-element.163.refs_1_), channel_id=1, source_target_pairs={{0,8},{4,12},{8,0},{12,4},{16,24},{20,28},{24,16},{28,20},{1,9},{5... | collective-permute-start | bytes 786440 | tf_op jit(solution)/shard_map/ppermute | solution.py:840
  168.4 44.1 %copy-start = (f32[1024,1024]{1,0:T(8,128)S(1)}, f32[1024,1024]{1,0:T(8,128)}, u32[]{:S(2)}) copy-start(f32[1024,1024]{1,0:T(8,128)} %refs_1_.9) | copy-start | bytes 12582916
  173.5 38.9 %collective-permute-start.22 = (f32[6,32,1024]{2,1,0:T(8,128)}, f32[6,32,1024]{2,1,0:T(8,128)S(1)}, u32[]{:S(2)}, u32[]{:S(2)}) collective-permute-start(f32[6,32,1024]{2,1,0:T(8,128)} %get-tuple-element.168), channel_id=1, source_target_pairs={{0,28},{4,8},{8,4},{12,16},{16,12},{20,24},{24,20},{28,0},{1,29},{... | collective-permute-start | bytes 2359304 | tf_op jit(solution)/shard_map/ppermute | solution.py:840
  176.5 28.8 %collective-permute-start.19 = (f32[4,32,1024]{2,1,0:T(8,128)}, f32[4,32,1024]{2,1,0:T(8,128)S(1)}, u32[]{:S(2)}, u32[]{:S(2)}) collective-permute-start(f32[4,32,1024]{2,1,0:T(8,128)} %get-tuple-element.162.refs_1_), channel_id=1, source_target_pairs={{0,4},{4,0},{8,12},{12,8},{16,20},{20,16},{24,28},{28,24},{1,5},{5... | collective-permute-start | bytes 1572872 | tf_op jit(solution)/shard_map/ppermute | solution.py:840
  177.2 31.5 %collective-permute-start.25 = (f32[2,32,1024]{2,1,0:T(8,128)}, f32[2,32,1024]{2,1,0:T(8,128)S(1)}, u32[]{:S(2)}, u32[]{:S(2)}) collective-permute-start(f32[2,32,1024]{2,1,0:T(8,128)} %get-tuple-element.173.refs_1_), channel_id=1, source_target_pairs={{0,8},{4,12},{8,0},{12,4},{16,24},{20,28},{24,16},{28,20},{1,9},{5... | collective-permute-start | bytes 786440 | tf_op jit(solution)/shard_map/ppermute | solution.py:840
  177.2 35.2 %collective-permute-start.24 = (f32[2,32,1024]{2,1,0:T(8,128)}, f32[2,32,1024]{2,1,0:T(8,128)S(1)}, u32[]{:S(2)}, u32[]{:S(2)}) collective-permute-start(f32[2,32,1024]{2,1,0:T(8,128)} %get-tuple-element.172), channel_id=1, source_target_pairs={{0,16},{4,20},{8,24},{12,28},{16,0},{20,4},{24,8},{28,12},{1,17},{... | collective-permute-start | bytes 786440 | tf_op jit(solution)/shard_map/ppermute | solution.py:840
  207.3 13.8 %collective-permute-start.23 = (f32[2,32,1024]{2,1,0:T(8,128)}, f32[2,32,1024]{2,1,0:T(8,128)}, u32[]{:S(2)}, u32[]{:S(2)}) collective-permute-start(f32[2,32,1024]{2,1,0:T(8,128)} %get-tuple-element.170.refs_1_), channel_id=1, source_target_pairs={{0,8},{4,12},{8,0},{12,4},{16,24},{20,28},{24,16},{28,20},{1,9},{5... | collective-permute-start | bytes 786440 | tf_op jit(solution)/shard_map/ppermute | solution.py:840
  210.5 14.8 %collective-permute-start.27 = (f32[2,32,1024]{2,1,0:T(8,128)}, f32[2,32,1024]{2,1,0:T(8,128)}, u32[]{:S(2)}, u32[]{:S(2)}) collective-permute-start(f32[2,32,1024]{2,1,0:T(8,128)} %get-tuple-element.179), channel_id=1, source_target_pairs={{0,16},{4,20},{8,24},{12,28},{16,0},{20,4},{24,8},{28,12},{1,17},{... | collective-permute-start | bytes 786440 | tf_op jit(solution)/shard_map/ppermute | solution.py:840
  222.8 13.8 %collective-permute-start.26 = (f32[2,32,1024]{2,1,0:T(8,128)}, f32[2,32,1024]{2,1,0:T(8,128)}, u32[]{:S(2)}, u32[]{:S(2)}) collective-permute-start(f32[2,32,1024]{2,1,0:T(8,128)} %get-tuple-element.177), channel_id=1, source_target_pairs={{0,16},{4,20},{8,24},{12,28},{16,0},{20,4},{24,8},{28,12},{1,17},{... | collective-permute-start | bytes 786440 | tf_op jit(solution)/shard_map/ppermute | solution.py:840
  (35 other events, 175.0 us)

commit v3 on v2

--- a/solution.py
+++ b/solution.py
@@ -910,16 +910,16 @@
     y_ex[0].step()
     y_ex[1].begin()
     for ex in z_ex:
-        (y_away,) = ex.step([y_away])
+        y_away, y_ex[2].own = ex.step([y_away, y_ex[2].own])
         ex.finish()
+    y_ex[2].begin()
     y_came = send("row", y_away, other_neighbour)
-    flux, (y_ex[2].own,) = flux_x_call(order, velocity, flux, derivative_x, 1, 2, [y_ex[2].own])
+    flux, _ = flux_x_call(order, velocity, flux, derivative_x, 1, 2, [])
     y_ex[0].step()
     y_ex[1].step()
-    y_ex[2].begin()
+    y_ex[2].step()
     (my, mz), (sy, sz), (fy, fz) = smoothing_call(order, pos, (smoothing_y, smoothing_z), lines)
     y_ex[1].step()
-    y_ex[2].step()
     z_came = None if four else send("col", z_away, other_neighbour)
 
     t_z, t_y = [None] * count_c, [None] * count_c
@@ -957,9 +957,9 @@
     whole = filter_yz(1, whole)
     g_ex[0].step()
     whole = filter_yz(2, whole)
+    came = send("row", whole, other_neighbour)
     g_ex[1].step()
-    (whole,) = g_ex[0].step([whole])
-    came = send("row", whole, other_neighbour)
+    g_ex[0].step()
     g_ex[2].step()
     g_ex[1].step()
     out = None

time: 248 us -> 235 us (0.948)
  waiting for transfers between devices: 66.3 us -> 33.9 us
  starting transfers between devices: 26.4 us -> 49.6 us
  local copies, waits for them, and re-layouts: 15.6 us -> 13.1 us
    ppermute x28, waiting for transfers between devices: 66.3 us -> 33.9 us  [send(): lax.ppermute(array, axis, [(i, target(i) % blocks) for i in range(blocks)])]
    ppermute x28, starting transfers between devices: 26.4 us -> 49.6 us  [send(): lax.ppermute(array, axis, [(i, target(i) % blocks) for i in range(blocks)])]
    unnamed x78 -> x70, local copies, waits for them, and re-layouts: 15 us -> 12.5 us
  transfers between devices with their start and end apart: 28 -> 28, of which waited for: 10 -> 12; matrix products, arithmetic and copies ran while one was open for 0% -> 0% of each run, Pallas kernels for 44% -> 47%
where the time goes in v3:
time: 235 us; the launch traced here: 233 us
  Pallas kernels  136 us (58%)
  starting transfers between devices  49.6 us (21%)
  waiting for transfers between devices  33.9 us (14%)
  local copies, waits for them, and re-layouts  13.1 us (6%)
    pallas_call x29, Pallas kernels, call(): pl.pallas_call(body, in_specs=list(in_specs) + untouched, out_specs=list(...  136 us
    ppermute x28, starting transfers between devices, send(): lax.ppermute(array, axis, [(i, target(i) % blocks) for i in range(blocks)])  49.6 us
    ppermute x28, waiting for transfers between devices, send(): lax.ppermute(array, axis, [(i, target(i) % blocks) for i in range(blocks)])  33.9 us
    unnamed x70, local copies, waits for them, and re-layouts  12.5 us
  transfers between devices with their start and end apart: 28, of which 12 were waited for; matrix products, arithmetic and copies ran while one was open for 0% of the time, Pallas kernels for 47%

profile of v3, /device:TPU:4, one launch (start us, length us, event | category | flops | bytes accessed | tf_op | source)
XLA Modules:
  0.0 233.2 jit_solution(6979104300769563551)
XLA Ops:
  1.2 17.4 %flux_yz.1 = (f32[3,32,32,1024]{3,2,1,0:T(8,128)}, f32[4,32,1024]{2,1,0:T(8,128)}, f32[4,32,1024]{2,1,0:T(8,128)}, f32[4,32,1024]{2,1,0:T(8,128)}, f32[6,32,1024...) custom-call(s32[2]{0:T(128)} %pad_add_fusion.refs_0_, ...), custom_call_target="tpu_custom_call", output_to_operand_aliasing={{11}: (5, {})} | custom-call | flops 12884901888000 | bytes 28311552000 | tf_op jit(solution)/shard_map/flux_yz/pallas_call | solution.py:657
  18.8 13.3 %flux_x.2 = (f32[3,32,32,1024]{3,2,1,0:T(8,128)}, f32[8,128]{1,0:T(8,128)}, f32[4,32,1024]{2,1,0:T(8,128)}, f32[4,32,1024]{2,1,0:T(8,128)}, f32[6,32,1024]{2,1,0:T(8,128)}) custom-call(f32[3,32,32,1024]{3,2,1,0:T(8,128)} %refs_0_.3, ...), custom_call_target="tpu_custom_call", output_to_operand_aliasing={{0}: (1, {}), {1}: (3, {}), {2}: (4, {}), {3}: (5, {}), {4}... | custom-call | flops 6442450944000 | bytes 20447232000 | tf_op jit(solution)/shard_map/flux_x/pallas_call | solution.py:657
  32.1 2.0 collective-permute-start.3
  42.4 2.8 %merge.17 = (f32[12,32,1024]{2,1,0:T(8,128)}, f32[8,128]{1,0:T(8,128)}, f32[6,32,1024]{2,1,0:T(8,128)}, f32[4,32,1024]{2,1,0:T(8,128)}) custom-call(f32[16,128]{1,0:T(8,128)S(1)} %copy-done.33, f32[12,32,1024]{2,1,0:T(8,128)S(1)} %copy-done.1, ...), custom_call_target="tpu_custom_call", output_to_operand_aliasing={{1}: (4, {}), {2}: (5, {}), {3}: (6, {})} | custom-call | flops 3145728000 | bytes 4718592000 | tf_op jit(solution)/shard_map/merge/pallas_call | solution.py:657
  47.2 13.3 %flux_x.3 = (f32[3,32,32,1024]{3,2,1,0:T(8,128)}, f32[8,128]{1,0:T(8,128)}) custom-call(f32[3,32,32,1024]{3,2,1,0:T(8,128)} %refs_0_.3, f32[3,32,32,1024]{3,2,1,0:T(8,128)} %get-tuple-element.99.refs_1_, f32[1024,1024]{1,0:T(8,128)} %refs_2_.6, f32[8,128]{1,0:T(8,128)} %get-tuple-element.109.refs_3_), custom_call_target="tpu_custom_call", output_to_operand_aliasing={{0}: (1, {}), {1}: (3, {})} | custom-call | flops 6442450944000 | bytes 20447232000 | tf_op jit(solution)/shard_map/flux_x/pallas_call | solution.py:657
  64.0 2.6 %collective-permute-start.7 = (f32[2,32,1024]{2,1,0:T(8,128)}, f32[2,32,1024]{2,1,0:T(8,128)S(1)}, u32[]{:S(2)}, u32[]{:S(2)}) collective-permute-start(f32[2,32,1024]{2,1,0:T(8,128)} %get-tuple-element.123), channel_id=1, source_target_pairs={{0,16},{4,20},{8,24},{12,28},{16,0},{20,4},{24,8},{28,12},{1,17},{... | collective-permute-start | bytes 786440 | tf_op jit(solution)/shard_map/ppermute | solution.py:840
  70.7 5.1 %collective-permute-done.2.refs_2_.refs_6_ = f32[4,32,1024]{2,1,0:T(8,128)} collective-permute-done((f32[4,32,1024]{2,1,0:T(8,128)}, f32[4,32,1024]{2,1,0:T(8,128)}, u32[]{:S(2)}, u32[]{:S(2)}) %collective-permute-start.2) | collective-permute-done | bytes 524320 | tf_op jit(solution)/shard_map/ppermute | solution.py:840
  83.4 2.7 %collective-permute-start.12 = (f32[2,32,1024]{2,1,0:T(8,128)}, f32[2,32,1024]{2,1,0:T(8,128)}, u32[]{:S(2)}, u32[]{:S(2)}) collective-permute-start(f32[2,32,1024]{2,1,0:T(8,128)} %get-tuple-element.133), channel_id=1, source_target_pairs={{0,16},{4,20},{8,24},{12,28},{16,0},{20,4},{24,8},{28,12},{1,17},{... | collective-permute-start | bytes 786440 | tf_op jit(solution)/shard_map/ppermute | solution.py:840
  86.8 7.6 %advance_z.3 = (f32[32,32,1024]{2,1,0:T(8,128)S(1)}, f32[4,32,1024]{2,1,0:T(8,128)}, f32[2,32,1024]{2,1,0:T(8,128)}, f32[8,128]{1,0:T(8,128)}) custom-call(f32[3,32,32,1024]{3,2,1,0:T(8,128)} %get-tuple-element.110.refs_0_, bf16[608,256]{1,0:T(8,128)(2,1)} %copy-done.32, ...), custom_call_target="tpu_custom_call", output_to_operand_aliasing={{3}: (12, {})} | custom-call | flops 2147483648000 | bytes 9437184000 | tf_op jit(solution)/shard_map/advance_z/pallas_call | solution.py:657
  96.5 2.6 %collective-permute-done.12.refs_9_ = f32[2,32,1024]{2,1,0:T(8,128)} collective-permute-done((f32[2,32,1024]{2,1,0:T(8,128)}, f32[2,32,1024]{2,1,0:T(8,128)}, u32[]{:S(2)}, u32[]{:S(2)}) %collective-permute-start.12) | collective-permute-done | bytes 262176 | tf_op jit(solution)/shard_map/ppermute | solution.py:840
  99.0 7.4 %advance_z.4 = (f32[32,32,1024]{2,1,0:T(8,128)S(1)}, f32[4,32,1024]{2,1,0:T(8,128)}, f32[2,32,1024]{2,1,0:T(8,128)}, f32[8,128]{1,0:T(8,128)}) custom-call(f32[3,32,32,1024]{3,2,1,0:T(8,128)} %get-tuple-element.110.refs_0_, bf16[608,256]{1,0:T(8,128)(2,1)} %copy-done.32, ...), custom_call_target="tpu_custom_call", output_to_operand_aliasing={{3}: (12, {})} | custom-call | flops 2147483648000 | bytes 9437184000 | tf_op jit(solution)/shard_map/advance_z/pallas_call | solution.py:657
  106.6 1.9 merge.23
  108.6 2.9 %collective-permute-done.10.refs_9_ = f32[2,32,1024]{2,1,0:T(8,128)} collective-permute-done((f32[2,32,1024]{2,1,0:T(8,128)}, f32[2,32,1024]{2,1,0:T(8,128)}, u32[]{:S(2)}, u32[]{:S(2)}) %collective-permute-start.10) | collective-permute-done | bytes 262176 | tf_op jit(solution)/shard_map/ppermute | solution.py:840
  111.5 7.4 %advance_z.5 = (f32[32,32,1024]{2,1,0:T(8,128)S(1)}, f32[4,32,1024]{2,1,0:T(8,128)}, f32[2,32,1024]{2,1,0:T(8,128)}, f32[8,128]{1,0:T(8,128)}) custom-call(f32[3,32,32,1024]{3,2,1,0:T(8,128)} %get-tuple-element.110.refs_0_, bf16[608,256]{1,0:T(8,128)(2,1)} %copy-done.32, ...), custom_call_target="tpu_custom_call", output_to_operand_aliasing={{3}: (12, {})} | custom-call | flops 2147483648000 | bytes 9437184000 | tf_op jit(solution)/shard_map/advance_z/pallas_call | solution.py:657
  119.0 1.9 merge.24
  122.4 5.5 %filter_y.3 = (f32[32,32,1024]{2,1,0:T(8,128)S(1)}, f32[4,32,1024]{2,1,0:T(8,128)}, f32[6,32,1024]{2,1,0:T(8,128)}, f32[8,128]{1,0:T(8,128)}) custom-call(f32[32,32,1024]{2,1,0:T(8,128)S(1)} %get-tuple-element.142.refs_0_, bf16[608,256]{1,0:T(8,128)(2,1)S(1)} %get-tuple-element.138.refs_1_, ...), custom_call_target="tpu_custom_call", output_to_operand_aliasing={{3}: (6, {})} | custom-call | flops 2147483648000 | bytes 9437184000 | tf_op jit(solution)/shard_map/filter_y/pallas_call | solution.py:657
  127.9 1.9 merge.25
  130.3 2.7 %collective-permute-start.18 = (f32[4,32,1024]{2,1,0:T(8,128)}, f32[4,32,1024]{2,1,0:T(8,128)}, u32[]{:S(2)}, u32[]{:S(2)}) collective-permute-start(f32[4,32,1024]{2,1,0:T(8,128)} %get-tuple-element.156.refs_1_), channel_id=1, source_target_pairs={{0,4},{4,0},{8,12},{12,8},{16,20},{20,16},{24,28},{28,24},{1,5},{5... | collective-permute-start | bytes 1572872 | tf_op jit(solution)/shard_map/ppermute | solution.py:840
  134.9 5.5 %filter_y.4 = (f32[32,32,1024]{2,1,0:T(8,128)S(1)}, f32[4,32,1024]{2,1,0:T(8,128)}, f32[6,32,1024]{2,1,0:T(8,128)}, f32[8,128]{1,0:T(8,128)}) custom-call(f32[32,32,1024]{2,1,0:T(8,128)S(1)} %get-tuple-element.150.refs_0_, bf16[608,256]{1,0:T(8,128)(2,1)S(1)} %get-tuple-element.138.refs_1_, ...), custom_call_target="tpu_custom_call", output_to_operand_aliasing={{2}: (6, {}), {3}: (7, {})} | custom-call | flops 2147483648000 | bytes 9437184000 | tf_op jit(solution)/shard_map/filter_y/pallas_call | solution.py:657
  140.9 4.8 %collective-permute-done.18.refs_2_.refs_4_ = f32[4,32,1024]{2,1,0:T(8,128)} collective-permute-done((f32[4,32,1024]{2,1,0:T(8,128)}, f32[4,32,1024]{2,1,0:T(8,128)}, u32[]{:S(2)}, u32[]{:S(2)}) %collective-permute-start.18) | collective-permute-done | bytes 524320 | tf_op jit(solution)/shard_map/ppermute | solution.py:840
  147.4 5.5 %filter_y.5 = (f32[32,32,1024]{2,1,0:T(8,128)S(1)}, f32[4,32,1024]{2,1,0:T(8,128)}, f32[6,32,1024]{2,1,0:T(8,128)}, f32[8,128]{1,0:T(8,128)}) custom-call(f32[32,32,1024]{2,1,0:T(8,128)S(1)} %get-tuple-element.137.refs_0_, bf16[608,256]{1,0:T(8,128)(2,1)S(1)} %get-tuple-element.138.refs_1_, ...), custom_call_target="tpu_custom_call", output_to_operand_aliasing={{2}: (6, {}), {3}: (7, {})} | custom-call | flops 2147483648000 | bytes 9437184000 | tf_op jit(solution)/shard_map/filter_y/pallas_call | solution.py:657
  152.9 5.3 %collective-permute-start.20 = (f32[6,32,1024]{2,1,0:T(8,128)}, f32[6,32,1024]{2,1,0:T(8,128)S(1)}, u32[]{:S(2)}, u32[]{:S(2)}) collective-permute-start(f32[6,32,1024]{2,1,0:T(8,128)} %get-tuple-element.162), channel_id=1, source_target_pairs={{0,28},{4,8},{8,4},{12,16},{16,12},{20,24},{24,20},{28,0},{1,29},{... | collective-permute-start | bytes 2359304 | tf_op jit(solution)/shard_map/ppermute | solution.py:840
  158.2 5.1 %collective-permute-start.19 = (f32[4,32,1024]{2,1,0:T(8,128)}, f32[4,32,1024]{2,1,0:T(8,128)S(1)}, u32[]{:S(2)}, u32[]{:S(2)}) collective-permute-start(f32[4,32,1024]{2,1,0:T(8,128)} %get-tuple-element.161.refs_1_), channel_id=1, source_target_pairs={{0,4},{4,0},{8,12},{12,8},{16,20},{20,16},{24,28},{28,24},{1,5},{5... | collective-permute-start | bytes 1572872 | tf_op jit(solution)/shard_map/ppermute | solution.py:840
  165.0 16.5 %collective-permute-start.25 = (f32[2,32,1024]{2,1,0:T(8,128)}, f32[2,32,1024]{2,1,0:T(8,128)S(1)}, u32[]{:S(2)}, u32[]{:S(2)}) collective-permute-start(f32[2,32,1024]{2,1,0:T(8,128)} %get-tuple-element.171.refs_1_), channel_id=1, source_target_pairs={{0,8},{4,12},{8,0},{12,4},{16,24},{20,28},{24,16},{28,20},{1,9},{5... | collective-permute-start | bytes 786440 | tf_op jit(solution)/shard_map/ppermute | solution.py:840
  181.6 3.9 %collective-permute-done.21.refs_2_.refs_6_ = f32[2,32,1024]{2,1,0:T(8,128)S(1)} collective-permute-done((f32[2,32,1024]{2,1,0:T(8,128)S(1)}, f32[2,32,1024]{2,1,0:T(8,128)S(1)}, u32[]{:S(2)}, u32[]{:S(2)}) %collective-permute-start.21) | collective-permute-done | bytes 262176 | tf_op jit(solution)/shard_map/ppermute | solution.py:840
  187.3 2.7 %collective-permute-done.19.refs_2_.refs_4_ = f32[4,32,1024]{2,1,0:T(8,128)S(1)} collective-permute-done((f32[4,32,1024]{2,1,0:T(8,128)}, f32[4,32,1024]{2,1,0:T(8,128)S(1)}, u32[]{:S(2)}, u32[]{:S(2)}) %collective-permute-start.19) | collective-permute-done | bytes 524320 | tf_op jit(solution)/shard_map/ppermute | solution.py:840
  194.7 3.4 %collective-permute-start.27 = (f32[2,32,1024]{2,1,0:T(8,128)}, f32[2,32,1024]{2,1,0:T(8,128)}, u32[]{:S(2)}, u32[]{:S(2)}) collective-permute-start(f32[2,32,1024]{2,1,0:T(8,128)} %get-tuple-element.177), channel_id=1, source_target_pairs={{0,16},{4,20},{8,24},{12,28},{16,0},{20,4},{24,8},{28,12},{1,17},{... | collective-permute-start | bytes 786440 | tf_op jit(solution)/shard_map/ppermute | solution.py:840
  198.1 3.9 %collective-permute-done.24.refs_7_ = f32[2,32,1024]{2,1,0:T(8,128)S(1)} collective-permute-done((f32[2,32,1024]{2,1,0:T(8,128)}, f32[2,32,1024]{2,1,0:T(8,128)S(1)}, u32[]{:S(2)}, u32[]{:S(2)}) %collective-permute-start.24) | collective-permute-done | bytes 262176 | tf_op jit(solution)/shard_map/ppermute | solution.py:840
  202.0 8.5 %filter_x.3 = (f32[3,32,32,1024]{3,2,1,0:T(8,128)}, f32[8,128]{1,0:T(8,128)}) custom-call(f32[32,32,1024]{2,1,0:T(8,128)S(1)} %get-tuple-element.169.refs_0_, f32[1024,1024]{1,0:T(8,128)S(1)} %copy-done, f32[28,128]{1,0:T(8,128)S(1)} %get-tuple-element.155.refs_0_.refs_2_, ...), custom_call_target="tpu_custom_call", output_to_operand_aliasing={{1}: (8, {})} | custom-call | flops 6442450944000 | bytes 13631488000 | tf_op jit(solution)/shard_map/filter_x/pallas_call | solution.py:657
  212.5 8.5 %filter_x.4 = (f32[3,32,32,1024]{3,2,1,0:T(8,128)}, f32[8,128]{1,0:T(8,128)}) custom-call(f32[32,32,1024]{2,1,0:T(8,128)S(1)} %get-tuple-element.176.refs_0_, f32[1024,1024]{1,0:T(8,128)S(1)} %copy-done, f32[28,128]{1,0:T(8,128)S(1)} %get-tuple-element.155.refs_0_.refs_2_, ...), custom_call_target="tpu_custom_call", output_to_operand_aliasing={{0}: (8, {}), {1}: (9, {})} | custom-call | flops 6442450944000 | bytes 13631488000 | tf_op jit(solution)/shard_map/filter_x/pallas_call | solution.py:657
  221.0 3.8 %collective-permute-done.26.refs_7_ = f32[2,32,1024]{2,1,0:T(8,128)} collective-permute-done((f32[2,32,1024]{2,1,0:T(8,128)}, f32[2,32,1024]{2,1,0:T(8,128)}, u32[]{:S(2)}, u32[]{:S(2)}) %collective-permute-start.26) | collective-permute-done | bytes 262176 | tf_op jit(solution)/shard_map/ppermute | solution.py:840
  224.8 8.4 %filter_x.5 = (f32[3,32,32,1024]{3,2,1,0:T(8,128)}, f32[8,128]{1,0:T(8,128)}) custom-call(f32[32,32,1024]{2,1,0:T(8,128)S(1)} %get-tuple-element.159.refs_0_, f32[1024,1024]{1,0:T(8,128)S(1)} %copy-done, f32[28,128]{1,0:T(8,128)S(1)} %get-tuple-element.155.refs_0_.refs_2_, ...), custom_call_target="tpu_custom_call", output_to_operand_aliasing={{0}: (8, {}), {1}: (9, {})} | custom-call | flops 6442450944000 | bytes 13631488000 | tf_op jit(solution)/shard_map/filter_x/pallas_call | solution.py:657
  (125 shorter events, 46.2 us)
Async XLA Ops:
  18.6 20.5 %collective-permute-start = (f32[12,32,1024]{2,1,0:T(8,128)}, f32[12,32,1024]{2,1,0:T(8,128)}, u32[]{:S(2)}, u32[]{:S(2)}) collective-permute-start(f32[12,32,1024]{2,1,0:T(8,128)} %get-tuple-element.101.refs_1_), channel_id=1, source_target_pairs={{0,1},{1,0},{2,3},{3,2},{4,5},{5,4},{6,7},{7,6},{8,9},{9,8},{10,11... | collective-permute-start | bytes 4718600 | tf_op jit(solution)/shard_map/ppermute | solution.py:840
  18.7 15.4 %collective-permute-start.1 = (f32[4,32,1024]{2,1,0:T(8,128)}, f32[4,32,1024]{2,1,0:T(8,128)}, u32[]{:S(2)}, u32[]{:S(2)}) collective-permute-start(f32[4,32,1024]{2,1,0:T(8,128)} %get-tuple-element.104.refs_1_), channel_id=1, source_target_pairs={{0,4},{4,0},{8,12},{12,8},{16,20},{20,16},{24,28},{28,24},{1,5},{5... | collective-permute-start | bytes 1572872 | tf_op jit(solution)/shard_map/ppermute | solution.py:840
  32.1 34.5 %collective-permute-start.3 = (f32[4,32,1024]{2,1,0:T(8,128)}, f32[4,32,1024]{2,1,0:T(8,128)}, u32[]{:S(2)}, u32[]{:S(2)}) collective-permute-start(f32[4,32,1024]{2,1,0:T(8,128)} %get-tuple-element.112.refs_1_), channel_id=1, source_target_pairs={{0,4},{4,0},{8,12},{12,8},{16,20},{20,16},{24,28},{28,24},{1,5},{5... | collective-permute-start | bytes 1572872 | tf_op jit(solution)/shard_map/ppermute | solution.py:840
  37.6 23.0 %collective-permute-start.4 = (f32[2,32,1024]{2,1,0:T(8,128)}, f32[2,32,1024]{2,1,0:T(8,128)}, u32[]{:S(2)}, u32[]{:S(2)}) collective-permute-start(f32[2,32,1024]{2,1,0:T(8,128)} %get-tuple-element.113.refs_1_), channel_id=1, source_target_pairs={{0,8},{4,12},{8,0},{12,4},{16,24},{20,28},{24,16},{28,20},{1,9},{5... | collective-permute-start | bytes 786440 | tf_op jit(solution)/shard_map/ppermute | solution.py:840
  45.2 30.6 %collective-permute-start.2 = (f32[4,32,1024]{2,1,0:T(8,128)}, f32[4,32,1024]{2,1,0:T(8,128)}, u32[]{:S(2)}, u32[]{:S(2)}) collective-permute-start(f32[4,32,1024]{2,1,0:T(8,128)} %get-tuple-element.111.refs_1_), channel_id=1, source_target_pairs={{0,4},{4,0},{8,12},{12,8},{16,20},{20,16},{24,28},{28,24},{1,5},{5... | collective-permute-start | bytes 1572872 | tf_op jit(solution)/shard_map/ppermute | solution.py:840
  45.7 40.4 %collective-permute-start.5 = (f32[6,32,1024]{2,1,0:T(8,128)}, f32[6,32,1024]{2,1,0:T(8,128)}, u32[]{:S(2)}, u32[]{:S(2)}) collective-permute-start(f32[6,32,1024]{2,1,0:T(8,128)} %get-tuple-element.121), channel_id=1, source_target_pairs={{0,28},{4,8},{8,4},{12,16},{16,12},{20,24},{24,20},{28,0},{1,29},{... | collective-permute-start | bytes 2359304 | tf_op jit(solution)/shard_map/ppermute | solution.py:840
  47.1 39.0 %collective-permute-start.8 = (f32[12,32,1024]{2,1,0:T(8,128)}, f32[12,32,1024]{2,1,0:T(8,128)}, u32[]{:S(2)}, u32[]{:S(2)}) collective-permute-start(f32[12,32,1024]{2,1,0:T(8,128)} %get-tuple-element.124), channel_id=1, source_target_pairs={{0,3},{1,2},{2,1},{3,0},{4,7},{5,6},{6,5},{7,4},{8,11},{9,10},{10,... | collective-permute-start | bytes 4718600 | tf_op jit(solution)/shard_map/ppermute | solution.py:840
  60.5 18.8 %copy-start.13 = (f32[256,256]{1,0:T(8,128)S(1)}, f32[256,256]{1,0:T(8,128)}, u32[]{:S(2)}) copy-start(f32[256,256]{1,0:T(8,128)} %refs_1_.6) | copy-start | bytes 786436
  62.2 17.0 %copy-start.23 = (f32[128,128]{1,0:T(8,128)S(1)}, f32[128,128]{1,0:T(8,128)}, u32[]{:S(2)}) copy-start(f32[128,128]{1,0:T(8,128)} %refs_2_.7) | copy-start | bytes 196612
  62.2 17.0 %copy-start.24 = (s32[2]{0:T(128)S(1)}, s32[2]{0:T(128)}, u32[]{:S(2)}) copy-start(s32[2]{0:T(128)} %pad_add_fusion.refs_0_) | copy-start | bytes 28
  64.0 22.1 %collective-permute-start.7 = (f32[2,32,1024]{2,1,0:T(8,128)}, f32[2,32,1024]{2,1,0:T(8,128)S(1)}, u32[]{:S(2)}, u32[]{:S(2)}) collective-permute-start(f32[2,32,1024]{2,1,0:T(8,128)} %get-tuple-element.123), channel_id=1, source_target_pairs={{0,16},{4,20},{8,24},{12,28},{16,0},{20,4},{24,8},{28,12},{1,17},{... | collective-permute-start | bytes 786440 | tf_op jit(solution)/shard_map/ppermute | solution.py:840
  69.4 12.6 %collective-permute-start.9 = (f32[2,32,1024]{2,1,0:T(8,128)}, f32[2,32,1024]{2,1,0:T(8,128)S(1)}, u32[]{:S(2)}, u32[]{:S(2)}) collective-permute-start(f32[2,32,1024]{2,1,0:T(8,128)} %get-tuple-element.125.refs_1_), channel_id=1, source_target_pairs={{0,8},{4,12},{8,0},{12,4},{16,24},{20,28},{24,16},{28,20},{1,9},{5... | collective-permute-start | bytes 786440 | tf_op jit(solution)/shard_map/ppermute | solution.py:840
  78.6 15.9 %collective-permute-start.6 = (f32[2,32,1024]{2,1,0:T(8,128)}, f32[2,32,1024]{2,1,0:T(8,128)}, u32[]{:S(2)}, u32[]{:S(2)}) collective-permute-start(f32[2,32,1024]{2,1,0:T(8,128)} %get-tuple-element.122.refs_1_), channel_id=1, source_target_pairs={{0,8},{4,12},{8,0},{12,4},{16,24},{20,28},{24,16},{28,20},{1,9},{5... | collective-permute-start | bytes 786440 | tf_op jit(solution)/shard_map/ppermute | solution.py:840
  83.4 15.7 %collective-permute-start.12 = (f32[2,32,1024]{2,1,0:T(8,128)}, f32[2,32,1024]{2,1,0:T(8,128)}, u32[]{:S(2)}, u32[]{:S(2)}) collective-permute-start(f32[2,32,1024]{2,1,0:T(8,128)} %get-tuple-element.133), channel_id=1, source_target_pairs={{0,16},{4,20},{8,24},{12,28},{16,0},{20,4},{24,8},{28,12},{1,17},{... | collective-permute-start | bytes 786440 | tf_op jit(solution)/shard_map/ppermute | solution.py:840
  96.2 15.3 %collective-permute-start.10 = (f32[2,32,1024]{2,1,0:T(8,128)}, f32[2,32,1024]{2,1,0:T(8,128)}, u32[]{:S(2)}, u32[]{:S(2)}) collective-permute-start(f32[2,32,1024]{2,1,0:T(8,128)} %get-tuple-element.129), channel_id=1, source_target_pairs={{0,16},{4,20},{8,24},{12,28},{16,0},{20,4},{24,8},{28,12},{1,17},{... | collective-permute-start | bytes 786440 | tf_op jit(solution)/shard_map/ppermute | solution.py:840
  96.4 10.1 %collective-permute-start.11 = (f32[4,32,1024]{2,1,0:T(8,128)}, f32[4,32,1024]{2,1,0:T(8,128)}, u32[]{:S(2)}, u32[]{:S(2)}) collective-permute-start(f32[4,32,1024]{2,1,0:T(8,128)} %get-tuple-element.131.refs_1_), channel_id=1, source_target_pairs={{0,1},{1,0},{2,3},{3,2},{4,5},{5,4},{6,7},{7,6},{8,9},{9,8},{10,11... | collective-permute-start | bytes 1572872 | tf_op jit(solution)/shard_map/ppermute | solution.py:840
  106.5 12.5 %collective-permute-start.15 = (f32[4,32,1024]{2,1,0:T(8,128)}, f32[4,32,1024]{2,1,0:T(8,128)}, u32[]{:S(2)}, u32[]{:S(2)}) collective-permute-start(f32[4,32,1024]{2,1,0:T(8,128)} %get-tuple-element.144.refs_1_), channel_id=1, source_target_pairs={{0,1},{1,0},{2,3},{3,2},{4,5},{5,4},{6,7},{7,6},{8,9},{9,8},{10,11... | collective-permute-start | bytes 1572872 | tf_op jit(solution)/shard_map/ppermute | solution.py:840
  108.5 13.9 %collective-permute-start.14 = (f32[4,32,1024]{2,1,0:T(8,128)}, f32[4,32,1024]{2,1,0:T(8,128)}, u32[]{:S(2)}, u32[]{:S(2)}) collective-permute-start(f32[4,32,1024]{2,1,0:T(8,128)} %get-tuple-element.143), channel_id=1, source_target_pairs={{0,3},{1,2},{2,1},{3,0},{4,7},{5,6},{6,5},{7,4},{8,11},{9,10},{10,... | collective-permute-start | bytes 1572872 | tf_op jit(solution)/shard_map/ppermute | solution.py:840
  118.9 9.0 %collective-permute-start.13 = (f32[4,32,1024]{2,1,0:T(8,128)}, f32[4,32,1024]{2,1,0:T(8,128)}, u32[]{:S(2)}, u32[]{:S(2)}) collective-permute-start(f32[4,32,1024]{2,1,0:T(8,128)} %get-tuple-element.140.refs_1_), channel_id=1, source_target_pairs={{0,1},{1,0},{2,3},{3,2},{4,5},{5,4},{6,7},{7,6},{8,9},{9,8},{10,11... | collective-permute-start | bytes 1572872 | tf_op jit(solution)/shard_map/ppermute | solution.py:840
  120.9 13.9 %collective-permute-start.17 = (f32[4,32,1024]{2,1,0:T(8,128)}, f32[4,32,1024]{2,1,0:T(8,128)}, u32[]{:S(2)}, u32[]{:S(2)}) collective-permute-start(f32[4,32,1024]{2,1,0:T(8,128)} %get-tuple-element.151), channel_id=1, source_target_pairs={{0,3},{1,2},{2,1},{3,0},{4,7},{5,6},{6,5},{7,4},{8,11},{9,10},{10,... | collective-permute-start | bytes 1572872 | tf_op jit(solution)/shard_map/ppermute | solution.py:840
  129.9 17.6 %collective-permute-start.16 = (f32[4,32,1024]{2,1,0:T(8,128)}, f32[4,32,1024]{2,1,0:T(8,128)}, u32[]{:S(2)}, u32[]{:S(2)}) collective-permute-start(f32[4,32,1024]{2,1,0:T(8,128)} %get-tuple-element.149), channel_id=1, source_target_pairs={{0,3},{1,2},{2,1},{3,0},{4,7},{5,6},{6,5},{7,4},{8,11},{9,10},{10,... | collective-permute-start | bytes 1572872 | tf_op jit(solution)/shard_map/ppermute | solution.py:840
  130.3 15.4 %collective-permute-start.18 = (f32[4,32,1024]{2,1,0:T(8,128)}, f32[4,32,1024]{2,1,0:T(8,128)}, u32[]{:S(2)}, u32[]{:S(2)}) collective-permute-start(f32[4,32,1024]{2,1,0:T(8,128)} %get-tuple-element.156.refs_1_), channel_id=1, source_target_pairs={{0,4},{4,0},{8,12},{12,8},{16,20},{20,16},{24,28},{28,24},{1,5},{5... | collective-permute-start | bytes 1572872 | tf_op jit(solution)/shard_map/ppermute | solution.py:840
  140.4 22.9 %collective-permute-start.22 = (f32[4,32,1024]{2,1,0:T(8,128)}, f32[4,32,1024]{2,1,0:T(8,128)}, u32[]{:S(2)}, u32[]{:S(2)}) collective-permute-start(f32[4,32,1024]{2,1,0:T(8,128)} %get-tuple-element.164.refs_1_), channel_id=1, source_target_pairs={{0,4},{4,0},{8,12},{12,8},{16,20},{20,16},{24,28},{28,24},{1,5},{5... | collective-permute-start | bytes 1572872 | tf_op jit(solution)/shard_map/ppermute | solution.py:840
  152.9 49.1 %copy-start = (f32[1024,1024]{1,0:T(8,128)S(1)}, f32[1024,1024]{1,0:T(8,128)}, u32[]{:S(2)}) copy-start(f32[1024,1024]{1,0:T(8,128)} %refs_1_.9) | copy-start | bytes 12582916
  152.9 49.1 %collective-permute-start.20 = (f32[6,32,1024]{2,1,0:T(8,128)}, f32[6,32,1024]{2,1,0:T(8,128)S(1)}, u32[]{:S(2)}, u32[]{:S(2)}) collective-permute-start(f32[6,32,1024]{2,1,0:T(8,128)} %get-tuple-element.162), channel_id=1, source_target_pairs={{0,28},{4,8},{8,4},{12,16},{16,12},{20,24},{24,20},{28,0},{1,29},{... | collective-permute-start | bytes 2359304 | tf_op jit(solution)/shard_map/ppermute | solution.py:840
  158.2 31.9 %collective-permute-start.19 = (f32[4,32,1024]{2,1,0:T(8,128)}, f32[4,32,1024]{2,1,0:T(8,128)S(1)}, u32[]{:S(2)}, u32[]{:S(2)}) collective-permute-start(f32[4,32,1024]{2,1,0:T(8,128)} %get-tuple-element.161.refs_1_), channel_id=1, source_target_pairs={{0,4},{4,0},{8,12},{12,8},{16,20},{20,16},{24,28},{28,24},{1,5},{5... | collective-permute-start | bytes 1572872 | tf_op jit(solution)/shard_map/ppermute | solution.py:840
  163.3 22.2 %collective-permute-start.21 = (f32[2,32,1024]{2,1,0:T(8,128)S(1)}, f32[2,32,1024]{2,1,0:T(8,128)S(1)}, u32[]{:S(2)}, u32[]{:S(2)}) collective-permute-start(f32[2,32,1024]{2,1,0:T(8,128)S(1)} %copy-done.18), channel_id=1, source_target_pairs={{0,8},{4,12},{8,0},{12,4},{16,24},{20,28},{24,16},{28,20},{1,9},{5... | collective-permute-start | bytes 786440 | tf_op jit(solution)/shard_map/ppermute | solution.py:840
  165.0 27.9 %collective-permute-start.25 = (f32[2,32,1024]{2,1,0:T(8,128)}, f32[2,32,1024]{2,1,0:T(8,128)S(1)}, u32[]{:S(2)}, u32[]{:S(2)}) collective-permute-start(f32[2,32,1024]{2,1,0:T(8,128)} %get-tuple-element.171.refs_1_), channel_id=1, source_target_pairs={{0,8},{4,12},{8,0},{12,4},{16,24},{20,28},{24,16},{28,20},{1,9},{5... | collective-permute-start | bytes 786440 | tf_op jit(solution)/shard_map/ppermute | solution.py:840
  186.3 15.7 %collective-permute-start.24 = (f32[2,32,1024]{2,1,0:T(8,128)}, f32[2,32,1024]{2,1,0:T(8,128)S(1)}, u32[]{:S(2)}, u32[]{:S(2)}) collective-permute-start(f32[2,32,1024]{2,1,0:T(8,128)} %get-tuple-element.170), channel_id=1, source_target_pairs={{0,16},{4,20},{8,24},{12,28},{16,0},{20,4},{24,8},{28,12},{1,17},{... | collective-permute-start | bytes 786440 | tf_op jit(solution)/shard_map/ppermute | solution.py:840
  192.1 18.5 %collective-permute-start.23 = (f32[2,32,1024]{2,1,0:T(8,128)}, f32[2,32,1024]{2,1,0:T(8,128)}, u32[]{:S(2)}, u32[]{:S(2)}) collective-permute-start(f32[2,32,1024]{2,1,0:T(8,128)} %get-tuple-element.168.refs_1_), channel_id=1, source_target_pairs={{0,8},{4,12},{8,0},{12,4},{16,24},{20,28},{24,16},{28,20},{1,9},{5... | collective-permute-start | bytes 786440 | tf_op jit(solution)/shard_map/ppermute | solution.py:840
  194.7 17.8 %collective-permute-start.27 = (f32[2,32,1024]{2,1,0:T(8,128)}, f32[2,32,1024]{2,1,0:T(8,128)}, u32[]{:S(2)}, u32[]{:S(2)}) collective-permute-start(f32[2,32,1024]{2,1,0:T(8,128)} %get-tuple-element.177), channel_id=1, source_target_pairs={{0,16},{4,20},{8,24},{12,28},{16,0},{20,4},{24,8},{28,12},{1,17},{... | collective-permute-start | bytes 786440 | tf_op jit(solution)/shard_map/ppermute | solution.py:840
  212.3 12.5 %collective-permute-start.26 = (f32[2,32,1024]{2,1,0:T(8,128)}, f32[2,32,1024]{2,1,0:T(8,128)}, u32[]{:S(2)}, u32[]{:S(2)}) collective-permute-start(f32[2,32,1024]{2,1,0:T(8,128)} %get-tuple-element.175), channel_id=1, source_target_pairs={{0,16},{4,20},{8,24},{12,28},{16,0},{20,4},{24,8},{28,12},{1,17},{... | collective-permute-start | bytes 786440 | tf_op jit(solution)/shard_map/ppermute | solution.py:840
  (31 other events, 171.9 us)

commit v4 on v3

--- a/solution.py
+++ b/solution.py
@@ -12,7 +12,7 @@
 PADE = 9.0 / 20.0
 PADE_STENCIL = (63.0 / 80.0, 9.0 / 100.0, -7.0 / 1200.0)
 SPAN = 128
-LANES = 256
+LANES = 512
 DEPTH = 256
 ROWS = 128
 TILE = 256

time: 235 us -> 235 us (level)
  waiting for transfers between devices: 33.9 us -> 30.1 us
  starting transfers between devices: 49.6 us -> 52.9 us
    ppermute x28, waiting for transfers between devices: 33.9 us -> 30.1 us  [send(): lax.ppermute(array, axis, [(i, target(i) % blocks) for i in range(blocks)])]
    ppermute x28, starting transfers between devices: 49.6 us -> 52.9 us  [send(): lax.ppermute(array, axis, [(i, target(i) % blocks) for i in range(blocks)])]
  transfers between devices with their start and end apart: 28 -> 28, of which waited for: 12 -> 12; matrix products, arithmetic and copies ran while one was open for 0% -> 0% of each run, Pallas kernels for 47% -> 46%
where the time goes in v4:
time: 235 us; the launch traced here: 231 us
  Pallas kernels  134 us (57%)
  starting transfers between devices  52.9 us (23%)
  waiting for transfers between devices  30.1 us (13%)
  local copies, waits for them, and re-layouts  13.1 us (6%)
    pallas_call x29, Pallas kernels, call(): pl.pallas_call(body, in_specs=list(in_specs) + untouched, out_specs=list(...  134 us
    ppermute x28, starting transfers between devices, send(): lax.ppermute(array, axis, [(i, target(i) % blocks) for i in range(blocks)])  52.9 us
    ppermute x28, waiting for transfers between devices, send(): lax.ppermute(array, axis, [(i, target(i) % blocks) for i in range(blocks)])  30.1 us
    unnamed x70, local copies, waits for them, and re-layouts  12.5 us
  transfers between devices with their start and end apart: 28, of which 12 were waited for; matrix products, arithmetic and copies ran while one was open for 0% of the time, Pallas kernels for 46%

profile of v4, /device:TPU:4, one launch (start us, length us, event | category | flops | bytes accessed | tf_op | source)
XLA Modules:
  0.0 231.4 jit_solution(8724473806970217153)
XLA Ops:
  1.2 18.9 %flux_yz.1 = (f32[3,32,32,1024]{3,2,1,0:T(8,128)}, f32[4,32,1024]{2,1,0:T(8,128)}, f32[4,32,1024]{2,1,0:T(8,128)}, f32[4,32,1024]{2,1,0:T(8,128)}, f32[6,32,1024...) custom-call(s32[2]{0:T(128)} %pad_add_fusion.refs_0_, ...), custom_call_target="tpu_custom_call", output_to_operand_aliasing={{11}: (5, {})} | custom-call | flops 12884901888000 | bytes 28311552000 | tf_op jit(solution)/shard_map/flux_yz/pallas_call | solution.py:657
  20.3 13.3 %flux_x.2 = (f32[3,32,32,1024]{3,2,1,0:T(8,128)}, f32[8,128]{1,0:T(8,128)}, f32[4,32,1024]{2,1,0:T(8,128)}, f32[4,32,1024]{2,1,0:T(8,128)}, f32[6,32,1024]{2,1,0:T(8,128)}) custom-call(f32[3,32,32,1024]{3,2,1,0:T(8,128)} %refs_0_.3, ...), custom_call_target="tpu_custom_call", output_to_operand_aliasing={{0}: (1, {}), {1}: (3, {}), {2}: (4, {}), {3}: (5, {}), {4}... | custom-call | flops 6442450944000 | bytes 20447232000 | tf_op jit(solution)/shard_map/flux_x/pallas_call | solution.py:657
  33.6 2.0 collective-permute-start.3
  43.9 2.8 %merge.17 = (f32[12,32,1024]{2,1,0:T(8,128)}, f32[8,128]{1,0:T(8,128)}, f32[6,32,1024]{2,1,0:T(8,128)}, f32[4,32,1024]{2,1,0:T(8,128)}) custom-call(f32[16,128]{1,0:T(8,128)S(1)} %copy-done.33, f32[12,32,1024]{2,1,0:T(8,128)S(1)} %copy-done.1, ...), custom_call_target="tpu_custom_call", output_to_operand_aliasing={{1}: (4, {}), {2}: (5, {}), {3}: (6, {})} | custom-call | flops 3145728000 | bytes 4718592000 | tf_op jit(solution)/shard_map/merge/pallas_call | solution.py:657
  48.8 13.3 %flux_x.3 = (f32[3,32,32,1024]{3,2,1,0:T(8,128)}, f32[8,128]{1,0:T(8,128)}) custom-call(f32[3,32,32,1024]{3,2,1,0:T(8,128)} %refs_0_.3, f32[3,32,32,1024]{3,2,1,0:T(8,128)} %get-tuple-element.99.refs_1_, f32[1024,1024]{1,0:T(8,128)} %refs_2_.6, f32[8,128]{1,0:T(8,128)} %get-tuple-element.109.refs_3_), custom_call_target="tpu_custom_call", output_to_operand_aliasing={{0}: (1, {}), {1}: (3, {})} | custom-call | flops 6442450944000 | bytes 20447232000 | tf_op jit(solution)/shard_map/flux_x/pallas_call | solution.py:657
  65.6 2.6 %collective-permute-start.7 = (f32[2,32,1024]{2,1,0:T(8,128)}, f32[2,32,1024]{2,1,0:T(8,128)S(1)}, u32[]{:S(2)}, u32[]{:S(2)}) collective-permute-start(f32[2,32,1024]{2,1,0:T(8,128)} %get-tuple-element.123), channel_id=1, source_target_pairs={{0,16},{4,20},{8,24},{12,28},{16,0},{20,4},{24,8},{28,12},{1,17},{... | collective-permute-start | bytes 786440 | tf_op jit(solution)/shard_map/ppermute | solution.py:840
  72.3 5.1 %collective-permute-done.2.refs_2_.refs_6_ = f32[4,32,1024]{2,1,0:T(8,128)} collective-permute-done((f32[4,32,1024]{2,1,0:T(8,128)}, f32[4,32,1024]{2,1,0:T(8,128)}, u32[]{:S(2)}, u32[]{:S(2)}) %collective-permute-start.2) | collective-permute-done | bytes 524320 | tf_op jit(solution)/shard_map/ppermute | solution.py:840
  85.0 2.7 %collective-permute-start.12 = (f32[2,32,1024]{2,1,0:T(8,128)}, f32[2,32,1024]{2,1,0:T(8,128)}, u32[]{:S(2)}, u32[]{:S(2)}) collective-permute-start(f32[2,32,1024]{2,1,0:T(8,128)} %get-tuple-element.133), channel_id=1, source_target_pairs={{0,16},{4,20},{8,24},{12,28},{16,0},{20,4},{24,8},{28,12},{1,17},{... | collective-permute-start | bytes 786440 | tf_op jit(solution)/shard_map/ppermute | solution.py:840
  88.3 7.1 %advance_z.3 = (f32[32,32,1024]{2,1,0:T(8,128)S(1)}, f32[4,32,1024]{2,1,0:T(8,128)}, f32[2,32,1024]{2,1,0:T(8,128)}, f32[8,128]{1,0:T(8,128)}) custom-call(f32[3,32,32,1024]{3,2,1,0:T(8,128)} %get-tuple-element.110.refs_0_, bf16[608,256]{1,0:T(8,128)(2,1)} %copy-done.32, ...), custom_call_target="tpu_custom_call", output_to_operand_aliasing={{3}: (12, {})} | custom-call | flops 2147483648000 | bytes 9437184000 | tf_op jit(solution)/shard_map/advance_z/pallas_call | solution.py:657
  97.4 3.2 %collective-permute-done.12.refs_9_ = f32[2,32,1024]{2,1,0:T(8,128)} collective-permute-done((f32[2,32,1024]{2,1,0:T(8,128)}, f32[2,32,1024]{2,1,0:T(8,128)}, u32[]{:S(2)}, u32[]{:S(2)}) %collective-permute-start.12) | collective-permute-done | bytes 262176 | tf_op jit(solution)/shard_map/ppermute | solution.py:840
  100.6 7.0 %advance_z.4 = (f32[32,32,1024]{2,1,0:T(8,128)S(1)}, f32[4,32,1024]{2,1,0:T(8,128)}, f32[2,32,1024]{2,1,0:T(8,128)}, f32[8,128]{1,0:T(8,128)}) custom-call(f32[3,32,32,1024]{3,2,1,0:T(8,128)} %get-tuple-element.110.refs_0_, bf16[608,256]{1,0:T(8,128)(2,1)} %copy-done.32, ...), custom_call_target="tpu_custom_call", output_to_operand_aliasing={{3}: (12, {})} | custom-call | flops 2147483648000 | bytes 9437184000 | tf_op jit(solution)/shard_map/advance_z/pallas_call | solution.py:657
  109.8 2.7 %collective-permute-done.10.refs_9_ = f32[2,32,1024]{2,1,0:T(8,128)} collective-permute-done((f32[2,32,1024]{2,1,0:T(8,128)}, f32[2,32,1024]{2,1,0:T(8,128)}, u32[]{:S(2)}, u32[]{:S(2)}) %collective-permute-start.10) | collective-permute-done | bytes 262176 | tf_op jit(solution)/shard_map/ppermute | solution.py:840
  112.5 7.0 %advance_z.5 = (f32[32,32,1024]{2,1,0:T(8,128)S(1)}, f32[4,32,1024]{2,1,0:T(8,128)}, f32[2,32,1024]{2,1,0:T(8,128)}, f32[8,128]{1,0:T(8,128)}) custom-call(f32[3,32,32,1024]{3,2,1,0:T(8,128)} %get-tuple-element.110.refs_0_, bf16[608,256]{1,0:T(8,128)(2,1)} %copy-done.32, ...), custom_call_target="tpu_custom_call", output_to_operand_aliasing={{3}: (12, {})} | custom-call | flops 2147483648000 | bytes 9437184000 | tf_op jit(solution)/shard_map/advance_z/pallas_call | solution.py:657
  119.6 1.9 merge.24
  121.6 2.0 collective-permute-done.14.refs_5_
  123.6 4.9 %filter_y.3 = (f32[32,32,1024]{2,1,0:T(8,128)S(1)}, f32[4,32,1024]{2,1,0:T(8,128)}, f32[6,32,1024]{2,1,0:T(8,128)}, f32[8,128]{1,0:T(8,128)}) custom-call(f32[32,32,1024]{2,1,0:T(8,128)S(1)} %get-tuple-element.142.refs_0_, bf16[608,256]{1,0:T(8,128)(2,1)S(1)} %get-tuple-element.138.refs_1_, ...), custom_call_target="tpu_custom_call", output_to_operand_aliasing={{3}: (6, {})} | custom-call | flops 2147483648000 | bytes 9437184000 | tf_op jit(solution)/shard_map/filter_y/pallas_call | solution.py:657
  128.6 1.9 merge.25
  130.9 2.7 %collective-permute-start.18 = (f32[4,32,1024]{2,1,0:T(8,128)}, f32[4,32,1024]{2,1,0:T(8,128)}, u32[]{:S(2)}, u32[]{:S(2)}) collective-permute-start(f32[4,32,1024]{2,1,0:T(8,128)} %get-tuple-element.156.refs_1_), channel_id=1, source_target_pairs={{0,4},{4,0},{8,12},{12,8},{16,20},{20,16},{24,28},{28,24},{1,5},{5... | collective-permute-start | bytes 1572872 | tf_op jit(solution)/shard_map/ppermute | solution.py:840
  135.5 4.9 %filter_y.4 = (f32[32,32,1024]{2,1,0:T(8,128)S(1)}, f32[4,32,1024]{2,1,0:T(8,128)}, f32[6,32,1024]{2,1,0:T(8,128)}, f32[8,128]{1,0:T(8,128)}) custom-call(f32[32,32,1024]{2,1,0:T(8,128)S(1)} %get-tuple-element.150.refs_0_, bf16[608,256]{1,0:T(8,128)(2,1)S(1)} %get-tuple-element.138.refs_1_, ...), custom_call_target="tpu_custom_call", output_to_operand_aliasing={{2}: (6, {}), {3}: (7, {})} | custom-call | flops 2147483648000 | bytes 9437184000 | tf_op jit(solution)/shard_map/filter_y/pallas_call | solution.py:657
  141.4 5.2 %collective-permute-done.18.refs_2_.refs_4_ = f32[4,32,1024]{2,1,0:T(8,128)} collective-permute-done((f32[4,32,1024]{2,1,0:T(8,128)}, f32[4,32,1024]{2,1,0:T(8,128)}, u32[]{:S(2)}, u32[]{:S(2)}) %collective-permute-start.18) | collective-permute-done | bytes 524320 | tf_op jit(solution)/shard_map/ppermute | solution.py:840
  148.4 5.1 %filter_y.5 = (f32[32,32,1024]{2,1,0:T(8,128)S(1)}, f32[4,32,1024]{2,1,0:T(8,128)}, f32[6,32,1024]{2,1,0:T(8,128)}, f32[8,128]{1,0:T(8,128)}) custom-call(f32[32,32,1024]{2,1,0:T(8,128)S(1)} %get-tuple-element.137.refs_0_, bf16[608,256]{1,0:T(8,128)(2,1)S(1)} %get-tuple-element.138.refs_1_, ...), custom_call_target="tpu_custom_call", output_to_operand_aliasing={{2}: (6, {}), {3}: (7, {})} | custom-call | flops 2147483648000 | bytes 9437184000 | tf_op jit(solution)/shard_map/filter_y/pallas_call | solution.py:657
  153.5 5.6 %collective-permute-start.20 = (f32[6,32,1024]{2,1,0:T(8,128)}, f32[6,32,1024]{2,1,0:T(8,128)S(1)}, u32[]{:S(2)}, u32[]{:S(2)}) collective-permute-start(f32[6,32,1024]{2,1,0:T(8,128)} %get-tuple-element.162), channel_id=1, source_target_pairs={{0,28},{4,8},{8,4},{12,16},{16,12},{20,24},{24,20},{28,0},{1,29},{... | collective-permute-start | bytes 2359304 | tf_op jit(solution)/shard_map/ppermute | solution.py:840
  159.2 4.9 %collective-permute-start.19 = (f32[4,32,1024]{2,1,0:T(8,128)}, f32[4,32,1024]{2,1,0:T(8,128)S(1)}, u32[]{:S(2)}, u32[]{:S(2)}) collective-permute-start(f32[4,32,1024]{2,1,0:T(8,128)} %get-tuple-element.161.refs_1_), channel_id=1, source_target_pairs={{0,4},{4,0},{8,12},{12,8},{16,20},{20,16},{24,28},{28,24},{1,5},{5... | collective-permute-start | bytes 1572872 | tf_op jit(solution)/shard_map/ppermute | solution.py:840
  165.8 16.9 %collective-permute-start.25 = (f32[2,32,1024]{2,1,0:T(8,128)}, f32[2,32,1024]{2,1,0:T(8,128)S(1)}, u32[]{:S(2)}, u32[]{:S(2)}) collective-permute-start(f32[2,32,1024]{2,1,0:T(8,128)} %get-tuple-element.171.refs_1_), channel_id=1, source_target_pairs={{0,8},{4,12},{8,0},{12,4},{16,24},{20,28},{24,16},{28,20},{1,9},{5... | collective-permute-start | bytes 786440 | tf_op jit(solution)/shard_map/ppermute | solution.py:840
  182.7 2.3 %collective-permute-done.21.refs_2_.refs_6_ = f32[2,32,1024]{2,1,0:T(8,128)S(1)} collective-permute-done((f32[2,32,1024]{2,1,0:T(8,128)S(1)}, f32[2,32,1024]{2,1,0:T(8,128)S(1)}, u32[]{:S(2)}, u32[]{:S(2)}) %collective-permute-start.21) | collective-permute-done | bytes 262176 | tf_op jit(solution)/shard_map/ppermute | solution.py:840
  185.9 2.4 %collective-permute-start.24 = (f32[2,32,1024]{2,1,0:T(8,128)}, f32[2,32,1024]{2,1,0:T(8,128)S(1)}, u32[]{:S(2)}, u32[]{:S(2)}) collective-permute-start(f32[2,32,1024]{2,1,0:T(8,128)} %get-tuple-element.170), channel_id=1, source_target_pairs={{0,16},{4,20},{8,24},{12,28},{16,0},{20,4},{24,8},{28,12},{1,17},{... | collective-permute-start | bytes 786440 | tf_op jit(solution)/shard_map/ppermute | solution.py:840
  195.3 3.4 %collective-permute-start.27 = (f32[2,32,1024]{2,1,0:T(8,128)}, f32[2,32,1024]{2,1,0:T(8,128)}, u32[]{:S(2)}, u32[]{:S(2)}) collective-permute-start(f32[2,32,1024]{2,1,0:T(8,128)} %get-tuple-element.177), channel_id=1, source_target_pairs={{0,16},{4,20},{8,24},{12,28},{16,0},{20,4},{24,8},{28,12},{1,17},{... | collective-permute-start | bytes 786440 | tf_op jit(solution)/shard_map/ppermute | solution.py:840
  198.7 2.2 collective-permute-done.24.refs_7_
  201.0 8.5 %filter_x.3 = (f32[3,32,32,1024]{3,2,1,0:T(8,128)}, f32[8,128]{1,0:T(8,128)}) custom-call(f32[32,32,1024]{2,1,0:T(8,128)S(1)} %get-tuple-element.169.refs_0_, f32[1024,1024]{1,0:T(8,128)S(1)} %copy-done, f32[28,128]{1,0:T(8,128)S(1)} %get-tuple-element.155.refs_0_.refs_2_, ...), custom_call_target="tpu_custom_call", output_to_operand_aliasing={{1}: (8, {})} | custom-call | flops 6442450944000 | bytes 13631488000 | tf_op jit(solution)/shard_map/filter_x/pallas_call | solution.py:657
  211.7 8.5 %filter_x.4 = (f32[3,32,32,1024]{3,2,1,0:T(8,128)}, f32[8,128]{1,0:T(8,128)}) custom-call(f32[32,32,1024]{2,1,0:T(8,128)S(1)} %get-tuple-element.176.refs_0_, f32[1024,1024]{1,0:T(8,128)S(1)} %copy-done, f32[28,128]{1,0:T(8,128)S(1)} %get-tuple-element.155.refs_0_.refs_2_, ...), custom_call_target="tpu_custom_call", output_to_operand_aliasing={{0}: (8, {}), {1}: (9, {})} | custom-call | flops 6442450944000 | bytes 13631488000 | tf_op jit(solution)/shard_map/filter_x/pallas_call | solution.py:657
  220.2 2.8 %collective-permute-done.26.refs_7_ = f32[2,32,1024]{2,1,0:T(8,128)} collective-permute-done((f32[2,32,1024]{2,1,0:T(8,128)}, f32[2,32,1024]{2,1,0:T(8,128)}, u32[]{:S(2)}, u32[]{:S(2)}) %collective-permute-start.26) | collective-permute-done | bytes 262176 | tf_op jit(solution)/shard_map/ppermute | solution.py:840
  223.0 8.4 %filter_x.5 = (f32[3,32,32,1024]{3,2,1,0:T(8,128)}, f32[8,128]{1,0:T(8,128)}) custom-call(f32[32,32,1024]{2,1,0:T(8,128)S(1)} %get-tuple-element.159.refs_0_, f32[1024,1024]{1,0:T(8,128)S(1)} %copy-done, f32[28,128]{1,0:T(8,128)S(1)} %get-tuple-element.155.refs_0_.refs_2_, ...), custom_call_target="tpu_custom_call", output_to_operand_aliasing={{0}: (8, {}), {1}: (9, {})} | custom-call | flops 6442450944000 | bytes 13631488000 | tf_op jit(solution)/shard_map/filter_x/pallas_call | solution.py:657
  (125 shorter events, 48.8 us)
Async XLA Ops:
  20.2 20.5 %collective-permute-start = (f32[12,32,1024]{2,1,0:T(8,128)}, f32[12,32,1024]{2,1,0:T(8,128)}, u32[]{:S(2)}, u32[]{:S(2)}) collective-permute-start(f32[12,32,1024]{2,1,0:T(8,128)} %get-tuple-element.101.refs_1_), channel_id=1, source_target_pairs={{0,1},{1,0},{2,3},{3,2},{4,5},{5,4},{6,7},{7,6},{8,9},{9,8},{10,11... | collective-permute-start | bytes 4718600 | tf_op jit(solution)/shard_map/ppermute | solution.py:840
  20.2 15.4 %collective-permute-start.1 = (f32[4,32,1024]{2,1,0:T(8,128)}, f32[4,32,1024]{2,1,0:T(8,128)}, u32[]{:S(2)}, u32[]{:S(2)}) collective-permute-start(f32[4,32,1024]{2,1,0:T(8,128)} %get-tuple-element.104.refs_1_), channel_id=1, source_target_pairs={{0,4},{4,0},{8,12},{12,8},{16,20},{20,16},{24,28},{28,24},{1,5},{5... | collective-permute-start | bytes 1572872 | tf_op jit(solution)/shard_map/ppermute | solution.py:840
  33.6 34.5 %collective-permute-start.3 = (f32[4,32,1024]{2,1,0:T(8,128)}, f32[4,32,1024]{2,1,0:T(8,128)}, u32[]{:S(2)}, u32[]{:S(2)}) collective-permute-start(f32[4,32,1024]{2,1,0:T(8,128)} %get-tuple-element.112.refs_1_), channel_id=1, source_target_pairs={{0,4},{4,0},{8,12},{12,8},{16,20},{20,16},{24,28},{28,24},{1,5},{5... | collective-permute-start | bytes 1572872 | tf_op jit(solution)/shard_map/ppermute | solution.py:840
  39.1 23.0 %collective-permute-start.4 = (f32[2,32,1024]{2,1,0:T(8,128)}, f32[2,32,1024]{2,1,0:T(8,128)}, u32[]{:S(2)}, u32[]{:S(2)}) collective-permute-start(f32[2,32,1024]{2,1,0:T(8,128)} %get-tuple-element.113.refs_1_), channel_id=1, source_target_pairs={{0,8},{4,12},{8,0},{12,4},{16,24},{20,28},{24,16},{28,20},{1,9},{5... | collective-permute-start | bytes 786440 | tf_op jit(solution)/shard_map/ppermute | solution.py:840
  46.7 30.6 %collective-permute-start.2 = (f32[4,32,1024]{2,1,0:T(8,128)}, f32[4,32,1024]{2,1,0:T(8,128)}, u32[]{:S(2)}, u32[]{:S(2)}) collective-permute-start(f32[4,32,1024]{2,1,0:T(8,128)} %get-tuple-element.111.refs_1_), channel_id=1, source_target_pairs={{0,4},{4,0},{8,12},{12,8},{16,20},{20,16},{24,28},{28,24},{1,5},{5... | collective-permute-start | bytes 1572872 | tf_op jit(solution)/shard_map/ppermute | solution.py:840
  47.2 40.4 %collective-permute-start.5 = (f32[6,32,1024]{2,1,0:T(8,128)}, f32[6,32,1024]{2,1,0:T(8,128)}, u32[]{:S(2)}, u32[]{:S(2)}) collective-permute-start(f32[6,32,1024]{2,1,0:T(8,128)} %get-tuple-element.121), channel_id=1, source_target_pairs={{0,28},{4,8},{8,4},{12,16},{16,12},{20,24},{24,20},{28,0},{1,29},{... | collective-permute-start | bytes 2359304 | tf_op jit(solution)/shard_map/ppermute | solution.py:840
  48.7 39.0 %collective-permute-start.8 = (f32[12,32,1024]{2,1,0:T(8,128)}, f32[12,32,1024]{2,1,0:T(8,128)}, u32[]{:S(2)}, u32[]{:S(2)}) collective-permute-start(f32[12,32,1024]{2,1,0:T(8,128)} %get-tuple-element.124), channel_id=1, source_target_pairs={{0,3},{1,2},{2,1},{3,0},{4,7},{5,6},{6,5},{7,4},{8,11},{9,10},{10,... | collective-permute-start | bytes 4718600 | tf_op jit(solution)/shard_map/ppermute | solution.py:840
  62.1 18.7 %copy-start.13 = (f32[256,256]{1,0:T(8,128)S(1)}, f32[256,256]{1,0:T(8,128)}, u32[]{:S(2)}) copy-start(f32[256,256]{1,0:T(8,128)} %refs_1_.6) | copy-start | bytes 786436
  63.8 17.0 %copy-start.23 = (f32[128,128]{1,0:T(8,128)S(1)}, f32[128,128]{1,0:T(8,128)}, u32[]{:S(2)}) copy-start(f32[128,128]{1,0:T(8,128)} %refs_2_.7) | copy-start | bytes 196612
  63.8 17.0 %copy-start.24 = (s32[2]{0:T(128)S(1)}, s32[2]{0:T(128)}, u32[]{:S(2)}) copy-start(s32[2]{0:T(128)} %pad_add_fusion.refs_0_) | copy-start | bytes 28
  65.6 22.1 %collective-permute-start.7 = (f32[2,32,1024]{2,1,0:T(8,128)}, f32[2,32,1024]{2,1,0:T(8,128)S(1)}, u32[]{:S(2)}, u32[]{:S(2)}) collective-permute-start(f32[2,32,1024]{2,1,0:T(8,128)} %get-tuple-element.123), channel_id=1, source_target_pairs={{0,16},{4,20},{8,24},{12,28},{16,0},{20,4},{24,8},{28,12},{1,17},{... | collective-permute-start | bytes 786440 | tf_op jit(solution)/shard_map/ppermute | solution.py:840
  70.9 12.6 %collective-permute-start.9 = (f32[2,32,1024]{2,1,0:T(8,128)}, f32[2,32,1024]{2,1,0:T(8,128)S(1)}, u32[]{:S(2)}, u32[]{:S(2)}) collective-permute-start(f32[2,32,1024]{2,1,0:T(8,128)} %get-tuple-element.125.refs_1_), channel_id=1, source_target_pairs={{0,8},{4,12},{8,0},{12,4},{16,24},{20,28},{24,16},{28,20},{1,9},{5... | collective-permute-start | bytes 786440 | tf_op jit(solution)/shard_map/ppermute | solution.py:840
  80.1 15.3 %collective-permute-start.6 = (f32[2,32,1024]{2,1,0:T(8,128)}, f32[2,32,1024]{2,1,0:T(8,128)}, u32[]{:S(2)}, u32[]{:S(2)}) collective-permute-start(f32[2,32,1024]{2,1,0:T(8,128)} %get-tuple-element.122.refs_1_), channel_id=1, source_target_pairs={{0,8},{4,12},{8,0},{12,4},{16,24},{20,28},{24,16},{28,20},{1,9},{5... | collective-permute-start | bytes 786440 | tf_op jit(solution)/shard_map/ppermute | solution.py:840
  85.0 15.6 %collective-permute-start.12 = (f32[2,32,1024]{2,1,0:T(8,128)}, f32[2,32,1024]{2,1,0:T(8,128)}, u32[]{:S(2)}, u32[]{:S(2)}) collective-permute-start(f32[2,32,1024]{2,1,0:T(8,128)} %get-tuple-element.133), channel_id=1, source_target_pairs={{0,16},{4,20},{8,24},{12,28},{16,0},{20,4},{24,8},{28,12},{1,17},{... | collective-permute-start | bytes 786440 | tf_op jit(solution)/shard_map/ppermute | solution.py:840
  97.2 15.3 %collective-permute-start.10 = (f32[2,32,1024]{2,1,0:T(8,128)}, f32[2,32,1024]{2,1,0:T(8,128)}, u32[]{:S(2)}, u32[]{:S(2)}) collective-permute-start(f32[2,32,1024]{2,1,0:T(8,128)} %get-tuple-element.129), channel_id=1, source_target_pairs={{0,16},{4,20},{8,24},{12,28},{16,0},{20,4},{24,8},{28,12},{1,17},{... | collective-permute-start | bytes 786440 | tf_op jit(solution)/shard_map/ppermute | solution.py:840
  97.4 10.3 %collective-permute-start.11 = (f32[4,32,1024]{2,1,0:T(8,128)}, f32[4,32,1024]{2,1,0:T(8,128)}, u32[]{:S(2)}, u32[]{:S(2)}) collective-permute-start(f32[4,32,1024]{2,1,0:T(8,128)} %get-tuple-element.131.refs_1_), channel_id=1, source_target_pairs={{0,1},{1,0},{2,3},{3,2},{4,5},{5,4},{6,7},{7,6},{8,9},{9,8},{10,11... | collective-permute-start | bytes 1572872 | tf_op jit(solution)/shard_map/ppermute | solution.py:840
  107.7 11.9 %collective-permute-start.15 = (f32[4,32,1024]{2,1,0:T(8,128)}, f32[4,32,1024]{2,1,0:T(8,128)}, u32[]{:S(2)}, u32[]{:S(2)}) collective-permute-start(f32[4,32,1024]{2,1,0:T(8,128)} %get-tuple-element.144.refs_1_), channel_id=1, source_target_pairs={{0,1},{1,0},{2,3},{3,2},{4,5},{5,4},{6,7},{7,6},{8,9},{9,8},{10,11... | collective-permute-start | bytes 1572872 | tf_op jit(solution)/shard_map/ppermute | solution.py:840
  109.7 13.9 %collective-permute-start.14 = (f32[4,32,1024]{2,1,0:T(8,128)}, f32[4,32,1024]{2,1,0:T(8,128)}, u32[]{:S(2)}, u32[]{:S(2)}) collective-permute-start(f32[4,32,1024]{2,1,0:T(8,128)} %get-tuple-element.143), channel_id=1, source_target_pairs={{0,3},{1,2},{2,1},{3,0},{4,7},{5,6},{6,5},{7,4},{8,11},{9,10},{10,... | collective-permute-start | bytes 1572872 | tf_op jit(solution)/shard_map/ppermute | solution.py:840
  119.5 9.0 %collective-permute-start.13 = (f32[4,32,1024]{2,1,0:T(8,128)}, f32[4,32,1024]{2,1,0:T(8,128)}, u32[]{:S(2)}, u32[]{:S(2)}) collective-permute-start(f32[4,32,1024]{2,1,0:T(8,128)} %get-tuple-element.140.refs_1_), channel_id=1, source_target_pairs={{0,1},{1,0},{2,3},{3,2},{4,5},{5,4},{6,7},{7,6},{8,9},{9,8},{10,11... | collective-permute-start | bytes 1572872 | tf_op jit(solution)/shard_map/ppermute | solution.py:840
  121.6 13.9 %collective-permute-start.17 = (f32[4,32,1024]{2,1,0:T(8,128)}, f32[4,32,1024]{2,1,0:T(8,128)}, u32[]{:S(2)}, u32[]{:S(2)}) collective-permute-start(f32[4,32,1024]{2,1,0:T(8,128)} %get-tuple-element.151), channel_id=1, source_target_pairs={{0,3},{1,2},{2,1},{3,0},{4,7},{5,6},{6,5},{7,4},{8,11},{9,10},{10,... | collective-permute-start | bytes 1572872 | tf_op jit(solution)/shard_map/ppermute | solution.py:840
  130.5 17.9 %collective-permute-start.16 = (f32[4,32,1024]{2,1,0:T(8,128)}, f32[4,32,1024]{2,1,0:T(8,128)}, u32[]{:S(2)}, u32[]{:S(2)}) collective-permute-start(f32[4,32,1024]{2,1,0:T(8,128)} %get-tuple-element.149), channel_id=1, source_target_pairs={{0,3},{1,2},{2,1},{3,0},{4,7},{5,6},{6,5},{7,4},{8,11},{9,10},{10,... | collective-permute-start | bytes 1572872 | tf_op jit(solution)/shard_map/ppermute | solution.py:840
  130.9 15.8 %collective-permute-start.18 = (f32[4,32,1024]{2,1,0:T(8,128)}, f32[4,32,1024]{2,1,0:T(8,128)}, u32[]{:S(2)}, u32[]{:S(2)}) collective-permute-start(f32[4,32,1024]{2,1,0:T(8,128)} %get-tuple-element.156.refs_1_), channel_id=1, source_target_pairs={{0,4},{4,0},{8,12},{12,8},{16,20},{20,16},{24,28},{28,24},{1,5},{5... | collective-permute-start | bytes 1572872 | tf_op jit(solution)/shard_map/ppermute | solution.py:840
  140.4 23.7 %collective-permute-start.22 = (f32[4,32,1024]{2,1,0:T(8,128)}, f32[4,32,1024]{2,1,0:T(8,128)}, u32[]{:S(2)}, u32[]{:S(2)}) collective-permute-start(f32[4,32,1024]{2,1,0:T(8,128)} %get-tuple-element.164.refs_1_), channel_id=1, source_target_pairs={{0,4},{4,0},{8,12},{12,8},{16,20},{20,16},{24,28},{28,24},{1,5},{5... | collective-permute-start | bytes 1572872 | tf_op jit(solution)/shard_map/ppermute | solution.py:840
  153.5 47.5 %copy-start = (f32[1024,1024]{1,0:T(8,128)S(1)}, f32[1024,1024]{1,0:T(8,128)}, u32[]{:S(2)}) copy-start(f32[1024,1024]{1,0:T(8,128)} %refs_1_.9) | copy-start | bytes 12582916
  153.5 47.4 %collective-permute-start.20 = (f32[6,32,1024]{2,1,0:T(8,128)}, f32[6,32,1024]{2,1,0:T(8,128)S(1)}, u32[]{:S(2)}, u32[]{:S(2)}) collective-permute-start(f32[6,32,1024]{2,1,0:T(8,128)} %get-tuple-element.162), channel_id=1, source_target_pairs={{0,28},{4,8},{8,4},{12,16},{16,12},{20,24},{24,20},{28,0},{1,29},{... | collective-permute-start | bytes 2359304 | tf_op jit(solution)/shard_map/ppermute | solution.py:840
  159.2 30.5 %collective-permute-start.19 = (f32[4,32,1024]{2,1,0:T(8,128)}, f32[4,32,1024]{2,1,0:T(8,128)S(1)}, u32[]{:S(2)}, u32[]{:S(2)}) collective-permute-start(f32[4,32,1024]{2,1,0:T(8,128)} %get-tuple-element.161.refs_1_), channel_id=1, source_target_pairs={{0,4},{4,0},{8,12},{12,8},{16,20},{20,16},{24,28},{28,24},{1,5},{5... | collective-permute-start | bytes 1572872 | tf_op jit(solution)/shard_map/ppermute | solution.py:840
  164.1 21.0 %collective-permute-start.21 = (f32[2,32,1024]{2,1,0:T(8,128)S(1)}, f32[2,32,1024]{2,1,0:T(8,128)S(1)}, u32[]{:S(2)}, u32[]{:S(2)}) collective-permute-start(f32[2,32,1024]{2,1,0:T(8,128)S(1)} %copy-done.18), channel_id=1, source_target_pairs={{0,8},{4,12},{8,0},{12,4},{16,24},{20,28},{24,16},{28,20},{1,9},{5... | collective-permute-start | bytes 786440 | tf_op jit(solution)/shard_map/ppermute | solution.py:840
  165.8 27.7 %collective-permute-start.25 = (f32[2,32,1024]{2,1,0:T(8,128)}, f32[2,32,1024]{2,1,0:T(8,128)S(1)}, u32[]{:S(2)}, u32[]{:S(2)}) collective-permute-start(f32[2,32,1024]{2,1,0:T(8,128)} %get-tuple-element.171.refs_1_), channel_id=1, source_target_pairs={{0,8},{4,12},{8,0},{12,4},{16,24},{20,28},{24,16},{28,20},{1,9},{5... | collective-permute-start | bytes 786440 | tf_op jit(solution)/shard_map/ppermute | solution.py:840
  185.9 15.1 %collective-permute-start.24 = (f32[2,32,1024]{2,1,0:T(8,128)}, f32[2,32,1024]{2,1,0:T(8,128)S(1)}, u32[]{:S(2)}, u32[]{:S(2)}) collective-permute-start(f32[2,32,1024]{2,1,0:T(8,128)} %get-tuple-element.170), channel_id=1, source_target_pairs={{0,16},{4,20},{8,24},{12,28},{16,0},{20,4},{24,8},{28,12},{1,17},{... | collective-permute-start | bytes 786440 | tf_op jit(solution)/shard_map/ppermute | solution.py:840
  191.7 17.9 %collective-permute-start.23 = (f32[2,32,1024]{2,1,0:T(8,128)}, f32[2,32,1024]{2,1,0:T(8,128)}, u32[]{:S(2)}, u32[]{:S(2)}) collective-permute-start(f32[2,32,1024]{2,1,0:T(8,128)} %get-tuple-element.168.refs_1_), channel_id=1, source_target_pairs={{0,8},{4,12},{8,0},{12,4},{16,24},{20,28},{24,16},{28,20},{1,9},{5... | collective-permute-start | bytes 786440 | tf_op jit(solution)/shard_map/ppermute | solution.py:840
  195.3 16.4 %collective-permute-start.27 = (f32[2,32,1024]{2,1,0:T(8,128)}, f32[2,32,1024]{2,1,0:T(8,128)}, u32[]{:S(2)}, u32[]{:S(2)}) collective-permute-start(f32[2,32,1024]{2,1,0:T(8,128)} %get-tuple-element.177), channel_id=1, source_target_pairs={{0,16},{4,20},{8,24},{12,28},{16,0},{20,4},{24,8},{28,12},{1,17},{... | collective-permute-start | bytes 786440 | tf_op jit(solution)/shard_map/ppermute | solution.py:840
  211.3 11.7 %collective-permute-start.26 = (f32[2,32,1024]{2,1,0:T(8,128)}, f32[2,32,1024]{2,1,0:T(8,128)}, u32[]{:S(2)}, u32[]{:S(2)}) collective-permute-start(f32[2,32,1024]{2,1,0:T(8,128)} %get-tuple-element.175), channel_id=1, source_target_pairs={{0,16},{4,20},{8,24},{12,28},{16,0},{20,4},{24,8},{28,12},{1,17},{... | collective-permute-start | bytes 786440 | tf_op jit(solution)/shard_map/ppermute | solution.py:840
  (31 other events, 165.1 us)
